TPU v7x, 32 devices: a whole 2x2x4 slice. The times are simulated.
32 devices in a mesh: seq: 16 (over z, y, x), tp: 2 (over core).
Axes of the slice: x: 2, y: 2, z: 4, core: 2. Of those that a mesh axis runs over, the one named last changes fastest.
Arguments:
- tokens: bfloat16 [2048, 1152], P('seq'), may hold values from -6 to 6
- norm_gain: float32 [1152], replicated, may hold values from 0.5 to 1.5
- in_conv_weight: bfloat16 [1152, 2304], P(None, 'tp'), may hold values from -0.1875 to 0.1875
- in_gate_weight: bfloat16 [1152, 2304], P(None, 'tp'), may hold values from -0.1875 to 0.1875
- conv_weight: float32 [4, 2304], P(None, 'tp'), may hold values from -3 to 3
- conv_bias: float32 [2304], P('tp'), may hold values from -3 to 3
- scan_proj_weight: bfloat16 [2304, 104], P('tp'), may hold values from -0.125 to 0.125
- step_proj_weight: bfloat16 [72, 2304], P(None, 'tp'), may hold values from -0.75 to 0.75
- step_bias: float32 [2304], P('tp'), may hold values from -9 to -2
- decay_log: float32 [16, 2304], P(None, 'tp'), may hold values from -3 to 1
- skip_gain: float32 [2304], P('tp'), may hold values from -4 to 4
- out_weight: bfloat16 [2304, 1152], P('tp'), may hold values from -0.125 to 0.125
- segment_ids: int32 [2048], replicated, may hold values from 0 to 4, as said below
- cotangent: bfloat16 [2048, 1152], P('seq'), may hold values from -6 to 6
Outputs:
- mixed: bfloat16 [2048, 1152], P('seq')
- input_grad: float32 [2048, 1152], P('seq')
- gain_grad: float32 [1152], replicated
- in_conv_grad: float32 [1152, 2304], P('seq', 'tp')
- in_gate_grad: float32 [1152, 2304], P('seq', 'tp')
- conv_weight_grad: float32 [4, 2304], P(None, 'tp')
- conv_bias_grad: float32 [2304], P('tp')
- scan_proj_grad: float32 [2304, 104], P('tp')
- step_proj_grad: float32 [72, 2304], P(None, 'tp')
- step_bias_grad: float32 [2304], P('tp')
- decay_log_grad: float32 [16, 2304], P(None, 'tp')
- skip_grad: float32 [2304], P('tp')
- out_grad: float32 [2304, 1152], P('tp', 'seq')
Inputs may be any that keep to these rules, and one draw needn't show every extreme that they name: `segment_ids`: segment ids never fall along the tokens and rise by one at each new segment; one segment begins among the first 128 tokens and ends among the last 128.
All inputs are finite; a program needn't handle non-finite values.
Results may differ from a plain program's by a relative error of at most 0.0055.
The roundings to bfloat16 on the way count: a program that leaves them out, or rounds other values in their place, can miss the bound.
Values may be sent and summed in bfloat16 or wider, within the bound.
No kernel may reach another device: no remote copies, remote signals or barrier semaphores. Data moves between devices by JAX's collectives and lax.ppermute only.
A program may use at most 192 MiB of HBM per device.

v0:
```python
import functools

import jax
import jax.numpy as jnp
from jax import lax
from jax.experimental import pallas as pl
from jax.experimental.pallas import tpu as pltpu
from jax.sharding import PartitionSpec as P

NORM_EPS = 1e-05
LANES = 128
CHUNKS = 8
LOG2E = 1.4426950408889634
LN2 = 0.6931471805599453
FAR = 1e30
VMEM = 48 * 1024 * 1024


def sigmoid(value):
    return 1.0 / (1.0 + jnp.exp(-value))


def silu_grad(value):
    sigma = sigmoid(value)
    return sigma * (1.0 + value * (1.0 - sigma))


def softplus(value):
    small = jnp.exp(-jnp.abs(value))
    series = small * (1.0 - small * (0.5 - small * (1.0 / 3.0 - small * 0.25)))
    return jnp.maximum(value, 0.0) + jnp.where(small < 0.01, series, jnp.log(1.0 + small))


def dot(first, second, contract):
    return lax.dot_general(
        first, second, (contract, ((), ())), preferred_element_type=jnp.float32
    )


def strided(number, length):
    return pl.ds(number, CHUNKS, stride=length // CHUNKS)


def spread(proj_ref, first, table_ref, states, length):
    for place in range(length // CHUNKS):
        rows = proj_ref[strided(place, length), :]
        for state in range(states):
            column = rows[:, first + state : first + state + 1]
            start = (place * states + state) * CHUNKS
            table_ref[start : start + CHUNKS, :] = jnp.broadcast_to(column, (CHUNKS, LANES))


def tile(ref, place, state, states):
    start = (place * states + state) * CHUNKS
    return ref[start : start + CHUNKS, :]


def ends_kernel(
    rank, states,
    own_ref, peer_ref, weight_ref, bias_ref, decay_ref, conv_ref, gg_ref, gate_ref, same_ref,
    step_ref, ends_ref, seeds_ref, totals_ref,
    proj_ref, in_ref, out_ref, long_ref, drive_ref, source_ref,
):
    length = conv_ref.shape[0]
    places = length // CHUNKS

    @pl.when(pl.program_id(0) == 0)
    def _():
        proj_ref[...] = own_ref[...] + peer_ref[...]
        spread(proj_ref, rank, in_ref, states, length)
        spread(proj_ref, rank + states, out_ref, states, length)

    low = proj_ref[:, :rank].astype(jnp.bfloat16)
    step_pre = dot(low, weight_ref[...], ((1,), (0,))) + bias_ref[...]
    step_ref[...] = step_pre
    step = softplus(step_pre)
    long_ref[...] = jnp.where(same_ref[...] > 0.0, step, FAR)
    drive_ref[...] = step * conv_ref[...].astype(jnp.float32)
    gate = gate_ref[...]
    source_ref[...] = gg_ref[...] * gate * sigmoid(gate)
    rate2 = -jnp.exp(decay_ref[...]) * LOG2E
    rates = [jnp.broadcast_to(rate2[n : n + 1, :], (CHUNKS, LANES)) for n in range(states)]
    hidden = [None] * states
    sums = None
    for place in range(places):
        long = long_ref[strided(place, length), :]
        drive = drive_ref[strided(place, length), :]
        sums = long if place == 0 else sums + long
        for n in range(states):
            term = tile(in_ref, place, n, states) * drive
            hidden[n] = term if place == 0 else jnp.exp2(long * rates[n]) * hidden[n] + term
    for n in range(states):
        ends_ref[n * CHUNKS : (n + 1) * CHUNKS, :] = hidden[n]
    back = [None] * states
    for place in reversed(range(places)):
        long = long_ref[strided(place, length), :]
        source = source_ref[strided(place, length), :]
        for n in range(states):
            term = tile(out_ref, place, n, states) * source
            term = term if place == places - 1 else back[n] + term
            back[n] = jnp.exp2(long * rates[n]) * term
    for n in range(states):
        seeds_ref[n * CHUNKS : (n + 1) * CHUNKS, :] = back[n]
    decays = [jnp.exp2(rate2 * sums[c : c + 1, :]) for c in range(CHUNKS)]
    end = jnp.zeros((states, LANES), jnp.float32)
    seed = jnp.zeros((states, LANES), jnp.float32)
    for c in range(CHUNKS):
        end = decays[c] * end + ends_ref[pl.ds(c, states, stride=CHUNKS), :]
    for c in reversed(range(CHUNKS)):
        seed = decays[c] * seed + seeds_ref[pl.ds(c, states, stride=CHUNKS), :]
    totals_ref[:states, :] = end
    totals_ref[states : 2 * states, :] = seed
    total = jnp.sum(sums, axis=0, keepdims=True)
    totals_ref[2 * states :, :] = jnp.broadcast_to(total, (8, LANES))


def scan_kernel(
    rank, states, groups,
    own_ref, peer_ref, weight_ref, decay_ref, skip_ref, conv_ref, gg_ref, gate_ref, same_ref,
    step_ref, ends_ref, seeds_ref, carry_ref, incoming_ref,
    pack_ref, gconv_ref, gproj_ref,
    proj_ref, in_ref, out_ref, long_ref, true_ref, drive_ref, source_ref,
    start_ref, last_ref, hidden_ref, in_acc, out_acc, low_acc, scan_ref, gstep_ref, mix_ref,
):
    length = conv_ref.shape[0]
    places = length // CHUNKS
    index = pl.program_id(0)

    @pl.when(index == 0)
    def _():
        proj_ref[...] = own_ref[...] + peer_ref[...]
        spread(proj_ref, rank, in_ref, states, length)
        spread(proj_ref, rank + states, out_ref, states, length)
        in_acc[...] = jnp.zeros_like(in_acc)
        out_acc[...] = jnp.zeros_like(out_acc)
        low_acc[...] = jnp.zeros_like(low_acc)

    step_pre = step_ref[...]
    step = softplus(step_pre)
    conv = conv_ref[...].astype(jnp.float32)
    gate = gate_ref[...]
    gg = gg_ref[...]
    sigma = sigmoid(gate)
    act = gate * sigma
    source_all = gg * act
    true_ref[...] = step
    long_ref[...] = jnp.where(same_ref[...] > 0.0, step, FAR)
    drive_ref[...] = step * conv
    source_ref[...] = source_all
    rate = -jnp.exp(decay_ref[...])
    rate2 = rate * LOG2E
    rates = [jnp.broadcast_to(rate2[n : n + 1, :], (CHUNKS, LANES)) for n in range(states)]
    sums = long_ref[strided(0, length), :]
    for place in range(1, places):
        sums = sums + long_ref[strided(place, length), :]
    decays = [jnp.exp2(rate2 * sums[c : c + 1, :]) for c in range(CHUNKS)]
    state = carry_ref[...]
    for c in range(CHUNKS):
        start_ref[pl.ds(c, states, stride=CHUNKS), :] = state
        state = decays[c] * state + ends_ref[pl.ds(c, states, stride=CHUNKS), :]
    state = incoming_ref[...]
    for c in reversed(range(CHUNKS)):
        last_ref[pl.ds(c, states, stride=CHUNKS), :] = state
        state = decays[c] * state + seeds_ref[pl.ds(c, states, stride=CHUNKS), :]

    hidden = [start_ref[n * CHUNKS : (n + 1) * CHUNKS, :] for n in range(states)]
    for place in range(places):
        long = long_ref[strided(place, length), :]
        drive = drive_ref[strided(place, length), :]
        source = source_ref[strided(place, length), :]
        rows = slice(place * CHUNKS, (place + 1) * CHUNKS)
        scan = None
        for n in range(states):
            lanes = slice(n * LANES, (n + 1) * LANES)
            value = jnp.exp2(long * rates[n]) * hidden[n] + tile(in_ref, place, n, states) * drive
            hidden[n] = value
            if place < places - 1:
                hidden_ref[(place * states + n) * CHUNKS : (place * states + n + 1) * CHUNKS, :] = value
            part = tile(out_ref, place, n, states) * value
            scan = part if n == 0 else scan + part
            out_acc[rows, lanes] += source * value
        scan_ref[strided(place, length), :] = scan

    back = [last_ref[n * CHUNKS : (n + 1) * CHUNKS, :] for n in range(states)]
    logs = [None] * states
    for place in reversed(range(places)):
        long = long_ref[strided(place, length), :]
        true = true_ref[strided(place, length), :]
        drive = drive_ref[strided(place, length), :]
        source = source_ref[strided(place, length), :]
        rows = slice(place * CHUNKS, (place + 1) * CHUNKS)
        gstep = None
        mixed = None
        for n in range(states):
            lanes = slice(n * LANES, (n + 1) * LANES)
            grad = back[n] + tile(out_ref, place, n, states) * source
            previous = (
                start_ref[n * CHUNKS : (n + 1) * CHUNKS, :] if place == 0
                else tile(hidden_ref, place - 1, n, states)
            )
            back[n] = jnp.exp2(long * rates[n]) * grad
            log = back[n] * previous
            part = log * true
            logs[n] = part if logs[n] is None else logs[n] + part
            part = log * rates[n]
            gstep = part if n == 0 else gstep + part
            part = grad * tile(in_ref, place, n, states)
            mixed = part if n == 0 else mixed + part
            in_acc[rows, lanes] += grad * drive
        gstep_ref[strided(place, length), :] = gstep
        mix_ref[strided(place, length), :] = mixed

    scan_out = scan_ref[...] + skip_ref[...] * conv
    gated = scan_out * act
    ggate = gg * scan_out * sigma * (1.0 + gate * (1.0 - sigma))
    mix = mix_ref[...]
    gconv_ref[...] = source_all * skip_ref[...] + mix * step
    gpre = (gstep_ref[...] * LN2 + mix * conv) * sigmoid(step_pre)
    gpre_low = gpre.astype(jnp.bfloat16)
    low_acc[:, :rank] += dot(gpre_low, weight_ref[...], ((1,), (1,)))
    low = proj_ref[...].astype(jnp.bfloat16)
    step_part = dot(gpre_low, low, ((0,), (0,)))
    row_number = lax.broadcasted_iota(jnp.int32, (LANES, LANES), 0)
    table = jnp.where(row_number == rank + states, jnp.sum(gpre, axis=0, keepdims=True), 0.0)
    table = jnp.where(
        row_number == rank + states + 1, jnp.sum(source_all * conv, axis=0, keepdims=True), table
    )
    for n in range(states):
        value = jnp.sum(logs[n], axis=0, keepdims=True) * rate[n : n + 1, :]
        table = jnp.where(row_number == rank + n, value, table)
    lane_number = lax.broadcasted_iota(jnp.int32, (LANES, LANES), 1)
    small = jnp.where(lane_number < rank, step_part, table.T)
    pack_ref[:, :LANES] = gated.T.astype(jnp.bfloat16)
    pack_ref[:, LANES : 2 * LANES] = ggate.T.astype(jnp.bfloat16)
    pack_ref[:, 2 * LANES :] = small.astype(jnp.bfloat16)

    @pl.when(index == groups - 1)
    def _():
        wide = states * LANES
        source_state = lax.broadcasted_iota(jnp.int32, (wide, LANES), 0) // LANES
        column = lax.broadcasted_iota(jnp.int32, (wide, LANES), 1)
        total = jnp.zeros((length, LANES), jnp.float32)
        for acc, first in ((in_acc, rank), (out_acc, rank + states)):
            pick = jnp.where(source_state + first == column, 1.0, 0.0).astype(jnp.bfloat16)
            value = acc[...]
            high = value.astype(jnp.bfloat16)
            rest = (value - high.astype(jnp.float32)).astype(jnp.bfloat16)
            total = total + dot(high, pick, ((1,), (0,))) + dot(rest, pick, ((1,), (0,)))
        scan_ref[...] = total
        for place in range(places):
            mix_ref[strided(place, length), :] = scan_ref[place * CHUNKS : (place + 1) * CHUNKS, :]
        gproj_ref[...] = mix_ref[...] + low_acc[...]


def column_block(rows, width=LANES):
    return pl.BlockSpec((rows, width), lambda g: (0, g))


def row_block(width):
    return pl.BlockSpec((LANES, width), lambda g: (g, 0))


def whole(*shape):
    return pl.BlockSpec(shape, lambda g: (0,) * len(shape))


def run_ends(own, peer, weight, bias, decay_log, conv, gg, gate, same):
    length, width = conv.shape
    rank, states = weight.shape[0], decay_log.shape[0]
    tall = length // CHUNKS * states * CHUNKS
    f32 = jnp.float32
    return pl.pallas_call(
        functools.partial(ends_kernel, rank, states),
        grid=(width // LANES,),
        in_specs=[
            whole(length, LANES), whole(length, LANES), column_block(rank), column_block(1),
            column_block(states), column_block(length), column_block(length), column_block(length),
            whole(length, 1),
        ],
        out_specs=[
            column_block(length), column_block(states * CHUNKS), column_block(states * CHUNKS),
            column_block(2 * states + 8),
        ],
        out_shape=[
            jax.ShapeDtypeStruct((length, width), f32),
            jax.ShapeDtypeStruct((states * CHUNKS, width), f32),
            jax.ShapeDtypeStruct((states * CHUNKS, width), f32),
            jax.ShapeDtypeStruct((2 * states + 8, width), f32),
        ],
        scratch_shapes=[
            pltpu.VMEM((length, LANES), f32), pltpu.VMEM((tall, LANES), f32),
            pltpu.VMEM((tall, LANES), f32), pltpu.VMEM((length, LANES), f32),
            pltpu.VMEM((length, LANES), f32), pltpu.VMEM((length, LANES), f32),
        ],
        compiler_params=pltpu.CompilerParams(vmem_limit_bytes=VMEM),
        name="ends",
    )(own, peer, weight, bias, decay_log, conv, gg, gate, same)


def run_scan(own, peer, weight, decay_log, skip, conv, gg, gate, same, step, ends, seeds, carry, incoming):
    length, width = conv.shape
    rank, states = weight.shape[0], decay_log.shape[0]
    places = length // CHUNKS
    tall = places * states * CHUNKS
    f32 = jnp.float32
    block = pltpu.VMEM((length, LANES), f32)
    return pl.pallas_call(
        functools.partial(scan_kernel, rank, states, width // LANES),
        grid=(width // LANES,),
        in_specs=[
            whole(length, LANES), whole(length, LANES), column_block(rank), column_block(states),
            column_block(1), column_block(length), column_block(length), column_block(length),
            whole(length, 1), column_block(length), column_block(states * CHUNKS),
            column_block(states * CHUNKS), column_block(states), column_block(states),
        ],
        out_specs=[row_block(3 * LANES), column_block(length), whole(length, LANES)],
        out_shape=[
            jax.ShapeDtypeStruct((width, 3 * LANES), jnp.bfloat16),
            jax.ShapeDtypeStruct((length, width), f32),
            jax.ShapeDtypeStruct((length, LANES), f32),
        ],
        scratch_shapes=[
            block, pltpu.VMEM((tall, LANES), f32), pltpu.VMEM((tall, LANES), f32),
            block, block, block, block,
            pltpu.VMEM((states * CHUNKS, LANES), f32), pltpu.VMEM((states * CHUNKS, LANES), f32),
            pltpu.VMEM((tall, LANES), f32),
            pltpu.VMEM((length, states * LANES), f32), pltpu.VMEM((length, states * LANES), f32),
            block, block, block, block,
        ],
        compiler_params=pltpu.CompilerParams(vmem_limit_bytes=VMEM),
        name="scan",
    )(own, peer, weight, decay_log, skip, conv, gg, gate, same, step, ends, seeds, carry, incoming)


def from_behind(block, axis, distance):
    devices = range(lax.axis_size(axis))
    route = [(i - distance, i) for i in devices if i - distance in devices]
    return lax.ppermute(block, axis, route)


def swap(block):
    return lax.ppermute(block, "tp", [(0, 1), (1, 0)])


def levels(members):
    found, stride = [], 1
    while stride < members:
        left = members // stride
        radix = 4 if left % 4 == 0 else 2 if left % 2 == 0 else left
        found.append((stride, radix))
        stride *= radix
    return found


def exchange(totals, rate2, states):
    members = lax.axis_size("seq")
    device = lax.axis_index("seq")
    end, seed, sums = totals[:states], totals[states : 2 * states], totals[2 * states : 2 * states + 1]
    carry = jnp.zeros_like(end)
    incoming = jnp.zeros_like(end)
    before = jnp.zeros_like(sums)
    behind = jnp.zeros_like(sums)
    for stride, radix in levels(members):
        digit = device // stride % radix
        payload = jnp.concatenate([end, seed, sums], axis=0)
        got = [payload]
        for hop in range(1, radix):
            route = []
            for i in range(members):
                own = i // stride % radix
                to = own ^ hop if radix in (2, 4) else (own + hop) % radix
                route.append((i, i + (to - own) * stride))
            got.append(lax.ppermute(payload, "seq", route))
        parts = []
        for number in range(radix):
            hop = (digit ^ number) if radix in (2, 4) else (digit - number) % radix
            value = got[0]
            for other in range(1, radix):
                value = jnp.where(hop == other, got[other], value)
            parts.append((value[:states], value[states : 2 * states], value[2 * states :]))
        near_carry, near_before = jnp.zeros_like(end), jnp.zeros_like(sums)
        end, sums_all = jnp.zeros_like(end), jnp.zeros_like(sums)
        for number in range(radix):
            part_end, _, part_sum = parts[number]
            decay = jnp.exp2(rate2 * part_sum)
            end = decay * end + part_end
            near_carry = jnp.where(number < digit, decay * near_carry + part_end, near_carry)
            near_before = jnp.where(number < digit, near_before + part_sum, near_before)
            sums_all = sums_all + part_sum
        near_incoming, near_behind, seed = jnp.zeros_like(seed), jnp.zeros_like(sums), jnp.zeros_like(seed)
        for number in reversed(range(radix)):
            _, part_seed, part_sum = parts[number]
            decay = jnp.exp2(rate2 * part_sum)
            seed = decay * seed + part_seed
            near_incoming = jnp.where(number > digit, decay * near_incoming + part_seed, near_incoming)
            near_behind = jnp.where(number > digit, near_behind + part_sum, near_behind)
        carry = carry + jnp.exp2(rate2 * before) * near_carry
        incoming = incoming + jnp.exp2(rate2 * behind) * near_incoming
        before, behind, sums = before + near_before, behind + near_behind, sums_all
    return carry, incoming


def shards(
    tokens, norm_gain, in_conv_weight, in_gate_weight, conv_weight, conv_bias, scan_proj_weight,
    step_proj_weight, step_bias, decay_log, skip_gain, out_weight, segment_ids, cotangent,
):
    f32, bf16 = jnp.float32, jnp.bfloat16
    length, model = tokens.shape
    rank = step_proj_weight.shape[0]
    states = decay_log.shape[0]
    kernel = conv_weight.shape[0]
    width = conv_weight.shape[1]
    members = lax.axis_size("seq")
    device = lax.axis_index("seq")
    core = lax.axis_index("tp")
    rows = width // members
    half = model // 2
    padded_ids = jnp.concatenate([jnp.full((kernel,), -1, jnp.int32), segment_ids])
    near_ids = lax.dynamic_slice_in_dim(padded_ids, device * length, length + kernel)
    own_ids = near_ids[kernel:]
    conv_masks = [
        (own_ids == near_ids[offset + 1 : offset + 1 + length]).astype(f32)[:, None]
        for offset in range(kernel)
    ]
    same_prev = conv_masks[kernel - 2]

    tok_float = tokens.astype(f32)
    inv_rms = lax.rsqrt(jnp.mean(tok_float * tok_float, axis=1, keepdims=True) + NORM_EPS)
    normed = (tok_float * inv_rms * norm_gain).astype(bf16)
    factor = jnp.where(
        core == 0,
        jnp.concatenate([normed[:, :half], cotangent[:, :half]], axis=1),
        jnp.concatenate([normed[:, half:], cotangent[:, half:]], axis=1),
    )
    factors = lax.all_gather(factor, "seq", axis=0, tiled=True)
    conv_in = dot(normed, in_conv_weight, ((1,), (0,))).astype(bf16)
    left_rim = from_behind(conv_in[length - (kernel - 1) :], "seq", 1)
    gate_in = dot(normed, in_gate_weight, ((1,), (0,)))
    grad_gated = dot(cotangent, out_weight, ((1,), (1,)))
    conv_ext = jnp.concatenate([left_rim, conv_in], axis=0).astype(f32)
    conv_pre = conv_bias + sum(
        conv_weight[offset] * conv_ext[offset : offset + length] * conv_masks[offset]
        for offset in range(kernel)
    )
    conv_out = (conv_pre * sigmoid(conv_pre)).astype(bf16)
    own = jnp.pad(
        dot(conv_out, scan_proj_weight, ((1,), (0,))), ((0, 0), (0, LANES - rank - 2 * states))
    )
    peer = swap(own)
    step_pre, ends, seeds, totals = run_ends(
        own, peer, step_proj_weight, step_bias[None], decay_log, conv_out, grad_gated, gate_in, same_prev
    )
    rate2 = -jnp.exp(decay_log) * LOG2E
    carry, incoming = exchange(totals, rate2, states)
    pack, grad_conv, low_own = run_scan(
        own, peer, step_proj_weight, decay_log, skip_gain[None], conv_out, grad_gated, gate_in,
        same_prev, step_pre, ends, seeds, carry, incoming,
    )
    first_got = lax.all_to_all(pack.reshape(members, rows, 3 * LANES), "seq", 0, 0, tiled=True)
    low_peer = swap(low_own)
    gated_t, ggate_t = pack[:, :LANES], pack[:, LANES : 2 * LANES]
    branch_own = dot(gated_t, out_weight, ((0,), (0,)))
    branch = branch_own + swap(branch_own)
    mixed_out = (tok_float + branch).astype(bf16)

    grad_proj = (low_own + low_peer).astype(bf16)[:, : rank + 2 * states]
    scan_proj_part = dot(conv_out, grad_proj, ((0,), (0,)))
    grad_conv = grad_conv + dot(grad_proj, scan_proj_weight, ((1,), (1,)))
    grad_cpre = grad_conv * silu_grad(conv_pre)
    conv_bias_part = jnp.sum(grad_cpre, axis=0)
    conv_weight_part = [
        jnp.sum(grad_cpre * conv_ext[offset : offset + length] * conv_masks[offset], axis=0)
        for offset in range(kernel)
    ]
    grad_ext = sum(
        jnp.pad(
            grad_cpre * conv_weight[offset] * conv_masks[offset],
            ((offset, kernel - 1 - offset), (0, 0)),
        )
        for offset in range(kernel)
    )
    rim_back = from_behind(grad_ext[: kernel - 1], "seq", -1)
    grad_conv_in = grad_ext[kernel - 1 :] + jnp.concatenate(
        [jnp.zeros((length - (kernel - 1), width), f32), rim_back], axis=0
    )
    grad_conv_low = grad_conv_in.astype(bf16)
    normed_own = dot(grad_conv_low, in_conv_weight, ((1,), (1,))) + dot(
        ggate_t, in_gate_weight, ((0,), (1,))
    )
    gain_part = jnp.sum(normed_own * tok_float * inv_rms, axis=0)
    small = jnp.concatenate(
        [scan_proj_part, jnp.stack(conv_weight_part + [conv_bias_part, gain_part], axis=1)], axis=1
    )
    small = jnp.pad(small, ((0, 0), (0, LANES - small.shape[1]))).astype(bf16)
    second = jnp.concatenate([grad_conv_low.T, small], axis=1)
    second_got = lax.all_to_all(second.reshape(members, rows, 2 * LANES), "seq", 0, 0, tiled=True)

    grad_normed = normed_own + swap(normed_own)
    scaled_grad = grad_normed * norm_gain
    input_grad = (
        cotangent.astype(f32)
        + inv_rms * scaled_grad
        - tok_float * inv_rms * inv_rms * inv_rms
        * jnp.mean(scaled_grad * tok_float, axis=1, keepdims=True)
    )

    late = jnp.stack([first_got[:, :, :LANES], first_got[:, :, LANES : 2 * LANES], second_got[:, :, :LANES]])
    late_peer = swap(late)
    normed_all = factors[:, :half].reshape(members, length, half)
    cot_all = factors[:, half:].reshape(members, length, half)

    def product(values, factor_all):
        return lax.dot_general(
            values, factor_all, (((0, 2), (0, 1)), ((), ())), preferred_element_type=f32
        )

    def products(values):
        return jnp.stack(
            [product(values[0], cot_all), product(values[1], normed_all), product(values[2], normed_all)]
        )

    kept = products(late)
    given = swap(products(late_peer))
    full = jnp.where(
        core == 0, jnp.concatenate([kept, given], axis=2), jnp.concatenate([given, kept], axis=2)
    )
    sums_first = jnp.sum(first_got[:, :, 2 * LANES :].astype(f32), axis=0)
    sums_second = jnp.sum(second_got[:, :, LANES:].astype(f32), axis=0)
    cols = model // members
    out_blocks = full.reshape(3, rows, members, cols).transpose(2, 1, 0, 3).reshape(members, rows, 3 * cols)
    final = lax.all_to_all(out_blocks, "seq", 0, 0, tiled=True).reshape(width, 3, cols)
    sums = jnp.concatenate([sums_first, sums_second], axis=1).astype(bf16)
    sums = lax.all_to_all(
        jnp.broadcast_to(sums[None], (members, rows, 2 * LANES)), "seq", 0, 0, tiled=True
    ).reshape(width, 2 * LANES).astype(f32)
    out_grad = final[:, 0]
    in_gate_grad = final[:, 1].T
    in_conv_grad = final[:, 2].T
    step_proj_grad = sums[:, :rank].T
    decay_log_grad = sums[:, rank : rank + states].T
    step_bias_grad = sums[:, rank + states]
    skip_grad = sums[:, rank + states + 1]
    base = LANES
    scan_width = rank + 2 * states
    scan_proj_grad = sums[:, base : base + scan_width]
    conv_weight_grad = sums[:, base + scan_width : base + scan_width + kernel].T
    conv_bias_grad = sums[:, base + scan_width + kernel]
    gain_grad = sums[:, base + scan_width + kernel + 1]
    gain_grad = gain_grad + swap(gain_grad)
    return (
        mixed_out, input_grad, gain_grad, in_conv_grad, in_gate_grad, conv_weight_grad,
        conv_bias_grad, scan_proj_grad, step_proj_grad, step_bias_grad, decay_log_grad, skip_grad,
        out_grad,
    )


def solution(mesh):
    in_specs = (
        P("seq", None), P(), P(None, "tp"), P(None, "tp"), P(None, "tp"), P("tp"), P("tp", None),
        P(None, "tp"), P("tp"), P(None, "tp"), P("tp"), P("tp", None), P(), P("seq", None),
    )
    out_specs = (
        P("seq", None), P("seq", None), P(), P("seq", "tp"), P("seq", "tp"), P(None, "tp"), P("tp"),
        P("tp", None), P(None, "tp"), P("tp"), P(None, "tp"), P("tp"), P("tp", "seq"),
    )
    return jax.shard_map(shards, mesh=mesh, in_specs=in_specs, out_specs=out_specs, check_vma=False)
```

profile of v0, /device:TPU:8, one launch (start us, length us, event | category | flops | bytes accessed | tf_op | source)
XLA Modules:
  0.0 279.9 jit_solution(9598357063363403929)
XLA Ops:
  7.2 1.3 fusion.24
  8.5 1.1 fusion.19
  9.6 2.3 convolution_convert_fusion
  12.6 3.4 %collective-permute-start = (bf16[3,1152]{1,0:T(4,128)(2,1)}, bf16[3,1152]{1,0:T(4,128)(2,1)}, u32[]{:S(2)}, u32[]{:S(2)}) collective-permute-start(bf16[3,1152]{1,0:T(4,128)(2,1)} %slice.284), channel_id=1, source_target_pairs={{0,2},{2,4},{4,6},{6,8},{8,10},{10,12},{12,14},{14,16},{16,18},{18... | collective-permute-start | bytes 20744 | tf_op jit(solution)/shard_map/ppermute | solution.py:338
  17.6 1.0 copy-done.24
  18.6 2.8 fusion.68.gg_ref
  23.2 1.3 multiply_convert_fusion
  27.6 1.1 copy-done.2
  31.3 8.9 %ends.1 = (f32[128,1152]{1,0:T(8,128)S(1)}, f32[128,1152]{1,0:T(8,128)S(1)}, f32[128,1152]{1,0:T(8,128)S(1)}, f32[40,1152]{1,0:T(8,128)}) custom-call(f32[128,128]{1,0:T(8,128)} %pad.27.own_ref, f32[128,128]{1,0:T(8,128)} %collective-permute-done.1.peer_ref, bf16[72,1152]{1,0:T(8,128)(2,1)S(1)} %copy-done.7, f32[1,1152]{1,0:T(1,128)S(1)} %broadcast_in_dim.10.bias_ref, ...), custom_call_target="tpu_custom_call" | custom-call | tf_op jit(solution)/shard_map/ends/pallas_call | solution.py:272
  42.7 1.5 collective-permute-start.4
  44.2 1.5 collective-permute-start.3
  46.2 2.0 maximum_select_fusion.1
  48.3 2.2 collective-permute-done.4
  50.5 4.8 %collective-permute-done.3 = f32[33,1152]{1,0:T(8,128)} collective-permute-done((f32[33,1152]{1,0:T(8,128)}, f32[33,1152]{1,0:T(8,128)}, u32[]{:S(2)}, u32[]{:S(2)}) %collective-permute-start.3) | collective-permute-done | bytes 152096 | tf_op jit(solution)/shard_map/ppermute | solution.py:373
  55.3 1.3 select_select_fusion.7
  57.4 1.0 multiply_add_fusion.1
  60.2 2.6 collective-permute-start.6
  64.2 7.9 %collective-permute-done.7 = f32[33,1152]{1,0:T(8,128)} collective-permute-done((f32[33,1152]{1,0:T(8,128)}, f32[33,1152]{1,0:T(8,128)}, u32[]{:S(2)}, u32[]{:S(2)}) %collective-permute-start.7) | collective-permute-done | bytes 152096 | tf_op jit(solution)/shard_map/ppermute | solution.py:373
  72.0 6.6 %collective-permute-done.6 = f32[33,1152]{1,0:T(8,128)} collective-permute-done((f32[33,1152]{1,0:T(8,128)}, f32[33,1152]{1,0:T(8,128)}, u32[]{:S(2)}, u32[]{:S(2)}) %collective-permute-start.6) | collective-permute-done | bytes 152096 | tf_op jit(solution)/shard_map/ppermute | solution.py:373
  78.6 4.7 %collective-permute-done.5 = f32[33,1152]{1,0:T(8,128)} collective-permute-done((f32[33,1152]{1,0:T(8,128)}, f32[33,1152]{1,0:T(8,128)}, u32[]{:S(2)}, u32[]{:S(2)}) %collective-permute-start.5) | collective-permute-done | bytes 152096 | tf_op jit(solution)/shard_map/ppermute | solution.py:373
  83.3 1.2 select_select_fusion.2
  84.6 1.2 select_select_fusion
  85.9 1.2 fusion.42.incoming_ref
  87.2 1.2 fusion.48.carry_ref
  88.4 15.8 %scan.1 = (bf16[1152,384]{1,0:T(8,128)(2,1)S(1)}, f32[128,1152]{1,0:T(8,128)S(1)}, f32[128,128]{1,0:T(8,128)}) custom-call(f32[128,128]{1,0:T(8,128)} %pad.27.own_ref, f32[128,128]{1,0:T(8,128)} %collective-permute-done.1.peer_ref, bf16[72,1152]{1,0:T(8,128)(2,1)S(1)} %copy-done.8, f32[16,1152]{1,0:T(8,128)S(1)} %copy-done.6, ...), custom_call_target="tpu_custom_call" | custom-call | tf_op jit(solution)/shard_map/scan/pallas_call | solution.py:307
  105.1 1.8 fusion.33
  106.9 5.3 %all-to-all-start = ((bf16[16,72,384]{2,1,0:T(8,128)(2,1)}), bf16[16,72,384]{2,1,0:T(8,128)(2,1)}, u32[]{:S(2)}, u32[]{:S(2)}) async-start(bf16[16,72,384]{2,1,0:T(8,128)(2,1)} %bitcast.106), calls=%async_computation | async-start | bytes 1769472 | tf_op jit(solution)/shard_map/all_to_all | solution.py:459
  113.1 1.2 fusion.70
  115.4 4.5 %collective-permute-start.10 = (f32[3,1152]{1,0:T(4,128)S(1)}, f32[3,1152]{1,0:T(4,128)S(1)}, u32[]{:S(2)}, u32[]{:S(2)}) collective-permute-start(f32[3,1152]{1,0:T(4,128)S(1)} %pad_add_fusion.1), channel_id=1, source_target_pairs={{2,0},{4,2},{6,4},{8,6},{10,8},{12,10},{14,12},{16,14},{18,16},{20... | collective-permute-start | bytes 41480 | tf_op jit(solution)/shard_map/ppermute | solution.py:338
  120.1 14.1 %collective-permute-done.10 = f32[3,1152]{1,0:T(4,128)S(1)} collective-permute-done((f32[3,1152]{1,0:T(4,128)S(1)}, f32[3,1152]{1,0:T(4,128)S(1)}, u32[]{:S(2)}, u32[]{:S(2)}) %collective-permute-start.10) | collective-permute-done | bytes 13856 | tf_op jit(solution)/shard_map/ppermute | solution.py:338
  135.2 1.0 convolution_convert_fusion.1
  140.9 3.2 %concatenate.51 = bf16[1152,110]{0,1:T(8,128)(2,1)} concatenate(bf16[1152,104]{0,1:T(8,128)(2,1)} %convolution_convert_fusion.1, bf16[1152,1]{0,1:T(2,128)(2,1)} %stack.54, bf16[1152,1]{0,1:T(2,128)(2,1)} %stack.55, bf16[1152,1]{0,1:T(2,128)(2,1)} %stack.56, bf16[1152,1]{0,1:T(2,128)(2,1)S(1)} %stack.57, bf16[1152,1]{0,1:T(2,128)(2,1)} %stack.58, bf16[1152,1]{0,1:T(2,128)(2,1)} %stack.59), dimensions={1} | concatenate | bytes 506880 | tf_op jit(solution)/shard_map/concatenate | solution.py:491
  144.1 1.9 fusion.23
  146.0 2.1 copy.77
  148.1 4.7 %all-to-all-done = bf16[16,72,384]{2,1,0:T(8,128)(2,1)} async-done(((bf16[16,72,384]{2,1,0:T(8,128)(2,1)}), bf16[16,72,384]{2,1,0:T(8,128)(2,1)}, u32[]{:S(2)}, u32[]{:S(2)}) %all-to-all-start) | async-done | bytes 884768 | tf_op jit(solution)/shard_map/all_to_all | solution.py:459
  152.8 19.7 %all-to-all-start.1 = ((bf16[16,72,256]{2,1,0:T(8,128)(2,1)}), bf16[16,72,256]{2,1,0:T(8,128)(2,1)S(1)}, u32[]{:S(2)}, u32[]{:S(2)}) async-start(bf16[16,72,256]{2,1,0:T(8,128)(2,1)} %bitcast.116), calls=%async_computation.1 | async-start | bytes 1179648 | tf_op jit(solution)/shard_map/all_to_all | solution.py:496
  172.5 2.5 fusion.35
  175.0 1.2 slice_bitcast_fusion.14
  176.2 12.8 %all-to-all-done.1 = bf16[16,72,256]{2,1,0:T(8,128)(2,1)S(1)} async-done(((bf16[16,72,256]{2,1,0:T(8,128)(2,1)}), bf16[16,72,256]{2,1,0:T(8,128)(2,1)S(1)}, u32[]{:S(2)}, u32[]{:S(2)}) %all-to-all-start.1) | async-done | bytes 589856 | tf_op jit(solution)/shard_map/all_to_all | solution.py:496
  189.1 1.0 pad_maximum_fusion
  191.0 4.6 %all-to-all-start.2 = ((bf16[16,72,256]{2,1,0:T(8,128)(2,1)}), bf16[16,72,256]{2,1,0:T(8,128)(2,1)}, u32[]{:S(2)}, u32[]{:S(2)}) async-start(bf16[16,72,256]{2,1,0:T(8,128)(2,1)} %broadcast_in_dim.11), calls=%async_computation.2 | async-start | bytes 1179648 | tf_op jit(solution)/shard_map/all_to_all | solution.py:533
  195.6 4.1 %fusion.64 = (bf16[2048,576]{1,0:T(8,128)(2,1)S(1)}, bf16[2048,576]{1,0:T(8,128)(2,1)S(1)}) fusion(bf16[2048,1152]{1,0:T(8,128)(2,1)} %all-gather.2.cloned.1.call-done), kind=kLoop, calls=%fused_computation.168 | loop fusion | bytes 9437184 | tf_op jit(solution)/shard_map/slice | solution.py:510
  199.7 1.8 convolution_bitcast_fusion
  201.5 1.6 convolution_bitcast_fusion.1
  203.1 1.6 convolution_bitcast_fusion.2
  205.5 3.4 %copy.80 = bf16[16,128,576]{1,0,2:T(8,128)(2,1)} copy(bf16[16,128,576]{2,1,0:T(8,128)(2,1)S(1)} %bitcast.109) | data formatting | bytes 4718592 | tf_op jit(solution)/shard_map/reshape | solution.py:509
  208.9 3.7 %fusion.11 = f32[1,72,8,72]{3,1,2,0:T(8,128)} fusion(bf16[8,72,16,128]{3,2,1,0:T(8,128)(2,1)} %bitcast.113, bf16[16,72,256]{2,1,0:T(8,128)(2,1)S(1)} %all-to-all-done.1), kind=kOutput, calls=%fused_computation.19 | convolution fusion | flops 169869312 | bytes 2820096 | tf_op jit(solution)/shard_map/dot_general | solution.py:513
  212.6 3.0 %fusion.8 = f32[1,72,8,72]{3,1,2,0:T(8,128)} fusion(bf16[8,72,16,128]{3,2,1,0:T(8,128)(2,1)S(1)} %bitcast.114, bf16[16,72,384]{2,1,0:T(8,128)(2,1)} %all-to-all-done), kind=kOutput, calls=%fused_computation.18 | convolution fusion | flops 169869312 | bytes 2820096 | tf_op jit(solution)/shard_map/dot_general | solution.py:513
  215.6 3.4 %copy.78 = bf16[16,128,576]{1,0,2:T(8,128)(2,1)} copy(bf16[16,128,576]{2,1,0:T(8,128)(2,1)S(1)} %bitcast.111) | data formatting | bytes 4718592 | tf_op jit(solution)/shard_map/reshape | solution.py:510
  219.0 3.7 %fusion.14 = f32[1,72,8,72]{3,1,2,0:T(8,128)} fusion(bf16[8,72,16,128]{3,2,1,0:T(8,128)(2,1)} %bitcast.115, bf16[16,72,384]{2,1,0:T(8,128)(2,1)} %all-to-all-done), kind=kOutput, calls=%fused_computation.20 | convolution fusion | flops 169869312 | bytes 2820096 | tf_op jit(solution)/shard_map/dot_general | solution.py:513
  222.7 1.5 concatenate.56
  224.3 1.6 fusion.6
  226.7 1.6 copy.89
  228.3 6.9 %all-to-all-start.3 = ((f32[16,72,216]{2,1,0:T(8,128)}), f32[16,72,216]{2,1,0:T(8,128)}, u32[]{:S(2)}, u32[]{:S(2)}) async-start(f32[16,72,216]{2,1,0:T(8,128)} %copy.89), calls=%async_computation.3 | async-start | bytes 2359296 | tf_op jit(solution)/shard_map/all_to_all | solution.py:531
  235.2 2.5 fusion.22
  237.7 1.1 convert.47
  238.9 1.8 slice_reduce_fusion
  241.1 1.0 slice.333
  242.1 1.0 copy.92
  243.1 0.9 copy.93
  246.4 18.0 %all-to-all-done.3 = f32[16,72,216]{2,1,0:T(8,128)} async-done(((f32[16,72,216]{2,1,0:T(8,128)}), f32[16,72,216]{2,1,0:T(8,128)}, u32[]{:S(2)}, u32[]{:S(2)}) %all-to-all-start.3) | async-done | bytes 995360 | tf_op jit(solution)/shard_map/all_to_all | solution.py:531
  264.4 3.6 %copy.90 = f32[16,72,216]{1,0,2:T(8,128)} copy(f32[16,72,216]{2,1,0:T(8,128)} %all-to-all-done.3) | data formatting | bytes 1990656 | tf_op jit(solution)/shard_map/all_to_all | solution.py:531
  268.0 3.0 %reshape.136 = f32[1152,3,72]{0,2,1:T(8,128)} reshape(f32[16,72,216]{1,0,2:T(8,128)} %copy.90) | data formatting | bytes 1990656 | tf_op jit(solution)/shard_map/reshape | solution.py:531
  270.9 2.1 slice_bitcast_fusion.3
  (214 shorter events, 30.9 us)
Async XLA Ops:
  7.2 9.8 %copy-start = (bf16[1152,1152]{1,0:T(8,128)(2,1)S(1)}, bf16[1152,1152]{1,0:T(8,128)(2,1)}, u32[]{:S(2)}) copy-start(bf16[1152,1152]{1,0:T(8,128)(2,1)} %param.17) | copy-start | bytes 7962628
  7.2 9.6 %copy-start.69 = (s32[2048]{0:T(1024)S(1)}, s32[2048]{0:T(1024)}, u32[]{:S(2)}) copy-start(s32[2048]{0:T(1024)} %param.26) | copy-start | bytes 24580
  7.2 188.4 %all-gather.2.cloned.1.call-start = ((), (), s32[]{:S(2)}) async-start(), calls=%async_computation.4 | async-start | bytes 5013504 | tf_op jit(solution)/shard_map/all_gather | solution.py:435
  8.5 8.4 %copy-start.70 = (f32[128]{0:T(128)}, f32[128]{0:T(128)S(1)}, u32[]{:S(2)}) copy-start(f32[128]{0:T(128)S(1)} %add_rsqrt_fusion) | copy-start | bytes 1540
  12.0 5.0 %copy-start.41 = (bf16[128,1152]{1,0:T(8,128)(2,1)}, bf16[128,1152]{1,0:T(8,128)(2,1)S(1)}, u32[]{:S(2)}) copy-start(bf16[128,1152]{1,0:T(8,128)(2,1)S(1)} %convolution_convert_fusion) | copy-start | bytes 884740
  12.6 8.8 %collective-permute-start = (bf16[3,1152]{1,0:T(4,128)(2,1)}, bf16[3,1152]{1,0:T(4,128)(2,1)}, u32[]{:S(2)}, u32[]{:S(2)}) collective-permute-start(bf16[3,1152]{1,0:T(4,128)(2,1)} %slice.284), channel_id=1, source_target_pairs={{0,2},{2,4},{4,6},{6,8},{8,10},{10,12},{12,14},{14,16},{16,18},{18... | collective-permute-start | bytes 20744 | tf_op jit(solution)/shard_map/ppermute | solution.py:338
  17.0 5.3 %copy-start.65 = (f32[128]{0:T(128)}, f32[128]{0:T(128)S(1)}, u32[]{:S(2)}) copy-start(f32[128]{0:T(128)S(1)} %get-tuple-element.121) | copy-start | bytes 1540
  17.0 5.4 %copy-start.67 = (f32[128]{0:T(128)}, f32[128]{0:T(128)S(1)}, u32[]{:S(2)}) copy-start(f32[128]{0:T(128)S(1)} %get-tuple-element.122) | copy-start | bytes 1540
  17.0 9.8 %copy-start.62 = (f32[128]{0:T(128)}, f32[128]{0:T(128)S(1)}, u32[]{:S(2)}) copy-start(f32[128]{0:T(128)S(1)} %get-tuple-element.123) | copy-start | bytes 1540
  18.6 4.6 %copy-start.64 = (f32[1152]{0:T(1024)S(1)}, f32[1152]{0:T(1024)}, u32[]{:S(2)}) copy-start(f32[1152]{0:T(1024)} %param.19) | copy-start | bytes 13828
  21.4 3.2 %copy-start.51 = (f32[1152]{0:T(1024)}, f32[1152]{0:T(1024)S(1)}, u32[]{:S(2)}) copy-start(f32[1152]{0:T(1024)S(1)} %get-tuple-element.82) | copy-start | bytes 13828
  21.5 3.9 %copy-start.30 = (bf16[128,1152]{1,0:T(8,128)(2,1)S(1)}, bf16[128,1152]{1,0:T(8,128)(2,1)}, u32[]{:S(2)}) copy-start(bf16[128,1152]{1,0:T(8,128)(2,1)} %param.27) | copy-start | bytes 884740
  25.4 2.2 collective-permute-start.1
  42.7 7.8 %collective-permute-start.4 = (f32[33,1152]{1,0:T(8,128)}, f32[33,1152]{1,0:T(8,128)}, u32[]{:S(2)}, u32[]{:S(2)}) collective-permute-start(f32[33,1152]{1,0:T(8,128)} %bitcast.105), channel_id=1, source_target_pairs={{0,2},{2,0},{4,6},{6,4},{8,10},{10,8},{12,14},{14,12},{16,18},{18,... | collective-permute-start | bytes 456200 | tf_op jit(solution)/shard_map/ppermute | solution.py:373
  44.2 11.0 %collective-permute-start.3 = (f32[33,1152]{1,0:T(8,128)}, f32[33,1152]{1,0:T(8,128)}, u32[]{:S(2)}, u32[]{:S(2)}) collective-permute-start(f32[33,1152]{1,0:T(8,128)} %bitcast.105), channel_id=1, source_target_pairs={{0,4},{2,6},{4,0},{6,2},{8,12},{10,14},{12,8},{14,10},{16,20},{18,... | collective-permute-start | bytes 456200 | tf_op jit(solution)/shard_map/ppermute | solution.py:373
  45.7 9.5 %collective-permute-start.2 = (f32[33,1152]{1,0:T(8,128)}, f32[33,1152]{1,0:T(8,128)}, u32[]{:S(2)}, u32[]{:S(2)}) collective-permute-start(f32[33,1152]{1,0:T(8,128)} %bitcast.105), channel_id=1, source_target_pairs={{0,6},{2,4},{4,2},{6,0},{8,14},{10,12},{12,10},{14,8},{16,22},{18,... | collective-permute-start | bytes 456200 | tf_op jit(solution)/shard_map/ppermute | solution.py:373
  57.4 5.4 %copy-start.48 = (f32[1152]{0:T(1024)}, f32[1152]{0:T(1024)S(1)}, u32[]{:S(2)}) copy-start(f32[1152]{0:T(1024)S(1)} %get-tuple-element.120) | copy-start | bytes 13828
  57.4 5.4 %copy-start.59 = (f32[1,1152]{1,0:T(1,128)}, f32[1,1152]{1,0:T(1,128)S(1)}, u32[]{:S(2)}) copy-start(f32[1,1152]{1,0:T(1,128)S(1)} %get-tuple-element.99) | copy-start | bytes 13828
  59.7 12.3 %collective-permute-start.7 = (f32[33,1152]{1,0:T(8,128)}, f32[33,1152]{1,0:T(8,128)}, u32[]{:S(2)}, u32[]{:S(2)}) collective-permute-start(f32[33,1152]{1,0:T(8,128)} %pad_maximum_fusion.2), channel_id=1, source_target_pairs={{0,8},{2,10},{4,12},{6,14},{8,0},{10,2},{12,4},{14,6},{16,24},{18,... | collective-permute-start | bytes 456200 | tf_op jit(solution)/shard_map/ppermute | solution.py:373
  60.2 18.4 %collective-permute-start.6 = (f32[33,1152]{1,0:T(8,128)}, f32[33,1152]{1,0:T(8,128)}, u32[]{:S(2)}, u32[]{:S(2)}) collective-permute-start(f32[33,1152]{1,0:T(8,128)} %pad_maximum_fusion.2), channel_id=1, source_target_pairs={{0,16},{2,18},{4,20},{6,22},{8,24},{10,26},{12,28},{14,30},{16,0},... | collective-permute-start | bytes 456200 | tf_op jit(solution)/shard_map/ppermute | solution.py:373
  62.8 20.5 %collective-permute-start.5 = (f32[33,1152]{1,0:T(8,128)}, f32[33,1152]{1,0:T(8,128)}, u32[]{:S(2)}, u32[]{:S(2)}) collective-permute-start(f32[33,1152]{1,0:T(8,128)} %pad_maximum_fusion.2), channel_id=1, source_target_pairs={{0,24},{2,26},{4,28},{6,30},{8,16},{10,18},{12,20},{14,22},{16,8},... | collective-permute-start | bytes 456200 | tf_op jit(solution)/shard_map/ppermute | solution.py:373
  63.2 23.9 %copy-start.6 = (f32[16,1152]{1,0:T(8,128)S(1)}, f32[16,1152]{1,0:T(8,128)}, u32[]{:S(2)}) copy-start(f32[16,1152]{1,0:T(8,128)} %decay_ref.3) | copy-start | bytes 221188
  63.2 23.9 %copy-start.47 = (f32[1152]{0:T(1024)S(1)}, f32[1152]{0:T(1024)}, u32[]{:S(2)}) copy-start(f32[1152]{0:T(1024)} %copy-done.46) | copy-start | bytes 13828
  63.2 23.9 %copy-start.49 = (f32[1152]{0:T(1024)S(1)}, f32[1152]{0:T(1024)}, u32[]{:S(2)}) copy-start(f32[1152]{0:T(1024)} %copy-done.48) | copy-start | bytes 13828
  63.2 23.9 %copy-start.60 = (f32[1152]{0:T(1024)S(1)}, f32[1152]{0:T(1024)}, u32[]{:S(2)}) copy-start(f32[1152]{0:T(1024)} %get-tuple-element.77) | copy-start | bytes 13828
  63.2 25.1 %copy-start.3 = (f32[128,1152]{1,0:T(8,128)S(1)}, f32[128,1152]{1,0:T(8,128)}, u32[]{:S(2)}) copy-start(f32[128,1152]{1,0:T(8,128)} %fusion.68.gg_ref) | copy-start | bytes 1769476
  63.3 25.1 %copy-start.8 = (bf16[72,1152]{1,0:T(8,128)(2,1)S(1)}, bf16[72,1152]{1,0:T(8,128)(2,1)}, u32[]{:S(2)}) copy-start(bf16[72,1152]{1,0:T(8,128)(2,1)} %weight_ref.3) | copy-start | bytes 497668
  63.3 25.1 %copy-start.10 = (f32[128,1]{1,0:T(8,128)S(1)}, f32[128,1]{1,0:T(8,128)}, u32[]{:S(2)}) copy-start(f32[128,1]{1,0:T(8,128)} %copy.76.same_ref) | copy-start | bytes 1540
  63.3 25.1 %copy-start.14 = (f32[128,1152]{1,0:T(8,128)S(1)}, f32[128,1152]{1,0:T(8,128)}, u32[]{:S(2)}) copy-start(f32[128,1152]{1,0:T(8,128)} %copy-done.13) | copy-start | bytes 1769476
  63.3 25.1 %copy-start.16 = (f32[128,1152]{1,0:T(8,128)S(1)}, f32[128,1152]{1,0:T(8,128)}, u32[]{:S(2)}) copy-start(f32[128,1152]{1,0:T(8,128)} %copy-done.15) | copy-start | bytes 1769476
  63.3 25.1 %copy-start.18 = (f32[128,1152]{1,0:T(8,128)S(1)}, f32[128,1152]{1,0:T(8,128)}, u32[]{:S(2)}) copy-start(f32[128,1152]{1,0:T(8,128)} %copy-done.17) | copy-start | bytes 1769476
  105.0 7.1 %collective-permute-start.9 = (f32[128,128]{1,0:T(8,128)}, f32[128,128]{1,0:T(8,128)}, u32[]{:S(2)}, u32[]{:S(2)}) collective-permute-start(f32[128,128]{1,0:T(8,128)} %get-tuple-element.26), channel_id=1, source_target_pairs={{0,1},{1,0},{2,3},{3,2},{4,5},{5,4},{6,7},{7,6},{8,9},{9,8},{10,11... | collective-permute-start | bytes 196616 | tf_op jit(solution)/shard_map/ppermute | solution.py:342
  105.0 9.2 %copy-start.12 = (f32[128,1152]{1,0:T(8,128)S(1)}, f32[128,1152]{1,0:T(8,128)}, u32[]{:S(2)}) copy-start(f32[128,1152]{1,0:T(8,128)} %copy-done.11) | copy-start | bytes 1769476
  105.0 9.2 %copy-start.63 = (f32[128]{0:T(128)S(1)}, f32[128]{0:T(128)}, u32[]{:S(2)}) copy-start(f32[128]{0:T(128)} %copy-done.62) | copy-start | bytes 1540
  105.1 9.2 %copy-start.66 = (f32[128]{0:T(128)S(1)}, f32[128]{0:T(128)}, u32[]{:S(2)}) copy-start(f32[128]{0:T(128)} %copy-done.65) | copy-start | bytes 1540
  105.1 9.2 %copy-start.68 = (f32[128]{0:T(128)S(1)}, f32[128]{0:T(128)}, u32[]{:S(2)}) copy-start(f32[128]{0:T(128)} %copy-done.67) | copy-start | bytes 1540
  106.9 7.4 %copy-start.20 = (f32[131,1152]{1,0:T(8,128)S(1)}, f32[131,1152]{1,0:T(8,128)}, u32[]{:S(2)}) copy-start(f32[131,1152]{1,0:T(8,128)} %copy-done.19) | copy-start | bytes 1810948
  106.9 7.4 %copy-start.32 = (f32[128,1152]{1,0:T(8,128)S(1)}, f32[128,1152]{1,0:T(8,128)}, u32[]{:S(2)}) copy-start(f32[128,1152]{1,0:T(8,128)} %get-tuple-element.88) | copy-start | bytes 1769476
  106.9 45.9 %all-to-all-start = ((bf16[16,72,384]{2,1,0:T(8,128)(2,1)}), bf16[16,72,384]{2,1,0:T(8,128)(2,1)}, u32[]{:S(2)}, u32[]{:S(2)}) async-start(bf16[16,72,384]{2,1,0:T(8,128)(2,1)} %bitcast.106), calls=%async_computation | async-start | bytes 1769472 | tf_op jit(solution)/shard_map/all_to_all | solution.py:459
  115.3 18.9 %copy-start.23 = (bf16[1152,1152]{1,0:T(8,128)(2,1)S(1)}, bf16[1152,1152]{1,0:T(8,128)(2,1)}, u32[]{:S(2)}) copy-start(bf16[1152,1152]{1,0:T(8,128)(2,1)} %param.16) | copy-start | bytes 7962628
  115.3 18.9 %copy-start.34 = (f32[128,1152]{1,0:T(8,128)S(1)}, f32[128,1152]{1,0:T(8,128)}, u32[]{:S(2)}) copy-start(f32[128,1152]{1,0:T(8,128)} %fusion.33) | copy-start | bytes 1769476
  115.4 18.9 %collective-permute-start.10 = (f32[3,1152]{1,0:T(4,128)S(1)}, f32[3,1152]{1,0:T(4,128)S(1)}, u32[]{:S(2)}, u32[]{:S(2)}) collective-permute-start(f32[3,1152]{1,0:T(4,128)S(1)} %pad_add_fusion.1), channel_id=1, source_target_pairs={{2,0},{4,2},{6,4},{8,6},{10,8},{12,10},{14,12},{16,14},{18,16},{20... | collective-permute-start | bytes 41480 | tf_op jit(solution)/shard_map/ppermute | solution.py:338
  120.1 19.5 %copy-start.28 = (bf16[128,1152]{1,0:T(8,128)(2,1)S(1)}, bf16[128,1152]{1,0:T(8,128)(2,1)}, u32[]{:S(2)}) copy-start(bf16[128,1152]{1,0:T(8,128)(2,1)} %param.14) | copy-start | bytes 884740
  120.1 19.5 %copy-start.50 = (f32[1152]{0:T(1024)S(1)}, f32[1152]{0:T(1024)}, u32[]{:S(2)}) copy-start(f32[1152]{0:T(1024)} %param.15) | copy-start | bytes 13828
  120.1 19.5 %copy-start.71 = (f32[128]{0:T(128)S(1)}, f32[128]{0:T(128)}, u32[]{:S(2)}) copy-start(f32[128]{0:T(128)} %copy-done.70) | copy-start | bytes 1540
  135.1 13.0 %copy-start.26 = (f32[128,1152]{1,0:T(8,128)}, f32[128,1152]{1,0:T(8,128)S(1)}, u32[]{:S(2)}) copy-start(f32[128,1152]{1,0:T(8,128)S(1)} %convolution_add_fusion) | copy-start | bytes 1769476
  135.2 3.5 %collective-permute-start.11 = (f32[128,1152]{1,0:T(8,128)S(1)}, f32[128,1152]{1,0:T(8,128)S(1)}, u32[]{:S(2)}, u32[]{:S(2)}) collective-permute-start(f32[128,1152]{1,0:T(8,128)S(1)} %convolution_add_fusion), channel_id=1, source_target_pairs={{0,1},{1,0},{2,3},{3,2},{4,5},{5,4},{6,7},{7,6},{8,9},{9,8},{10,11... | collective-permute-start | bytes 1769480 | tf_op jit(solution)/shard_map/ppermute | solution.py:342
  140.3 32.2 %copy-start.25 = (bf16[1152,1152]{1,0:T(8,128)(2,1)S(1)}, bf16[1152,1152]{1,0:T(8,128)(2,1)}, u32[]{:S(2)}) copy-start(bf16[1152,1152]{1,0:T(8,128)(2,1)} %param.25) | copy-start | bytes 7962628
  152.8 36.2 %all-to-all-start.1 = ((bf16[16,72,256]{2,1,0:T(8,128)(2,1)}), bf16[16,72,256]{2,1,0:T(8,128)(2,1)S(1)}, u32[]{:S(2)}, u32[]{:S(2)}) async-start(bf16[16,72,256]{2,1,0:T(8,128)(2,1)} %bitcast.116), calls=%async_computation.1 | async-start | bytes 1179648 | tf_op jit(solution)/shard_map/all_to_all | solution.py:496
  175.0 15.1 %copy-start.73 = (f32[128]{0:T(128)S(1)}, f32[128]{0:T(128)}, u32[]{:S(2)}) copy-start(f32[128]{0:T(128)} %get-tuple-element.75) | copy-start | bytes 1540
  175.0 60.2 %collective-permute-start.8 = (f32[128,1152]{1,0:T(8,128)}, f32[128,1152]{1,0:T(8,128)}, u32[]{:S(2)}, u32[]{:S(2)}) collective-permute-start(f32[128,1152]{1,0:T(8,128)} %fusion.35), channel_id=1, source_target_pairs={{0,1},{1,0},{2,3},{3,2},{4,5},{5,4},{6,7},{7,6},{8,9},{9,8},{10,11... | collective-permute-start | bytes 1769480 | tf_op jit(solution)/shard_map/ppermute | solution.py:342
  190.1 9.6 %collective-permute-start.13 = (bf16[3,16,72,128]{3,2,1,0:T(8,128)(2,1)}, bf16[3,16,72,128]{3,2,1,0:T(8,128)(2,1)}, u32[]{:S(2)}, u32[]{:S(2)}) collective-permute-start(bf16[3,16,72,128]{3,2,1,0:T(8,128)(2,1)} %pad_maximum_fusion), channel_id=1, source_target_pairs={{0,1},{1,0},{2,3},{3,2},{4,5},{5,4},{6,7},{7,6},{8,9},{9,8},{10,11... | collective-permute-start | bytes 2654216 | tf_op jit(solution)/shard_map/ppermute | solution.py:342
  191.0 37.3 %all-to-all-start.2 = ((bf16[16,72,256]{2,1,0:T(8,128)(2,1)}), bf16[16,72,256]{2,1,0:T(8,128)(2,1)}, u32[]{:S(2)}, u32[]{:S(2)}) async-start(bf16[16,72,256]{2,1,0:T(8,128)(2,1)} %broadcast_in_dim.11), calls=%async_computation.2 | async-start | bytes 1179648 | tf_op jit(solution)/shard_map/all_to_all | solution.py:533
  199.7 3.4 %copy-start.21 = (bf16[2048,576]{1,0:T(8,128)(2,1)}, bf16[2048,576]{1,0:T(8,128)(2,1)S(1)}, u32[]{:S(2)}) copy-start(bf16[2048,576]{1,0:T(8,128)(2,1)S(1)} %get-tuple-element.89) | copy-start | bytes 7077892
  208.9 3.7 %copy-start.33 = (bf16[16,128,576]{1,0,2:T(8,128)(2,1)S(1)}, bf16[16,128,576]{1,0,2:T(8,128)(2,1)}, u32[]{:S(2)}) copy-start(bf16[16,128,576]{1,0,2:T(8,128)(2,1)} %copy.80) | copy-start | bytes 7077892
  208.9 13.8 %collective-permute-start.14 = (f32[3,72,576]{2,1,0:T(8,128)}, f32[3,72,576]{2,1,0:T(8,128)}, u32[]{:S(2)}, u32[]{:S(2)}) collective-permute-start(f32[3,72,576]{2,1,0:T(8,128)} %pad_maximum_fusion.1), channel_id=1, source_target_pairs={{0,1},{1,0},{2,3},{3,2},{4,5},{5,4},{6,7},{7,6},{8,9},{9,8},{10,11... | collective-permute-start | bytes 1493000 | tf_op jit(solution)/shard_map/ppermute | solution.py:342
  226.6 8.6 %copy-start.27 = (f32[128,1152]{1,0:T(8,128)S(1)}, f32[128,1152]{1,0:T(8,128)}, u32[]{:S(2)}) copy-start(f32[128,1152]{1,0:T(8,128)} %copy-done.26) | copy-start | bytes 1769476
  226.6 8.6 %copy-start.29 = (bf16[128,1152]{1,0:T(8,128)(2,1)S(1)}, bf16[128,1152]{1,0:T(8,128)(2,1)}, u32[]{:S(2)}) copy-start(bf16[128,1152]{1,0:T(8,128)(2,1)} %param.14) | copy-start | bytes 884740
  226.7 8.6 %copy-start.31 = (bf16[128,1152]{1,0:T(8,128)(2,1)S(1)}, bf16[128,1152]{1,0:T(8,128)(2,1)}, u32[]{:S(2)}) copy-start(bf16[128,1152]{1,0:T(8,128)(2,1)} %param.27) | copy-start | bytes 884740
  226.7 8.6 %copy-start.36 = (f32[128,1152]{1,0:T(8,128)S(1)}, f32[128,1152]{1,0:T(8,128)}, u32[]{:S(2)}) copy-start(f32[128,1152]{1,0:T(8,128)} %copy-done.35) | copy-start | bytes 1769476
  226.7 8.6 %copy-start.72 = (f32[128]{0:T(128)S(1)}, f32[128]{0:T(128)}, u32[]{:S(2)}) copy-start(f32[128]{0:T(128)} %copy-done.70) | copy-start | bytes 1540
  228.3 36.1 %all-to-all-start.3 = ((f32[16,72,216]{2,1,0:T(8,128)}), f32[16,72,216]{2,1,0:T(8,128)}, u32[]{:S(2)}, u32[]{:S(2)}) async-start(f32[16,72,216]{2,1,0:T(8,128)} %copy.89), calls=%async_computation.3 | async-start | bytes 2359296 | tf_op jit(solution)/shard_map/all_to_all | solution.py:531
  240.6 5.1 %collective-permute-start.12 = (f32[1152]{0:T(1024)S(1)}, f32[1152]{0:T(1024)S(1)}, u32[]{:S(2)}, u32[]{:S(2)}) collective-permute-start(f32[1152]{0:T(1024)S(1)} %get-tuple-element.73), channel_id=1, source_target_pairs={{0,1},{1,0},{2,3},{3,2},{4,5},{5,4},{6,7},{7,6},{8,9},{9,8},{10,11... | collective-permute-start | bytes 13832 | tf_op jit(solution)/shard_map/ppermute | solution.py:342
  264.4 8.7 %copy-start.1 = (bf16[1152,1152]{1,0:T(8,128)(2,1)S(1)}, bf16[1152,1152]{1,0:T(8,128)(2,1)}, u32[]{:S(2)}) copy-start(bf16[1152,1152]{1,0:T(8,128)(2,1)} %param.17) | copy-start | bytes 7962628
  (30 other events, 48.0 us)
Sparse Core Ops, SparseCore 0:
  48.4 102.4 all-gather.1
where the time goes:
time: 282 us; the launch traced here: 280 us
  waiting for transfers between devices  75.7 us (27%)
  local copies, waits for them, and re-layouts  55.4 us (20%)
  starting transfers between devices  51.5 us (18%)
  other arithmetic  29.1 us (10%)
  matrix products  28.5 us (10%)
  Pallas kernels  24.7 us (9%)
  between operations  15 us (5%)
    ppermute x6, waiting for transfers between devices, exchange(): got.append(lax.ppermute(payload, 'seq', route))  26.1 us
    all_to_all x1, starting transfers between devices, shards(): lax.all_to_all(second.reshape(members, rows, 2 * LANES), 'seq', 0, 0, til...  19.7 us
    all_to_all x1, waiting for transfers between devices, shards(): lax.all_to_all(out_blocks, 'seq', 0, 0, tiled=True).reshape(width, 3, cols)  18 us
    pallas_call x1, Pallas kernels, run_scan(): pl.pallas_call(functools.partial(scan_kernel, rank, states, width // LANE...  15.8 us
    dot_general x6, matrix products, product(): lax.dot_general(values, factor_all, (((0, 2), (0, 1)), ((), ())), preferr...  15.2 us
    unnamed x152, local copies, waits for them, and re-layouts  14.2 us
    ppermute x2, waiting for transfers between devices, from_behind(): return lax.ppermute(block, axis, route)  14.1 us
    dot_general x9, matrix products, dot(): lax.dot_general(first, second, (contract, ((), ())), preferred_element_ty...  13.3 us
  transfers between devices with their start and end apart: 20, of which 9 were waited for; matrix products, arithmetic and copies ran while one was open for 30% of the time, Pallas kernels for 6%

commit v1 on v0

v1 whole, which is shorter than its diff:
```python
import functools

import jax
import jax.numpy as jnp
from jax import lax
from jax.experimental import pallas as pl
from jax.experimental.pallas import tpu as pltpu
from jax.sharding import PartitionSpec as P

NORM_EPS = 1e-05
LANES = 128
PLANE = 4
CHUNKS = 8
LOG2E = 1.4426950408889634
LN2 = 0.6931471805599453
FAR = 1e30
MIB = 1024 * 1024
TAP_BIAS, STEP_BIAS, SKIP, GAIN = 0, 1, 2, 3


def sigmoid(value):
    return 1.0 / (1.0 + jnp.exp(-value))


def silu_grad(value):
    sigma = sigmoid(value)
    return sigma * (1.0 + value * (1.0 - sigma))


def softplus(value):
    small = jnp.exp(-jnp.abs(value))
    series = small * (1.0 - small * (0.5 - small * (1.0 / 3.0 - small * 0.25)))
    return jnp.maximum(value, 0.0) + jnp.where(small < 0.01, series, jnp.log(1.0 + small))


def dot(first, second, contract):
    return lax.dot_general(
        first, second, (contract, ((), ())), preferred_element_type=jnp.float32
    )


def strided(number, length):
    return pl.ds(number, CHUNKS, stride=length // CHUNKS)


def spread(proj_ref, first, table_ref, states, length):
    for place in range(length // CHUNKS):
        rows = proj_ref[strided(place, length), :]
        for state in range(states):
            column = rows[:, first + state : first + state + 1]
            start = (place * states + state) * CHUNKS
            table_ref[start : start + CHUNKS, :] = jnp.broadcast_to(column, (CHUNKS, LANES))


def tile(ref, place, state, states):
    start = (place * states + state) * CHUNKS
    return ref[start : start + CHUNKS, :]


def row(ref, number):
    return ref[number : number + 1, :]


def inverse_rms(tokens):
    return lax.rsqrt(jnp.mean(tokens * tokens, axis=1, keepdims=True) + NORM_EPS)


def columns(masks_ref, tap):
    return jnp.broadcast_to(row(masks_ref, tap), (LANES, masks_ref.shape[1])).T


def two_rows(line):
    high = line.astype(jnp.bfloat16).astype(jnp.float32)
    number = lax.broadcasted_iota(jnp.int32, (2 * CHUNKS, line.shape[1]), 0)
    return jnp.where(number == 0, high, jnp.where(number == 1, line - high, 0.0)).astype(jnp.bfloat16)


def group_at(group):
    return pl.ds(pl.multiple_of(group * LANES, LANES), LANES)


def params():
    return pltpu.CompilerParams(vmem_limit_bytes=64 * MIB)


def cost(us):
    return pl.CostEstimate(flops=0, bytes_accessed=int(us * 3e6), transcendentals=0)


def shifted(block, rim, back):
    if back == 0:
        return block
    moved = pltpu.roll(block, back, 0)
    near = lax.broadcasted_iota(jnp.int32, (CHUNKS, block.shape[1]), 0)
    top = jnp.where(near < back, pltpu.roll(rim, back, 0), moved[:CHUNKS])
    return jnp.concatenate([top, moved[CHUNKS:]], axis=0)


def enter_kernel(
    kernel, scan_width,
    tokens_ref, rim_tokens_ref, cot_ref, tap_bias_ref, step_bias_ref, skip_ref, gain_ref, masks_ref,
    conv_w_ref, gate_w_ref, out_w_ref, taps_ref, weight_ref,
    conv_ref, rim_ref, out_ref, gate_ref, gg_ref, normed_ref, proj_ref, stacked_ref,
    both_ref, mask_ref, bias_ref,
):
    length = tokens_ref.shape[0]
    block = conv_w_ref.shape[1]

    @pl.when(pl.program_id(0) == 0)
    def _():
        for number, ref in enumerate((tap_bias_ref, step_bias_ref, skip_ref, gain_ref)):
            stacked_ref[number : number + 1, :] = ref[...].reshape(1, ref.shape[0])
        for tap in range(kernel):
            mask_ref[tap] = columns(masks_ref, tap)
        gain = row(stacked_ref, GAIN)
        tokens = tokens_ref[...].astype(jnp.float32)
        normed = (tokens * inverse_rms(tokens) * gain).astype(jnp.bfloat16)
        rim = rim_tokens_ref[...].astype(jnp.float32)
        rim = (rim * inverse_rms(rim) * gain).astype(jnp.bfloat16)
        normed_ref[...] = normed
        both_ref[:length, :] = normed
        both_ref[length:, :] = jnp.concatenate([rim, rim], axis=0)
        proj_ref[...] = jnp.zeros_like(proj_ref)

    normed = both_ref[...]
    conv_in = dot(normed, conv_w_ref[...], ((1,), (0,))).astype(jnp.bfloat16)
    conv_ref[...] = conv_in[:length]
    wide = conv_in[:length].astype(jnp.float32)
    rim = conv_in[length : length + CHUNKS].astype(jnp.float32)
    rim_ref[...] = rim
    at = pl.ds(pl.multiple_of(pl.program_id(0) * block, LANES), block)
    total = jnp.broadcast_to(stacked_ref[TAP_BIAS : TAP_BIAS + 1, at], (length, block))
    for tap in range(kernel):
        mask = jnp.concatenate([mask_ref[tap]] * (block // LANES), axis=1)
        total = total + row(taps_ref, tap) * shifted(wide, rim, kernel - 1 - tap) * mask
    out = (total * sigmoid(total)).astype(jnp.bfloat16)
    out_ref[...] = out
    proj_ref[:, :scan_width] += dot(out, weight_ref[...], ((1,), (1,)))
    gate_ref[...] = dot(normed[:length], gate_w_ref[...], ((1,), (0,)))
    gg_ref[...] = dot(cot_ref[...], out_w_ref[...], ((1,), (1,)))


def run_enter(tokens, rim, cot, vectors, masks, conv_w, gate_w, out_w, taps, weight):
    length, model = tokens.shape
    width = conv_w.shape[1]
    block = 3 * LANES
    f32, bf16 = jnp.float32, jnp.bfloat16
    flat = pl.BlockSpec(memory_space=pltpu.VMEM)
    return pl.pallas_call(
        functools.partial(enter_kernel, taps.shape[0], weight.shape[0]),
        grid=(width // block,),
        in_specs=[whole(length, model), whole(CHUNKS, model), whole(length, model)] + [flat] * 4 + [
            whole(*masks.shape), column_block(model, block), column_block(model, block),
            pl.BlockSpec((block, model), lambda g: (g, 0)), column_block(taps.shape[0], block),
            column_block(weight.shape[0], block),
        ],
        out_specs=[
            column_block(length, block), column_block(CHUNKS, block), column_block(length, block),
            column_block(length, block), column_block(length, block), whole(length, model),
            whole(length, LANES), whole(len(vectors), width),
        ],
        out_shape=[
            jax.ShapeDtypeStruct((length, width), bf16), jax.ShapeDtypeStruct((CHUNKS, width), f32),
            jax.ShapeDtypeStruct((length, width), bf16), jax.ShapeDtypeStruct((length, width), f32),
            jax.ShapeDtypeStruct((length, width), f32), jax.ShapeDtypeStruct((length, model), bf16),
            jax.ShapeDtypeStruct((length, LANES), f32),
            jax.ShapeDtypeStruct((len(vectors), width), f32),
        ],
        scratch_shapes=[
            pltpu.VMEM((length + 2 * CHUNKS, model), bf16),
            pltpu.VMEM((taps.shape[0], length, LANES), f32), pltpu.VMEM((8, LANES), f32),
        ],
        compiler_params=params(), cost_estimate=cost(6), name="enter",
    )(tokens, rim, cot, *vectors, masks, conv_w, gate_w, out_w, taps, weight)


def early_kernel(members, where_ref, normed_ref, cot_ref, *rest):
    early_refs, turned_ref = rest[:PLANE], rest[PLANE]
    model = normed_ref.shape[1]
    for group in range(model // LANES):
        at = slice(group * LANES, (group + 1) * LANES)
        turned_ref[at, :] = normed_ref[:, at].astype(jnp.float32).T
        turned_ref[model + group * LANES : model + (group + 1) * LANES, :] = (
            cot_ref[:, at].astype(jnp.float32).T
        )
    rows, lines = model // members, members // PLANE
    for mask, early_ref in enumerate(early_refs):
        place = jnp.bitwise_xor(where_ref[0] % PLANE, mask)
        for source in range(2):
            pieces = []
            for line in range(lines):
                first = source * model + (line * PLANE + place) * rows
                if rows % 8 == 0:
                    first = pl.multiple_of(first, 8)
                pieces.append(turned_ref[pl.ds(first, rows), :])
            at = slice(source * lines * rows, (source + 1) * lines * rows)
            early_ref[at, :] = jnp.concatenate(pieces, axis=0).astype(jnp.bfloat16)


def run_early(where, normed, cot):
    length, model = normed.shape
    members = lax.axis_size("seq")
    vmem = pl.BlockSpec(memory_space=pltpu.VMEM)
    early = jax.ShapeDtypeStruct((2 * model // PLANE, length), jnp.bfloat16)
    return pl.pallas_call(
        functools.partial(early_kernel, members),
        in_specs=[pl.BlockSpec(memory_space=pltpu.SMEM), vmem, vmem],
        out_specs=[vmem] * PLANE, out_shape=[early] * PLANE,
        scratch_shapes=[pltpu.VMEM((2 * model, length), jnp.float32)],
        compiler_params=params(), cost_estimate=cost(3), name="early",
    )(where, normed, cot)


def ends_kernel(
    rank, states,
    own_ref, peer_ref, weight_ref, bias_ref, decay_ref, conv_ref, gg_ref, gate_ref, masks_ref,
    ends_ref, seeds_ref, totals_ref,
    proj_ref, in_ref, out_ref, same_ref, *scratch,
):
    length, width = conv_ref.shape
    proj_ref[...] = own_ref[...] + peer_ref[...]
    spread(proj_ref, rank, in_ref, states, length)
    spread(proj_ref, rank + states, out_ref, states, length)
    same_ref[...] = columns(masks_ref, masks_ref.shape[0] - 2)

    @pl.loop(0, width // LANES)
    def _(group):
        at = group_at(group)
        views = [ref.at[:, at] for ref in (weight_ref, bias_ref, decay_ref, conv_ref, gg_ref, gate_ref)]
        outs = [ref.at[:, at] for ref in (ends_ref, seeds_ref, totals_ref)]
        ends_group(rank, states, *views, *outs, proj_ref, in_ref, out_ref, same_ref, *scratch)


def ends_group(
    rank, states,
    weight_ref, bias_ref, decay_ref, conv_ref, gg_ref, gate_ref,
    ends_ref, seeds_ref, totals_ref,
    proj_ref, in_ref, out_ref, same_ref, long_ref, drive_ref, source_ref, end_ref, seed_ref,
):
    length = conv_ref.shape[0]
    places = length // CHUNKS
    low = proj_ref[:, :rank].astype(jnp.bfloat16)
    step_pre = dot(low, weight_ref[...], ((1,), (0,))) + row(bias_ref, STEP_BIAS)
    step = softplus(step_pre)
    long_ref[...] = jnp.where(same_ref[...] > 0.0, step, FAR)
    drive_ref[...] = step * conv_ref[...].astype(jnp.float32)
    gate = gate_ref[...]
    source_ref[...] = gg_ref[...] * gate * sigmoid(gate)
    rate2 = -jnp.exp(decay_ref[...]) * LOG2E
    rates = [jnp.broadcast_to(rate2[n : n + 1, :], (CHUNKS, LANES)) for n in range(states)]
    hidden = [None] * states
    sums = None
    for place in range(places):
        long = long_ref[strided(place, length), :]
        drive = drive_ref[strided(place, length), :]
        sums = long if place == 0 else sums + long
        for n in range(states):
            term = tile(in_ref, place, n, states) * drive
            hidden[n] = term if place == 0 else jnp.exp2(long * rates[n]) * hidden[n] + term
    for n in range(states):
        end_ref[n * CHUNKS : (n + 1) * CHUNKS, :] = hidden[n]
    back = [None] * states
    for place in reversed(range(places)):
        long = long_ref[strided(place, length), :]
        source = source_ref[strided(place, length), :]
        for n in range(states):
            term = tile(out_ref, place, n, states) * source
            term = term if place == places - 1 else back[n] + term
            back[n] = jnp.exp2(long * rates[n]) * term
    for n in range(states):
        seed_ref[n * CHUNKS : (n + 1) * CHUNKS, :] = back[n]
    ends_ref[...] = end_ref[...]
    seeds_ref[...] = seed_ref[...]
    decays = [jnp.exp2(rate2 * sums[c : c + 1, :]) for c in range(CHUNKS)]
    end = jnp.zeros((states, LANES), jnp.float32)
    seed = jnp.zeros((states, LANES), jnp.float32)
    for c in range(CHUNKS):
        end = decays[c] * end + end_ref[pl.ds(c, states, stride=CHUNKS), :]
    for c in reversed(range(CHUNKS)):
        seed = decays[c] * seed + seed_ref[pl.ds(c, states, stride=CHUNKS), :]
    totals_ref[:states, :] = end.astype(jnp.bfloat16)
    totals_ref[states : 2 * states, :] = seed.astype(jnp.bfloat16)
    totals_ref[2 * states :, :] = two_rows(jnp.sum(sums, axis=0, keepdims=True))


def scan_kernel(
    rank, states, members,
    where_ref, own_ref, peer_ref, weight_ref, bias_ref, decay_ref, conv_ref, gg_ref, gate_ref, masks_ref,
    ends_ref, seeds_ref, near_ref, *rest,
):
    stride, radix = levels(members)[-1]
    far_refs = rest[: radix - 1]
    both_ref, small_ref, gconv_ref, gproj_ref = rest[-22:-18]
    scratch = rest[-18:]
    (
        proj_ref, in_ref, out_ref, long_ref, true_ref, drive_ref, source_ref, same_ref,
        start_ref, last_ref, hidden_ref, in_acc, out_acc, scan_ref, gstep_ref, mix_ref, end_ref, seed_ref,
    ) = scratch
    length, width = conv_ref.shape
    places = length // CHUNKS
    proj_ref[...] = own_ref[...] + peer_ref[...]
    spread(proj_ref, rank, in_ref, states, length)
    spread(proj_ref, rank + states, out_ref, states, length)
    same_ref[...] = columns(masks_ref, masks_ref.shape[0] - 2)
    in_acc[...] = jnp.zeros_like(in_acc)
    out_acc[...] = jnp.zeros_like(out_acc)
    gproj_ref[...] = jnp.zeros_like(gproj_ref)
    digit = where_ref[0] // stride % radix

    @pl.loop(0, width // LANES)
    def _(group):
        at = group_at(group)
        sliced = (
            weight_ref, bias_ref, decay_ref, conv_ref, gg_ref, gate_ref, ends_ref, seeds_ref, near_ref,
            both_ref, gconv_ref,
        )
        views = [ref.at[:, at] for ref in sliced]
        scan_group(
            rank, states, digit, [ref.at[:, at] for ref in far_refs], *views, small_ref.at[at, :],
            gproj_ref, *scratch,
        )

    wide = states * LANES
    source_state = lax.broadcasted_iota(jnp.int32, (wide, LANES), 0) // LANES
    column = lax.broadcasted_iota(jnp.int32, (wide, LANES), 1)
    total = jnp.zeros((length, LANES), jnp.float32)
    for acc, first in ((in_acc, rank), (out_acc, rank + states)):
        pick = jnp.where(source_state + first == column, 1.0, 0.0).astype(jnp.bfloat16)
        value = acc[...]
        high = value.astype(jnp.bfloat16)
        rest = (value - high.astype(jnp.float32)).astype(jnp.bfloat16)
        total = total + dot(high, pick, ((1,), (0,))) + dot(rest, pick, ((1,), (0,)))
    scan_ref[...] = total
    for place in range(places):
        mix_ref[strided(place, length), :] = scan_ref[place * CHUNKS : (place + 1) * CHUNKS, :]
    gproj_ref[...] += mix_ref[...]


def scan_group(
    rank, states, digit, far_refs,
    weight_ref, bias_ref, decay_ref, conv_ref, gg_ref, gate_ref, ends_ref, seeds_ref, near_ref,
    both_ref, gconv_ref, small_ref, gproj_ref,
    proj_ref, in_ref, out_ref, long_ref, true_ref, drive_ref, source_ref, same_ref,
    start_ref, last_ref, hidden_ref, in_acc, out_acc, scan_ref, gstep_ref, mix_ref, end_ref, seed_ref,
):
    length = conv_ref.shape[0]
    places = length // CHUNKS
    low = proj_ref[:, :rank].astype(jnp.bfloat16)
    step_pre = dot(low, weight_ref[...], ((1,), (0,))) + row(bias_ref, STEP_BIAS)
    step = softplus(step_pre)
    conv = conv_ref[...].astype(jnp.float32)
    gate = gate_ref[...]
    gg = gg_ref[...]
    sigma = sigmoid(gate)
    act = gate * sigma
    source_all = gg * act
    true_ref[...] = step
    long_ref[...] = jnp.where(same_ref[...] > 0.0, step, FAR)
    drive_ref[...] = step * conv
    source_ref[...] = source_all
    rate = -jnp.exp(decay_ref[...])
    rate2 = rate * LOG2E
    rates = [jnp.broadcast_to(rate2[n : n + 1, :], (CHUNKS, LANES)) for n in range(states)]
    sums = long_ref[strided(0, length), :]
    for place in range(1, places):
        sums = sums + long_ref[strided(place, length), :]
    decays = [jnp.exp2(rate2 * sums[c : c + 1, :]) for c in range(CHUNKS)]
    carry, incoming = arrive(digit, rate2, near_ref, far_refs, states)
    end_ref[...] = ends_ref[...]
    seed_ref[...] = seeds_ref[...]
    state = carry
    for c in range(CHUNKS):
        start_ref[pl.ds(c, states, stride=CHUNKS), :] = state
        state = decays[c] * state + end_ref[pl.ds(c, states, stride=CHUNKS), :]
    state = incoming
    for c in reversed(range(CHUNKS)):
        last_ref[pl.ds(c, states, stride=CHUNKS), :] = state
        state = decays[c] * state + seed_ref[pl.ds(c, states, stride=CHUNKS), :]

    hidden = [start_ref[n * CHUNKS : (n + 1) * CHUNKS, :] for n in range(states)]
    for place in range(places):
        long = long_ref[strided(place, length), :]
        drive = drive_ref[strided(place, length), :]
        source = source_ref[strided(place, length), :]
        rows = slice(place * CHUNKS, (place + 1) * CHUNKS)
        scan = None
        for n in range(states):
            lanes = slice(n * LANES, (n + 1) * LANES)
            value = jnp.exp2(long * rates[n]) * hidden[n] + tile(in_ref, place, n, states) * drive
            hidden[n] = value
            if place < places - 1:
                hidden_ref[(place * states + n) * CHUNKS : (place * states + n + 1) * CHUNKS, :] = value
            part = tile(out_ref, place, n, states) * value
            scan = part if n == 0 else scan + part
            out_acc[rows, lanes] += source * value
        scan_ref[strided(place, length), :] = scan

    back = [last_ref[n * CHUNKS : (n + 1) * CHUNKS, :] for n in range(states)]
    logs = [None] * states
    for place in reversed(range(places)):
        long = long_ref[strided(place, length), :]
        true = true_ref[strided(place, length), :]
        drive = drive_ref[strided(place, length), :]
        source = source_ref[strided(place, length), :]
        rows = slice(place * CHUNKS, (place + 1) * CHUNKS)
        gstep = None
        mixed = None
        for n in range(states):
            lanes = slice(n * LANES, (n + 1) * LANES)
            grad = back[n] + tile(out_ref, place, n, states) * source
            previous = (
                start_ref[n * CHUNKS : (n + 1) * CHUNKS, :] if place == 0
                else tile(hidden_ref, place - 1, n, states)
            )
            back[n] = jnp.exp2(long * rates[n]) * grad
            log = back[n] * previous
            part = log * true
            logs[n] = part if logs[n] is None else logs[n] + part
            part = log * rates[n]
            gstep = part if n == 0 else gstep + part
            part = grad * tile(in_ref, place, n, states)
            mixed = part if n == 0 else mixed + part
            in_acc[rows, lanes] += grad * drive
        gstep_ref[strided(place, length), :] = gstep
        mix_ref[strided(place, length), :] = mixed

    scan_out = scan_ref[...] + row(bias_ref, SKIP) * conv
    gated = scan_out * act
    ggate = gg * scan_out * sigma * (1.0 + gate * (1.0 - sigma))
    mix = mix_ref[...]
    gconv_ref[...] = source_all * row(bias_ref, SKIP) + mix * step
    gpre = (gstep_ref[...] * LN2 + mix * conv) * sigmoid(step_pre)
    gpre_low = gpre.astype(jnp.bfloat16)
    gproj_ref[:, :rank] += dot(gpre_low, weight_ref[...], ((1,), (1,)))
    step_part = dot(gpre_low, proj_ref[...].astype(jnp.bfloat16), ((0,), (0,)))
    row_number = lax.broadcasted_iota(jnp.int32, (LANES, LANES), 0)
    table = jnp.where(row_number == rank + states, jnp.sum(gpre, axis=0, keepdims=True), 0.0)
    table = jnp.where(
        row_number == rank + states + 1, jnp.sum(source_all * conv, axis=0, keepdims=True), table
    )
    for n in range(states):
        value = jnp.sum(logs[n], axis=0, keepdims=True) * rate[n : n + 1, :]
        table = jnp.where(row_number == rank + n, value, table)
    lane_number = lax.broadcasted_iota(jnp.int32, (LANES, LANES), 1)
    small = jnp.where(lane_number < rank, step_part, table.T)
    both_ref[:length, :] = gated.astype(jnp.bfloat16)
    both_ref[length:, :] = ggate.astype(jnp.bfloat16)
    small_ref[...] = small.astype(jnp.bfloat16)


def column_block(rows, width=LANES):
    return pl.BlockSpec((rows, width), lambda g: (0, g))


def whole(*shape):
    return pl.BlockSpec(shape, lambda g: (0,) * len(shape))


def run_ends(own, peer, weight, stacked, decay_log, conv, gg, gate, masks):
    length, width = conv.shape
    rank, states = weight.shape[0], decay_log.shape[0]
    tall = length // CHUNKS * states * CHUNKS
    f32 = jnp.float32
    block = pltpu.VMEM((length, LANES), f32)
    vmem = pl.BlockSpec(memory_space=pltpu.VMEM)
    return pl.pallas_call(
        functools.partial(ends_kernel, rank, states),
        in_specs=[vmem] * 9, out_specs=[vmem] * 3,
        out_shape=[
            jax.ShapeDtypeStruct((states * CHUNKS, width), f32),
            jax.ShapeDtypeStruct((states * CHUNKS, width), f32),
            jax.ShapeDtypeStruct((2 * states + 2 * CHUNKS, width), jnp.bfloat16),
        ],
        scratch_shapes=[
            block, pltpu.VMEM((tall, LANES), f32), pltpu.VMEM((tall, LANES), f32),
            block, block, block, block,
            pltpu.VMEM((states * CHUNKS, LANES), f32), pltpu.VMEM((states * CHUNKS, LANES), f32),
        ],
        compiler_params=params(), cost_estimate=cost(8), name="ends",
    )(own, peer, weight, stacked, decay_log, conv, gg, gate, masks)


def run_scan(where, own, peer, weight, stacked, decay_log, conv, gg, gate, masks, ends, seeds, near, far, deps):
    length, width = conv.shape
    members = lax.axis_size("seq")
    rank, states = weight.shape[0], decay_log.shape[0]
    places = length // CHUNKS
    tall = places * states * CHUNKS
    f32, bf16 = jnp.float32, jnp.bfloat16
    block = pltpu.VMEM((length, LANES), f32)
    table = pltpu.VMEM((tall, LANES), f32)
    vmem = pl.BlockSpec(memory_space=pltpu.VMEM)
    return pl.pallas_call(
        functools.partial(scan_kernel, rank, states, members),
        in_specs=[pl.BlockSpec(memory_space=pltpu.SMEM)] + [vmem] * (12 + len(far))
        + [pl.BlockSpec(memory_space=pl.ANY) for _ in deps],
        out_specs=[vmem] * 4,
        out_shape=[
            jax.ShapeDtypeStruct((2 * length, width), bf16),
            jax.ShapeDtypeStruct((width, LANES), bf16),
            jax.ShapeDtypeStruct((length, width), f32),
            jax.ShapeDtypeStruct((length, LANES), f32),
        ],
        scratch_shapes=[
            block, table, table, block, block, block, block, block,
            pltpu.VMEM((states * CHUNKS, LANES), f32), pltpu.VMEM((states * CHUNKS, LANES), f32),
            table, pltpu.VMEM((length, states * LANES), f32),
            pltpu.VMEM((length, states * LANES), f32), block, block, block,
            pltpu.VMEM((states * CHUNKS, LANES), f32), pltpu.VMEM((states * CHUNKS, LANES), f32),
        ],
        compiler_params=params(), cost_estimate=cost(15), name="scan",
    )(where, own, peer, weight, stacked, decay_log, conv, gg, gate, masks, ends, seeds, near, *far, *deps)


def levels(members):
    found, stride = [], 1
    while stride < members:
        radix = 4 if members // stride % 4 == 0 else 2
        found.append((stride, radix))
        stride *= radix
    return found


def chosen(refs, own, hop):
    value = own
    for mask, ref in enumerate(refs, 1):
        value = jnp.where(hop == mask, ref[...].astype(jnp.float32), value)
    return value


def arrive(digit, rate2, near_ref, far_refs, states):
    near = near_ref[...]
    radix = len(far_refs) + 1
    carry = jnp.zeros_like(rate2)
    incoming = jnp.zeros_like(rate2)
    blank = jnp.zeros(far_refs[0].shape, jnp.float32)
    for number in range(radix):
        value = chosen(far_refs, blank, digit ^ number)
        decay = jnp.exp2(rate2 * (value[states : states + 1] + value[states + 1 : states + 2]))
        carry = jnp.where(number < digit, decay * carry + value[:states], carry)
    for number in reversed(range(radix)):
        value = chosen(far_refs, blank, digit ^ number)
        decay = jnp.exp2(rate2 * (value[states : states + 1] + value[states + 1 : states + 2]))
        incoming = jnp.where(number > digit, decay * incoming + value[:states], incoming)
    before, behind = near[2 * states : 2 * states + 1], near[2 * states + 1 : 2 * states + 2]
    carry = near[:states] + jnp.exp2(rate2 * before) * carry
    incoming = near[states : 2 * states] + jnp.exp2(rate2 * behind) * incoming
    return carry, incoming


def fold_kernel(states, level, members, start, where_ref, decay_ref, *refs):
    stride, radix = levels(members)[level]
    next_stride, next_radix = levels(members)[level + 1]
    last = level + 2 == len(levels(members))
    digit = where_ref[0] // stride % radix
    if not start:
        old = refs[0][...]
        refs = refs[1:]
    own = refs[0][...]
    got = refs[1:radix]
    near_ref, outs = refs[radix], refs[radix + 1 :]
    rate2 = -jnp.exp(decay_ref[...]) * LOG2E
    own = own.astype(jnp.float32)
    values = [chosen(got, own, digit ^ number) for number in range(radix)]
    first = 2 * states
    sums = [value[first : first + 1] + value[first + 1 : first + 2] for value in values]
    decays = [jnp.exp2(rate2 * one) for one in sums]
    zero, line = jnp.zeros_like(rate2), jnp.zeros_like(sums[0])
    end, seed, carry, incoming, before, behind, total = zero, zero, zero, zero, line, line, line
    for number in range(radix):
        part = values[number][:states]
        end = decays[number] * end + part
        carry = jnp.where(number < digit, decays[number] * carry + part, carry)
        before = jnp.where(number < digit, before + sums[number], before)
        total = total + sums[number]
    for number in reversed(range(radix)):
        part = values[number][states : 2 * states]
        seed = decays[number] * seed + part
        incoming = jnp.where(number > digit, decays[number] * incoming + part, incoming)
        behind = jnp.where(number > digit, behind + sums[number], behind)
    if not start:
        old_before, old_behind = old[2 * states : 2 * states + 1], old[2 * states + 1 : 2 * states + 2]
        carry = old[:states] + jnp.exp2(rate2 * old_before) * carry
        incoming = old[states : 2 * states] + jnp.exp2(rate2 * old_behind) * incoming
        before, behind = before + old_before, behind + old_behind
    pad = jnp.zeros((6, line.shape[1]), jnp.float32)
    near_ref[...] = jnp.concatenate([carry, incoming, before, behind, pad], axis=0)
    tail = two_rows(total)
    if last:
        next_digit = where_ref[0] // next_stride % next_radix
        for mask, out in enumerate(outs, 1):
            value = jnp.where(next_digit < (next_digit ^ mask), end, seed)
            out[:states, :] = value.astype(jnp.bfloat16)
            out[states:, :] = tail
    else:
        outs[0][: 2 * states, :] = jnp.concatenate([end, seed], axis=0).astype(jnp.bfloat16)
        outs[0][2 * states :, :] = tail


def run_fold(level, where, decay_log, near, parts):
    states, width = decay_log.shape
    members = lax.axis_size("seq")
    f32, bf16 = jnp.float32, jnp.bfloat16
    vmem = pl.BlockSpec(memory_space=pltpu.VMEM)
    tall = jax.ShapeDtypeStruct((2 * states + 8, width), f32)
    if level + 2 == len(levels(members)):
        sent = [jax.ShapeDtypeStruct((states + 2 * CHUNKS, width), bf16)] * (levels(members)[-1][1] - 1)
    else:
        sent = [jax.ShapeDtypeStruct((2 * states + 2 * CHUNKS, width), bf16)]
    extra = [] if near is None else [near]
    return pl.pallas_call(
        functools.partial(fold_kernel, states, level, members, near is None),
        in_specs=[pl.BlockSpec(memory_space=pltpu.SMEM)] + [vmem] * (1 + len(extra) + len(parts)),
        out_specs=[vmem] * (1 + len(sent)),
        out_shape=[tall] + sent,
        compiler_params=params(), cost_estimate=cost(2), name="fold",
    )(where, decay_log, *extra, *parts)


def exchange(where, totals, decay_log):
    members = lax.axis_size("seq")
    found = levels(members)
    near = None
    for level, (stride, radix) in enumerate(found[:-1]):
        parts = [totals] + [hop(totals, mask * stride) for mask in range(1, radix)]
        near, *sent = run_fold(level, where, decay_log, near, parts)
        totals = sent[0]
    stride, radix = found[-1]
    return near, [hop(one, mask * stride) for mask, one in enumerate(sent, 1)]


def taps_kernel(
    kernel, ndeps,
    own_ref, peer_ref, conv_ref, in_ref, ext_ref, weight_ref, gconv_ref, taps_ref, params_ref, masks_ref,
    first_small_ref, *rest,
):
    main_ref, rim_ref, small_ref = rest[ndeps:]
    length, total_width = conv_ref.shape
    width = weight_ref.shape[0]
    grad_proj = (own_ref[...] + peer_ref[...]).astype(jnp.bfloat16)
    masks = [columns(masks_ref, tap) for tap in range(kernel)]
    row_number = lax.broadcasted_iota(jnp.int32, (LANES, LANES), 0)
    lane_number = lax.broadcasted_iota(jnp.int32, (LANES, LANES), 1)
    near_row = lax.broadcasted_iota(jnp.int32, (CHUNKS, LANES), 0)
    token = lax.broadcasted_iota(jnp.int32, (length, LANES), 0)
    for group in range(total_width // LANES):
        at = slice(group * LANES, (group + 1) * LANES)
        taps = [taps_ref[tap : tap + 1, at] for tap in range(kernel)]
        conv_in = in_ref[:, at].astype(jnp.float32)
        ext = ext_ref[:, at]
        seen = [shifted(conv_in, ext, kernel - 1 - tap) * masks[tap] for tap in range(kernel)]
        pre = jnp.broadcast_to(params_ref[TAP_BIAS : TAP_BIAS + 1, at], (length, LANES))
        for tap in range(kernel):
            pre = pre + taps[tap] * seen[tap]
        scan_part = dot(conv_ref[:, at], grad_proj, ((0,), (0,)))
        grad = gconv_ref[:, at] + dot(grad_proj[:, :width], weight_ref[:, at], ((1,), (0,)))
        grad = grad * silu_grad(pre)
        table = jnp.where(row_number == width + kernel, jnp.sum(grad, axis=0, keepdims=True), 0.0)
        main = jnp.zeros((length, LANES), jnp.float32)
        rim = jnp.zeros((CHUNKS, LANES), jnp.float32)
        for tap in range(kernel):
            back = kernel - 1 - tap
            part = jnp.sum(grad * seen[tap], axis=0, keepdims=True)
            table = jnp.where(row_number == width + tap, part, table)
            masked = grad * masks[tap] * taps[tap]
            if back == 0:
                main = main + masked
            else:
                moved = pltpu.roll(masked, length - back, 0)
                main = main + jnp.where(token < length - back, moved, 0.0)
                rim = rim + jnp.where(
                    near_row >= CHUNKS - back, pltpu.roll(masked[:CHUNKS], CHUNKS - back, 0), 0.0
                )
        main_ref[:, at] = main
        rim_ref[:, at] = rim
        small_ref[at, :LANES] = first_small_ref[at, :]
        small_ref[at, LANES:] = jnp.where(lane_number < width, scan_part, table.T).astype(jnp.bfloat16)


def run_taps(own, peer, conv, conv_in, ext, weight, gconv, taps, stacked, masks, small, deps):
    length, width = conv.shape
    kernel = taps.shape[0]
    f32 = jnp.float32
    vmem = pl.BlockSpec(memory_space=pltpu.VMEM)
    return pl.pallas_call(
        functools.partial(taps_kernel, kernel, len(deps)),
        in_specs=[vmem] * 11 + [pl.BlockSpec(memory_space=pl.ANY) for _ in deps],
        out_specs=[vmem] * 3,
        out_shape=[
            jax.ShapeDtypeStruct((length, width), f32),
            jax.ShapeDtypeStruct((CHUNKS, width), f32),
            jax.ShapeDtypeStruct((width, 2 * LANES), jnp.bfloat16),
        ],
        compiler_params=params(), cost_estimate=cost(4), name="taps",
    )(own, peer, conv, conv_in, ext, weight, gconv, taps, stacked, masks, small, *deps)


def inputs_kernel(
    ndeps, main_ref, rim_ref, weight_ref, gate_part_ref, tokens_ref, *rest,
):
    low_ref, normed_ref = rest[ndeps:]
    length, width = main_ref.shape
    main = main_ref[...]
    low = jnp.concatenate(
        [main[: length - CHUNKS], main[length - CHUNKS :] + rim_ref[...]], axis=0
    ).astype(jnp.bfloat16)
    normed = dot(low, weight_ref[...], ((1,), (1,))) + gate_part_ref[...]
    normed_ref[...] = normed
    tokens = tokens_ref[...].astype(jnp.float32)
    gain = jnp.sum(normed * tokens * inverse_rms(tokens), axis=0, keepdims=True)
    low_ref[:length, :] = low
    low_ref[length:, :] = two_rows(gain)


def run_inputs(main, rim, weight, gate_part, tokens, deps):
    length, width = main.shape
    return pl.pallas_call(
        functools.partial(inputs_kernel, len(deps)),
        in_specs=[pl.BlockSpec(memory_space=pltpu.VMEM)] * 5
        + [pl.BlockSpec(memory_space=pl.ANY) for _ in deps],
        out_shape=[
            jax.ShapeDtypeStruct((length + 2 * CHUNKS, width), jnp.bfloat16),
            jax.ShapeDtypeStruct((length, weight.shape[0]), jnp.float32),
        ],
        compiler_params=params(), cost_estimate=cost(3), name="inputs",
    )(main, rim, weight, gate_part, tokens, *deps)


def pick(rows, lanes, shift):
    row = lax.broadcasted_iota(jnp.int32, (rows, lanes), 0)
    lane = lax.broadcasted_iota(jnp.int32, (rows, lanes), 1)
    return jnp.where(lane == row + shift, 1.0, 0.0).astype(jnp.bfloat16)


def products_kernel(
    halves, members, gain, ndeps,
    where_ref, e0_ref, e1_ref, e2_ref, e3_ref, here_ref, x_ref, y_ref, first_ref, second_ref,
    *rest,
):
    kept_ref, *sent_refs, total_ref = rest[ndeps:]
    f32, bf16 = jnp.float32, jnp.bfloat16
    lines = members // PLANE
    tall, width = here_ref.shape
    length = e0_ref.shape[1]
    share = e0_ref.shape[0] // 2
    rows = share // lines
    early = (e0_ref, e1_ref, e2_ref, e3_ref)
    cut = tall // 2
    for number, half in enumerate(halves):
        at = slice(number * length, (number + 1) * length)
        total = None
        for mask in range(PLANE):
            if mask < 3:
                late = (here_ref, x_ref, y_ref)[mask][at, :]
            else:
                late = jnp.concatenate([first_ref[...], second_ref[...]], axis=0)[at]
            part = dot(early[mask][half * share : (half + 1) * share, :], late, ((1,), (0,)))
            total = part if total is None else total + part
        for line in range(lines):
            total_ref[line, number * rows : (number + 1) * rows, :] = total[line * rows : (line + 1) * rows]
    if gain:
        last = slice(tall - 2 * CHUNKS, tall)
        line = jnp.zeros((1, width), f32)
        for ref in (here_ref, x_ref, y_ref):
            line = line + jnp.sum(ref[last, :].astype(f32), axis=0, keepdims=True)
        tail = second_ref[second_ref.shape[0] - 2 * CHUNKS :, :]
        line = line + jnp.sum(tail.astype(f32), axis=0, keepdims=True)
        for number in range(lines):
            total_ref[number, len(halves) * rows :, :] = jnp.broadcast_to(
                line, (total_ref.shape[1] - len(halves) * rows, width)
            )
    send(where_ref[0], levels(members)[1:], 0, total_ref, kept_ref, sent_refs, gain)


def split_gain(value, gain):
    if not gain:
        return value.astype(jnp.bfloat16)
    number = value.shape[0] - 2 * CHUNKS
    return jnp.concatenate(
        [value[:number].astype(jnp.bfloat16), two_rows(value[number : number + 1])], axis=0
    )


def send(device, found, level, total_ref, kept_ref, sent_refs, gain):
    stride, radix = found[len(found) - 1 - level]
    digit = device // stride % radix
    size = total_ref.shape[0] // radix
    for mask in range(radix):
        for block in range(size):
            value = total_ref[jnp.bitwise_xor(digit, mask) * size + block]
            if mask == 0:
                kept_ref[block] = value
            else:
                sent_refs[mask - 1][block] = split_gain(value, gain)


def gather_kernel(members, level, gain, where_ref, kept_ref, *refs):
    found = levels(members)[1:]
    radix = found[len(found) - 1 - level][1]
    got, outs = refs[: radix - 1], refs[radix - 1 :]
    total = kept_ref[...]
    number = total.shape[1] - (2 * CHUNKS if gain else 0)
    pieces = total[:, :number, :]
    line = total[:, number : number + 1, :] if gain else None
    for ref in got:
        value = ref[...].astype(jnp.float32)
        pieces = pieces + value[:, :number, :]
        if gain:
            line = line + value[:, number : number + 1, :] + value[:, number + 1 : number + 2, :]
    if level + 1 == len(found):
        if gain:
            outs[0][...] = pieces[0]
            outs[1][...] = line[0]
        else:
            rows = outs[0].shape[0]
            for index, out in enumerate(outs):
                out[...] = pieces[0, index * rows : (index + 1) * rows, :]
        return
    total_ref = refs[-1]
    total_ref[:, :number, :] = pieces
    if gain:
        total_ref[:, number:, :] = jnp.broadcast_to(line, (total.shape[0], 2 * CHUNKS, total.shape[2]))
    send(where_ref[0], found, level + 1, total_ref, outs[0], outs[1:-1], gain)


def gather_plane(late):
    cut = late.shape[0] // 2
    x, y = hop(late, 1), hop(late, 2)
    return late, x, y, hop(x[:cut], 2), hop(y[cut:], 1)


def multiply(halves, where, early, late, gain, deps):
    f32, bf16 = jnp.float32, jnp.bfloat16
    members = lax.axis_size("seq")
    lines = members // PLANE
    width = late[0].shape[1]
    rows = early[0].shape[0] // 2 // lines
    block = len(halves) * rows + (2 * CHUNKS if gain else 0)
    vmem = pl.BlockSpec(memory_space=pltpu.VMEM)
    out_shape = level_shapes(0, lines, block, width)
    return pl.pallas_call(
        functools.partial(products_kernel, halves, members, gain, len(deps)),
        in_specs=[pl.BlockSpec(memory_space=pltpu.SMEM)] + [vmem] * 9
        + [pl.BlockSpec(memory_space=pl.ANY) for _ in deps],
        out_specs=[vmem] * len(out_shape), out_shape=out_shape,
        scratch_shapes=[pltpu.VMEM((lines, block, width), f32)],
        compiler_params=params(), cost_estimate=cost(4), name="products",
    )(where, *early, *late, *deps)


def level_shapes(level, left, block, width):
    found = levels(lax.axis_size("seq"))[1:]
    radix = found[len(found) - 1 - level][1]
    kept = (left // radix, block, width)
    return [jax.ShapeDtypeStruct(kept, jnp.float32)] + [
        jax.ShapeDtypeStruct(kept, jnp.bfloat16)
    ] * (radix - 1)


def add_lines(where, kept, sent, count, gain):
    f32 = jnp.float32
    members = lax.axis_size("seq")
    found = levels(members)[1:]
    vmem = pl.BlockSpec(memory_space=pltpu.VMEM)
    for level in range(len(found)):
        stride, radix = found[len(found) - 1 - level]
        got = [hop(one, mask * stride) for mask, one in enumerate(sent, 1)]
        left, block, width = kept.shape
        scratch = []
        if level + 1 == len(found):
            rows = (block - (2 * CHUNKS if gain else 0)) // count
            out_shape = [jax.ShapeDtypeStruct((rows, width), f32)] * count
            if gain:
                out_shape = out_shape + [jax.ShapeDtypeStruct((1, width), f32)]
        else:
            out_shape = level_shapes(level + 1, left, block, width)
            scratch = [pltpu.VMEM((left, block, width), f32)]
        kept, *sent = pl.pallas_call(
            functools.partial(gather_kernel, members, level, gain),
            in_specs=[pl.BlockSpec(memory_space=pltpu.SMEM)] + [vmem] * (1 + len(got)),
            out_specs=[vmem] * len(out_shape), out_shape=out_shape, scratch_shapes=scratch,
            compiler_params=params(), cost_estimate=cost(2), name="gather",
        )(where, kept, *got)
    return kept, *sent


def place_kernel(counts, got_ref, *refs):
    members, rows, wide = got_ref.shape
    width = members * rows
    table_ref = refs[-1]
    table_ref[...] = jnp.zeros_like(table_ref)
    for source in range(members):
        start = rows * source // LANES * LANES
        at = slice(start, start + 2 * LANES)
        place = pick(rows, 2 * LANES, rows * source - start)
        table_ref[:, at] += dot(got_ref[source], place, ((0,), (0,)))
    for out, (first, count) in zip(refs[:-1], counts, strict=True):
        out[...] = table_ref[first : first + count, :width]


def run_place(got, counts):
    members, rows, wide = got.shape
    width = members * rows
    f32 = jnp.float32
    padded = rows * (members - 1) // LANES * LANES + 2 * LANES
    return pl.pallas_call(
        functools.partial(place_kernel, counts),
        out_shape=[jax.ShapeDtypeStruct((count, width), f32) for _, count in counts],
        scratch_shapes=[pltpu.VMEM((wide, padded), f32)],
        compiler_params=params(), cost_estimate=cost(3), name="place",
    )(got)


def spread_kernel(got_ref, out_ref):
    members = got_ref.shape[0]
    total = got_ref[0].astype(jnp.float32)
    for member in range(1, members):
        total = total + got_ref[member].astype(jnp.float32)
    total = total.astype(out_ref.dtype)
    for member in range(members):
        out_ref[member] = total


def run_spread(got):
    return pl.pallas_call(
        spread_kernel, out_shape=jax.ShapeDtypeStruct(got.shape, got.dtype),
        compiler_params=params(), cost_estimate=cost(2), name="spread",
    )(got)


def from_behind(block, axis, distance):
    devices = range(lax.axis_size(axis))
    route = [(i - distance, i) for i in devices if i - distance in devices]
    return lax.ppermute(block, axis, route)


def swap(block):
    return lax.ppermute(block, "tp", [(0, 1), (1, 0)])


def hop(block, mask):
    members = lax.axis_size("seq")
    return lax.ppermute(block, "seq", [(i, i ^ mask) for i in range(members)])


def shards(
    tokens, norm_gain, in_conv_weight, in_gate_weight, conv_weight, conv_bias, scan_proj_weight,
    step_proj_weight, step_bias, decay_log, skip_gain, out_weight, segment_ids, cotangent,
):
    f32 = jnp.float32
    length, model = tokens.shape
    rank = step_proj_weight.shape[0]
    states = decay_log.shape[0]
    kernel = conv_weight.shape[0]
    width = conv_weight.shape[1]
    members = lax.axis_size("seq")
    device = lax.axis_index("seq")
    where = jnp.stack([device, lax.axis_index("tp")]).astype(jnp.int32)
    rows = width // members
    scan_width = rank + 2 * states
    rim_tokens = from_behind(tokens[length - CHUNKS :], "seq", 1)
    padded_ids = jnp.concatenate([jnp.full((kernel,), -1, jnp.int32), segment_ids])
    near_ids = lax.dynamic_slice_in_dim(padded_ids, device * length, length + kernel)
    masks = jnp.stack(
        [near_ids[kernel:] == near_ids[tap + 1 : tap + 1 + length] for tap in range(kernel)]
    ).astype(f32)
    scan_weight = scan_proj_weight.T

    conv_in, ext, conv_out, gate_in, grad_gated, normed, own, stacked = run_enter(
        tokens, rim_tokens, cotangent, (conv_bias, step_bias, skip_gain, norm_gain), masks,
        in_conv_weight, in_gate_weight, out_weight, conv_weight, scan_weight,
    )
    kept_early, *sent_early = run_early(where, normed, cotangent)
    early = [kept_early] + [hop(one, mask) for mask, one in enumerate(sent_early, 1)]
    peer = swap(own)
    ends, seeds, totals = run_ends(
        own, peer, step_proj_weight, stacked, decay_log, conv_out, grad_gated, gate_in, masks
    )
    near, far = exchange(where, totals, decay_log)
    both, first_small, grad_conv, low_own = run_scan(
        where, own, peer, step_proj_weight, stacked, decay_log, conv_out, grad_gated, gate_in, masks,
        ends, seeds, near, far, early[1:],
    )
    low_peer = swap(low_own)
    main, rim, small = run_taps(
        low_own, low_peer, conv_out, conv_in, ext, scan_weight, grad_conv, conv_weight, stacked, masks,
        first_small, (),
    )
    small = lax.all_to_all(small.reshape(members, rows, 2 * LANES), "seq", 0, 0, tiled=True)
    rim = from_behind(rim, "seq", -1)
    gated, ggate = both[:length], both[length:]
    first_late = gather_plane(both)
    gate_part = dot(ggate, in_gate_weight, ((1,), (1,)))
    low, normed_own = run_inputs(main, rim, in_conv_weight, gate_part, tokens, first_late[1:3])

    tok_float = tokens.astype(f32)
    inv_rms = inverse_rms(tok_float)
    branch_own = dot(gated, out_weight, ((1,), (0,)))
    branch = branch_own + swap(branch_own)
    mixed_out = (tok_float + branch).astype(jnp.bfloat16)
    grad_normed = normed_own + swap(normed_own)
    scaled_grad = grad_normed * norm_gain
    input_grad = (
        cotangent.astype(f32)
        + inv_rms * scaled_grad
        - tok_float * inv_rms * inv_rms * inv_rms
        * jnp.mean(scaled_grad * tok_float, axis=1, keepdims=True)
    )

    first_kept, *first_sent = multiply((1, 0), where, early, first_late, False, ())
    second_kept, *second_sent = multiply((0,), where, early, gather_plane(low), True, (first_kept,))
    out_grad, in_gate_grad = add_lines(where, first_kept, first_sent, 2, False)
    in_conv_grad, gain_grad = add_lines(where, second_kept, second_sent, 1, True)
    small = lax.all_to_all(run_spread(small), "seq", 0, 0, tiled=True)
    step_proj_grad, decay_log_grad, vectors, scan_proj_grad, conv_weight_grad, conv_bias_grad = run_place(
        small,
        (
            (0, rank), (rank, states), (rank + states, 2), (LANES, scan_width),
            (LANES + scan_width, kernel), (LANES + scan_width + kernel, 1),
        ),
    )
    gain_grad = gain_grad + swap(gain_grad)
    return (
        mixed_out, input_grad, gain_grad[0], in_conv_grad, in_gate_grad, conv_weight_grad,
        conv_bias_grad[0], scan_proj_grad.T, step_proj_grad, vectors[0], decay_log_grad, vectors[1],
        out_grad.T,
    )


def solution(mesh):
    in_specs = (
        P("seq", None), P(), P(None, "tp"), P(None, "tp"), P(None, "tp"), P("tp"), P("tp", None),
        P(None, "tp"), P("tp"), P(None, "tp"), P("tp"), P("tp", None), P(), P("seq", None),
    )
    out_specs = (
        P("seq", None), P("seq", None), P(), P("seq", "tp"), P("seq", "tp"), P(None, "tp"), P("tp"),
        P("tp", None), P(None, "tp"), P("tp"), P(None, "tp"), P("tp"), P("tp", "seq"),
    )
    return jax.shard_map(shards, mesh=mesh, in_specs=in_specs, out_specs=out_specs, check_vma=False)
```

time: 282 us -> 204 us (0.72)
  local copies, waits for them, and re-layouts: 55.4 us -> 7.04 us
  Pallas kernels: 24.7 us -> 61.9 us
  matrix products: 28.5 us -> 6.84 us
  other arithmetic: 29.1 us -> 9.09 us
  between operations: 15 us -> 0.76 us
  waiting for transfers between devices: 75.7 us -> 62.8 us
    pallas_call x2 -> x13, Pallas kernels: 24.7 us -> 61.9 us  [the longest x1 17 us: run_scan(): pl.pallas_call(functools.partial(scan_kernel, rank, states, members), in_...]
    all_to_all x4 -> x2, waiting for transfers between devices: 35.5 us -> 0.01 us  [the longest x1 0.01 us: shards(): lax.all_to_all(small.reshape(members, rows, 2 * LANES), 'seq', 0, 0, tile...]
    ppermute x6 -> x23, waiting for transfers between devices: 26.1 us -> 56.2 us  [hop(): return lax.ppermute(block, 'seq', [(i, i ^ mask) for i in range(members)])]
    ppermute x6 -> x23, starting transfers between devices: 6.98 us -> 32.1 us  [hop(): return lax.ppermute(block, 'seq', [(i, i ^ mask) for i in range(members)])]
    all_to_all x4 -> x2, starting transfers between devices: 36.5 us -> 13.6 us  [the longest x1 8.49 us: shards(): small = lax.all_to_all(run_spread(small), 'seq', 0, 0, tiled=True)]
    dot_general x6 -> x0, matrix products: 15.2 us -> none  [product(): lax.dot_general(values, factor_all, (((0, 2), (0, 1)), ((), ())), preferr...]
    unnamed x152 -> x4, local copies, waits for them, and re-layouts: 14.2 us -> 0.72 us
    reshape x4 -> x0, local copies, waits for them, and re-layouts: 11.3 us -> none  [the longest x1 3.37 us: shards(): normed_all = factors[:, :half].reshape(members, length, half)]
  transfers between devices with their start and end apart: 20 -> 32, of which waited for: 9 -> 14; matrix products, arithmetic and copies ran while one was open for 30% -> 9% of each run, Pallas kernels for 6% -> 13%
where the time goes in v1:
time: 204 us; the launch traced here: 202 us
  waiting for transfers between devices  62.8 us (31%)
  Pallas kernels  61.9 us (30%)
  starting transfers between devices  53.6 us (26%)
  other arithmetic  9.09 us (4%)
  local copies, waits for them, and re-layouts  7.04 us (3%)
  matrix products  6.84 us (3%)
    ppermute x23, waiting for transfers between devices, hop(): return lax.ppermute(block, 'seq', [(i, i ^ mask) for i in range(members)])  56.2 us
    ppermute x23, starting transfers between devices, hop(): return lax.ppermute(block, 'seq', [(i, i ^ mask) for i in range(members)])  32.1 us
    pallas_call x1, Pallas kernels, run_scan(): pl.pallas_call(functools.partial(scan_kernel, rank, states, members), in_...  17 us
    pallas_call x1, Pallas kernels, run_ends(): pl.pallas_call(functools.partial(ends_kernel, rank, states), in_specs=[vm...  8.63 us
    all_to_all x1, starting transfers between devices, shards(): small = lax.all_to_all(run_spread(small), 'seq', 0, 0, tiled=True)  8.49 us
    pallas_call x2, Pallas kernels, multiply(): pl.pallas_call(functools.partial(products_kernel, halves, members, gain,...  7.94 us
    ppermute x2, starting transfers between devices, from_behind(): return lax.ppermute(block, axis, route)  7.83 us
    pallas_call x1, Pallas kernels, run_enter(): pl.pallas_call(functools.partial(enter_kernel, taps.shape[0], weight.shap...  7.23 us
  transfers between devices with their start and end apart: 32, of which 14 were waited for; matrix products, arithmetic and copies ran while one was open for 9% of the time, Pallas kernels for 13%

profile of v1, /device:TPU:8, one launch (start us, length us, event | category | flops | bytes accessed | tf_op | source)
XLA Modules:
  0.0 202.1 jit_solution(16632681758141927268)
XLA Ops:
  0.6 0.7 slice.43
  1.4 3.4 %collective-permute-start = (bf16[8,1152]{1,0:T(8,128)(2,1)S(1)}, bf16[8,1152]{1,0:T(8,128)(2,1)}, u32[]{:S(2)}, u32[]{:S(2)}) collective-permute-start(bf16[8,1152]{1,0:T(8,128)(2,1)S(1)} %slice.43), channel_id=1, source_target_pairs={{0,2},{2,4},{4,6},{6,8},{8,10},{10,12},{12,14},{14,16},{16,18},{18... | collective-permute-start | bytes 55304 | tf_op jit(solution)/shard_map/ppermute | solution.py:934
  4.8 0.8 pad_dynamic-slice_fusion
  5.7 0.7 add_convert_fusion.masks_ref
  6.4 2.6 %collective-permute-done.rim_tokens_ref = bf16[8,1152]{1,0:T(8,128)(2,1)} collective-permute-done((bf16[8,1152]{1,0:T(8,128)(2,1)S(1)}, bf16[8,1152]{1,0:T(8,128)(2,1)}, u32[]{:S(2)}, u32[]{:S(2)}) %collective-permute-start) | collective-permute-done | bytes 18464 | tf_op jit(solution)/shard_map/ppermute | solution.py:934
  8.9 7.2 %enter.1 = (bf16[128,1152]{1,0:T(8,128)(2,1)}, f32[8,1152]{1,0:T(8,128)}, bf16[128,1152]{1,0:T(8,128)(2,1)}, f32[128,1152]{1,0:T(8,128)}, f32[128,1152]{1,0:T(8,...) custom-call(bf16[128,1152]{1,0:T(8,128)(2,1)} %tokens_ref.3, ...), custom_call_target="tpu_custom_call" | custom-call | bytes 18000000 | tf_op jit(solution)/shard_map/enter/pallas_call | solution.py:149
  16.2 1.6 collective-permute-done.1.peer_ref
  17.8 8.6 %ends.1 = (f32[128,1152]{1,0:T(8,128)}, f32[128,1152]{1,0:T(8,128)}, bf16[48,1152]{1,0:T(8,128)(2,1)}) custom-call(f32[128,128]{1,0:T(8,128)} %get-tuple-element.59.own_ref, f32[128,128]{1,0:T(8,128)} %collective-permute-done.1.peer_ref, bf16[72,1152]{1,0:T(8,128)(2,1)} %weight_ref.4, f32[4,1152]{1,0:T(4,128)} %get-tuple-element.60.bias_ref.params_ref, ...), custom_call_target="tpu_custom_call" | custom-call | bytes 24000000 | tf_op jit(solution)/shard_map/ends/pallas_call | solution.py:466
  26.4 0.6 pad_add_fusion.where_ref
  27.0 2.1 %early.1 = (bf16[576,128]{1,0:T(8,128)(2,1)}, bf16[576,128]{1,0:T(8,128)(2,1)}, bf16[576,128]{1,0:T(8,128)(2,1)}, bf16[576,128]{1,0:T(8,128)(2,1)}) custom-call(s32[2]{0:T(128)} %pad_add_fusion.where_ref, bf16[128,1152]{1,0:T(8,128)(2,1)} %get-tuple-element.71.normed_ref, bf16[128,1152]{1,0:T(8,128)(2,1)} %cot_ref.3), custom_call_target="tpu_custom_call" | custom-call | bytes 9000000 | tf_op jit(solution)/shard_map/early/pallas_call | solution.py:205
  29.2 2.1 %collective-permute-start.10 = (bf16[576,128]{1,0:T(8,128)(2,1)}, bf16[576,128]{1,0:T(8,128)(2,1)}, u32[]{:S(2)}, u32[]{:S(2)}) collective-permute-start(bf16[576,128]{1,0:T(8,128)(2,1)} %get-tuple-element.74), channel_id=1, source_target_pairs={{0,6},{2,4},{4,2},{6,0},{8,14},{10,12},{12,10},{14,8},{16,22},{18,... | collective-permute-start | bytes 442376 | tf_op jit(solution)/shard_map/ppermute | solution.py:943
  31.2 1.4 collective-permute-start.3
  32.6 0.6 collective-permute-start.4
  33.3 1.4 collective-permute-start.8
  34.7 1.4 collective-permute-start.9
  36.1 5.0 %collective-permute-done.3.refs_2_ = bf16[48,1152]{1,0:T(8,128)(2,1)} collective-permute-done((bf16[48,1152]{1,0:T(8,128)(2,1)}, bf16[48,1152]{1,0:T(8,128)(2,1)}, u32[]{:S(2)}, u32[]{:S(2)}) %collective-permute-start.3) | collective-permute-done | bytes 110624 | tf_op jit(solution)/shard_map/ppermute | solution.py:943
  41.1 2.1 %fold.1 = (f32[40,1152]{1,0:T(8,128)}, bf16[32,1152]{1,0:T(8,128)(2,1)}, bf16[32,1152]{1,0:T(8,128)(2,1)}, bf16[32,1152]{1,0:T(8,128)(2,1)}) custom-call(s32[2]{0:T(128)} %pad_add_fusion.where_ref, f32[16,1152]{1,0:T(8,128)} %decay_ref.5, bf16[48,1152]{1,0:T(8,128)(2,1)} %get-tuple-element.66.refs_0_, bf16[48,1152]{1,0:T(8,128)(2,1)} %collective-permute-done.2.refs_1_, ...), custom_call_target="tpu_custom_call" | custom-call | bytes 6000000 | tf_op jit(solution)/shard_map/fold/pallas_call | solution.py:611
  43.2 3.0 %collective-permute-start.6 = (bf16[32,1152]{1,0:T(8,128)(2,1)}, bf16[32,1152]{1,0:T(8,128)(2,1)}, u32[]{:S(2)}, u32[]{:S(2)}) collective-permute-start(bf16[32,1152]{1,0:T(8,128)(2,1)} %get-tuple-element.69), channel_id=1, source_target_pairs={{0,16},{2,18},{4,20},{6,22},{8,24},{10,26},{12,28},{14,30},{16,0},... | collective-permute-start | bytes 221192 | tf_op jit(solution)/shard_map/ppermute | solution.py:943
  46.3 0.5 collective-permute-start.7
  46.7 1.2 collective-permute-done.5.rest_0_
  47.9 4.0 %collective-permute-done.6.rest_1_ = bf16[32,1152]{1,0:T(8,128)(2,1)} collective-permute-done((bf16[32,1152]{1,0:T(8,128)(2,1)}, bf16[32,1152]{1,0:T(8,128)(2,1)}, u32[]{:S(2)}, u32[]{:S(2)}) %collective-permute-start.6) | collective-permute-done | bytes 73760 | tf_op jit(solution)/shard_map/ppermute | solution.py:943
  51.9 1.7 collective-permute-done.7.rest_2_
  53.6 17.0 %scan.1 = (bf16[256,1152]{1,0:T(8,128)(2,1)}, bf16[1152,128]{1,0:T(8,128)(2,1)}, f32[128,1152]{1,0:T(8,128)}, f32[128,128]{1,0:T(8,128)}) custom-call(s32[2]{0:T(128)} %pad_add_fusion.where_ref, f32[128,128]{1,0:T(8,128)} %get-tuple-element.59.own_ref, f32[128,128]{1,0:T(8,128)} %collective-permute-done.1.peer_ref, bf16[72,1152]{1,0:T(8,128)(2,1)} %weight_ref.4, ...), custom_call_target="tpu_custom_call" | custom-call | bytes 45000000 | tf_op jit(solution)/shard_map/scan/pallas_call | solution.py:493
  70.6 2.2 %collective-permute-start.15 = (bf16[256,1152]{1,0:T(8,128)(2,1)}, bf16[256,1152]{1,0:T(8,128)(2,1)}, u32[]{:S(2)}, u32[]{:S(2)}) collective-permute-start(bf16[256,1152]{1,0:T(8,128)(2,1)} %get-tuple-element.75.here_ref), channel_id=1, source_target_pairs={{0,4},{2,6},{4,0},{6,2},{8,12},{10,14},{12,8},{14,10},{16,20},{18,... | collective-permute-start | bytes 1769480 | tf_op jit(solution)/shard_map/ppermute | solution.py:943
  72.8 1.6 collective-permute-done.12.peer_ref
  74.4 4.0 %taps.1 = (f32[128,1152]{1,0:T(8,128)}, f32[8,1152]{1,0:T(8,128)}, bf16[1152,256]{1,0:T(8,128)(2,1)}) custom-call(f32[128,128]{1,0:T(8,128)} %get-tuple-element.76.own_ref, f32[128,128]{1,0:T(8,128)} %collective-permute-done.12.peer_ref, bf16[128,1152]{1,0:T(8,128)(2,1)} %get-tuple-element.61.conv_ref, bf16[128,1152]{1,0:T(8,128)(2,1)} %get-tuple-element.77.in_ref, ...), custom_call_target="tpu_custom_call" | custom-call | bytes 12000000 | tf_op jit(solution)/shard_map/taps/pallas_call | solution.py:685
  78.4 5.1 %all-to-all-start = ((bf16[16,72,256]{2,1,0:T(8,128)(2,1)}), bf16[16,72,256]{2,1,0:T(8,128)(2,1)}, u32[]{:S(2)}, u32[]{:S(2)}) async-start(bf16[16,72,256]{2,1,0:T(8,128)(2,1)} %bitcast.17), calls=%async_computation | async-start | bytes 1179648 | tf_op jit(solution)/shard_map/all_to_all | solution.py:989
  83.5 4.4 %collective-permute-start.13 = (f32[8,1152]{1,0:T(8,128)}, f32[8,1152]{1,0:T(8,128)}, u32[]{:S(2)}, u32[]{:S(2)}) collective-permute-start(f32[8,1152]{1,0:T(8,128)} %get-tuple-element.82), channel_id=1, source_target_pairs={{2,0},{4,2},{6,4},{8,6},{10,8},{12,10},{14,12},{16,14},{18,16},{20... | collective-permute-start | bytes 110600 | tf_op jit(solution)/shard_map/ppermute | solution.py:934
  88.0 3.6 %fusion.7.gate_part_ref = f32[128,1152]{1,0:T(8,128)} fusion(bf16[1152,1152]{1,0:T(8,128)(2,1)} %gate_w_ref.1, bf16[256,1152]{1,0:T(8,128)(2,1)} %get-tuple-element.75.here_ref), kind=kOutput, calls=%fused_computation.12 | convolution fusion | flops 339738624 | bytes 3538944 | tf_op jit(solution)/shard_map/dot_general | solution.py:37
  91.6 0.8 collective-permute-done.13.rim_ref
  92.4 4.0 %inputs.1 = (bf16[144,1152]{1,0:T(8,128)(2,1)}, f32[128,1152]{1,0:T(8,128)}) custom-call(f32[128,1152]{1,0:T(8,128)} %get-tuple-element.81.main_ref, f32[8,1152]{1,0:T(8,128)} %collective-permute-done.13.rim_ref, bf16[1152,1152]{1,0:T(8,128)(2,1)} %weight_ref.5, f32[128,1152]{1,0:T(8,128)} %fusion.7.gate_part_ref, bf16[128,1152]{1,0:T(8,128)(2,1)} %tokens_ref.3, ...), custom_call_target="tpu_custom_call" | custom-call | bytes 9000000 | tf_op jit(solution)/shard_map/inputs/pallas_call | solution.py:717
  96.4 9.9 %collective-permute-start.18 = (bf16[144,1152]{1,0:T(8,128)(2,1)}, bf16[144,1152]{1,0:T(8,128)(2,1)S(1)}, u32[]{:S(2)}, u32[]{:S(2)}) collective-permute-start(bf16[144,1152]{1,0:T(8,128)(2,1)} %get-tuple-element.85.here_ref), channel_id=1, source_target_pairs={{0,4},{2,6},{4,0},{6,2},{8,12},{10,14},{12,8},{14,10},{16,20},{18,... | collective-permute-start | bytes 995336 | tf_op jit(solution)/shard_map/ppermute | solution.py:943
  106.3 1.0 slice.58
  107.4 1.0 slice.59
  108.4 0.1 collective-permute-start.22
  108.5 3.3 %fusion.9 = f32[128,1152]{1,0:T(8,128)} fusion(bf16[1152,1152]{1,0:T(8,128)(2,1)} %out_w_ref.1, bf16[256,1152]{1,0:T(8,128)(2,1)} %get-tuple-element.75.here_ref), kind=kOutput, calls=%fused_computation.14 | convolution fusion | flops 339738624 | bytes 3538944 | tf_op jit(solution)/shard_map/dot_general | solution.py:37
  111.8 0.7 copy-done
  112.5 0.7 slice.56
  113.2 1.9 collective-permute-done.18.y_ref
  115.2 2.0 %collective-permute-start.19 = (bf16[72,1152]{1,0:T(8,128)(2,1)}, bf16[72,1152]{1,0:T(8,128)(2,1)}, u32[]{:S(2)}, u32[]{:S(2)}) collective-permute-start(bf16[72,1152]{1,0:T(8,128)(2,1)} %slice.56), channel_id=1, source_target_pairs={{0,4},{2,6},{4,0},{6,2},{8,12},{10,14},{12,8},{14,10},{16,20},{18,... | collective-permute-start | bytes 497672 | tf_op jit(solution)/shard_map/ppermute | solution.py:943
  117.2 0.7 slice.57
  117.9 3.7 %collective-permute-done.21.first_ref = bf16[128,1152]{1,0:T(8,128)(2,1)} collective-permute-done((bf16[128,1152]{1,0:T(8,128)(2,1)S(1)}, bf16[128,1152]{1,0:T(8,128)(2,1)}, u32[]{:S(2)}, u32[]{:S(2)}) %collective-permute-start.21) | collective-permute-done | bytes 294944 | tf_op jit(solution)/shard_map/ppermute | solution.py:943
  121.6 0.1 collective-permute-start.20
  121.7 4.6 %products.2 = (f32[1,144,1152]{2,1,0:T(8,128)}, bf16[1,144,1152]{2,1,0:T(8,128)(2,1)}, bf16[1,144,1152]{2,1,0:T(8,128)(2,1)}, bf16[1,144,1152]{2,1,0:T(8,128)(2,1)}) custom-call(s32[2]{0:T(128)} %pad_add_fusion.where_ref, bf16[576,128]{1,0:T(8,128)(2,1)} %get-tuple-element.84.e0_ref, bf16[576,128]{1,0:T(8,128)(2,1)} %collective-permute-done.8.rest_3_.e1_ref, ...), custom_call_target="tpu_custom_call" | custom-call | bytes 12000000 | tf_op jit(solution)/shard_map/products/pallas_call | solution.py:841
  126.3 1.1 collective-permute-done.20.second_ref
  127.4 3.3 %products.3 = (f32[1,88,1152]{2,1,0:T(8,128)}, bf16[1,88,1152]{2,1,0:T(8,128)(2,1)}, bf16[1,88,1152]{2,1,0:T(8,128)(2,1)}, bf16[1,88,1152]{2,1,0:T(8,128)(2,1)}) custom-call(s32[2]{0:T(128)} %pad_add_fusion.where_ref, bf16[576,128]{1,0:T(8,128)(2,1)} %get-tuple-element.84.e0_ref, bf16[576,128]{1,0:T(8,128)(2,1)} %collective-permute-done.8.rest_3_.e1_ref, ...), custom_call_target="tpu_custom_call" | custom-call | bytes 12000000 | tf_op jit(solution)/shard_map/products/pallas_call | solution.py:841
  130.7 0.9 collective-permute-start.23
  131.7 2.0 spread.1
  133.7 8.5 %all-to-all-start.1 = ((bf16[16,72,256]{2,1,0:T(8,128)(2,1)}), bf16[16,72,256]{2,1,0:T(8,128)(2,1)}, u32[]{:S(2)}, u32[]{:S(2)}) async-start(bf16[16,72,256]{2,1,0:T(8,128)(2,1)} %spread.1), calls=%async_computation.1 | async-start | bytes 1179648 | tf_op jit(solution)/shard_map/all_to_all | solution.py:1014
  142.2 1.5 collective-permute-start.25
  143.7 1.6 fusion.1
  145.3 0.5 add_rsqrt_fusion
  145.8 1.0 collective-permute-start.28
  146.8 3.6 %collective-permute-start.29 = (bf16[1,144,1152]{2,1,0:T(8,128)(2,1)}, bf16[1,144,1152]{2,1,0:T(8,128)(2,1)}, u32[]{:S(2)}, u32[]{:S(2)}) collective-permute-start(bf16[1,144,1152]{2,1,0:T(8,128)(2,1)} %get-tuple-element.95), channel_id=1, source_target_pairs={{0,24},{2,26},{4,28},{6,30},{8,16},{10,18},{12,20},{14,22},{16,8},... | collective-permute-start | bytes 995336 | tf_op jit(solution)/shard_map/ppermute | solution.py:943
  150.5 29.4 %collective-permute-done.25.refs_2_ = bf16[1,88,1152]{2,1,0:T(8,128)(2,1)} collective-permute-done((bf16[1,88,1152]{2,1,0:T(8,128)(2,1)}, bf16[1,88,1152]{2,1,0:T(8,128)(2,1)}, u32[]{:S(2)}, u32[]{:S(2)}) %collective-permute-start.25) | collective-permute-done | bytes 202784 | tf_op jit(solution)/shard_map/ppermute | solution.py:943
  179.8 2.0 %gather.2 = (f32[72,1152]{1,0:T(8,128)}, f32[1,1152]{1,0:T(1,128)}) custom-call(s32[2]{0:T(128)} %pad_add_fusion.where_ref, f32[1,88,1152]{2,1,0:T(8,128)} %get-tuple-element.87.kept_ref, bf16[1,88,1152]{2,1,0:T(8,128)(2,1)} %collective-permute-done.23.refs_0_, bf16[1,88,1152]{2,1,0:T(8,128)(2,1)} %collective-permute-done.24.refs_1_, ...), custom_call_target="tpu_custom_call" | custom-call | bytes 6000000 | tf_op jit(solution)/shard_map/gather/pallas_call | solution.py:878
  181.9 3.1 %fusion.5 = (f32[128,1152]{1,0:T(8,128)}, bf16[128,1152]{1,0:T(8,128)(2,1)}) fusion(bf16[128,1152]{1,0:T(8,128)(2,1)} %tokens_ref.3, bf16[128,1152]{1,0:T(8,128)(2,1)} %cot_ref.3, f32[128]{0:T(128)} %get-tuple-element.115, f32[128]{0:T(128)} %get-tuple-element.114, f32[1152]{0:T(1024)} %gain_ref.1, f32[128,1152]{1,0:T(8,128)} %get-tuple-element.83, ...), kind=kLoop, calls=%fused_computation.9 | loop fusion | flops 2064384 | bytes 3839488 | tf_op jit(solution)/shard_map/sub | solution.py:1004
  184.9 2.0 collective-permute-done.28.refs_1_
  186.9 6.2 %collective-permute-done.29.refs_2_ = bf16[1,144,1152]{2,1,0:T(8,128)(2,1)} collective-permute-done((bf16[1,144,1152]{2,1,0:T(8,128)(2,1)}, bf16[1,144,1152]{2,1,0:T(8,128)(2,1)}, u32[]{:S(2)}, u32[]{:S(2)}) %collective-permute-start.29) | collective-permute-done | bytes 331808 | tf_op jit(solution)/shard_map/ppermute | solution.py:943
  193.2 2.3 %gather.3 = (f32[72,1152]{1,0:T(8,128)}, f32[72,1152]{1,0:T(8,128)}) custom-call(s32[2]{0:T(128)} %pad_add_fusion.where_ref, f32[1,144,1152]{2,1,0:T(8,128)} %get-tuple-element.86.rest_0_.kept_ref, bf16[1,144,1152]{2,1,0:T(8,128)(2,1)} %collective-permute-done.27.refs_0_, bf16[1,144,1152]{2,1,0:T(8,128)(2,1)} %collective-permute-done.28.refs_1_, ...), custom_call_target="tpu_custom_call" | custom-call | bytes 6000000 | tf_op jit(solution)/shard_map/gather/pallas_call | solution.py:878
  195.5 1.3 add_reduce_fusion
  196.8 2.6 %place.1 = (f32[72,1152]{1,0:T(8,128)}, f32[16,1152]{1,0:T(8,128)}, f32[2,1152]{1,0:T(2,128)}, f32[104,1152]{1,0:T(8,128)}, f32[4,1152]{1,0:T(4,128)}, /*index=5*/f32[1,1152]{1,0:T(1,128)}) custom-call(bf16[16,72,256]{2,1,0:T(8,128)(2,1)} %all-to-all-done.1.got_ref), custom_call_target="tpu_custom_call" | custom-call | bytes 9000000 | tf_op jit(solution)/shard_map/place/pallas_call | solution.py:906
  199.4 1.4 slice_reduce_fusion
  200.8 1.3 reduce.1
  (35 shorter events, 0.4 us)
Async XLA Ops:
  1.4 7.5 %collective-permute-start = (bf16[8,1152]{1,0:T(8,128)(2,1)S(1)}, bf16[8,1152]{1,0:T(8,128)(2,1)}, u32[]{:S(2)}, u32[]{:S(2)}) collective-permute-start(bf16[8,1152]{1,0:T(8,128)(2,1)S(1)} %slice.43), channel_id=1, source_target_pairs={{0,2},{2,4},{4,6},{6,8},{8,10},{10,12},{12,14},{14,16},{16,18},{18... | collective-permute-start | bytes 55304 | tf_op jit(solution)/shard_map/ppermute | solution.py:934
  16.1 1.7 collective-permute-start.1
  26.4 8.3 %collective-permute-start.2 = (bf16[48,1152]{1,0:T(8,128)(2,1)}, bf16[48,1152]{1,0:T(8,128)(2,1)}, u32[]{:S(2)}, u32[]{:S(2)}) collective-permute-start(bf16[48,1152]{1,0:T(8,128)(2,1)} %get-tuple-element.66.refs_0_), channel_id=1, source_target_pairs={{0,2},{2,0},{4,6},{6,4},{8,10},{10,8},{12,14},{14,12},{16,18},{18,... | collective-permute-start | bytes 331784 | tf_op jit(solution)/shard_map/ppermute | solution.py:943
  29.2 17.1 %collective-permute-start.10 = (bf16[576,128]{1,0:T(8,128)(2,1)}, bf16[576,128]{1,0:T(8,128)(2,1)}, u32[]{:S(2)}, u32[]{:S(2)}) collective-permute-start(bf16[576,128]{1,0:T(8,128)(2,1)} %get-tuple-element.74), channel_id=1, source_target_pairs={{0,6},{2,4},{4,2},{6,0},{8,14},{10,12},{12,10},{14,8},{16,22},{18,... | collective-permute-start | bytes 442376 | tf_op jit(solution)/shard_map/ppermute | solution.py:943
  31.2 9.9 %collective-permute-start.3 = (bf16[48,1152]{1,0:T(8,128)(2,1)}, bf16[48,1152]{1,0:T(8,128)(2,1)}, u32[]{:S(2)}, u32[]{:S(2)}) collective-permute-start(bf16[48,1152]{1,0:T(8,128)(2,1)} %get-tuple-element.66.refs_0_), channel_id=1, source_target_pairs={{0,4},{2,6},{4,0},{6,2},{8,12},{10,14},{12,8},{14,10},{16,20},{18,... | collective-permute-start | bytes 331784 | tf_op jit(solution)/shard_map/ppermute | solution.py:943
  32.6 8.5 %collective-permute-start.4 = (bf16[48,1152]{1,0:T(8,128)(2,1)}, bf16[48,1152]{1,0:T(8,128)(2,1)}, u32[]{:S(2)}, u32[]{:S(2)}) collective-permute-start(bf16[48,1152]{1,0:T(8,128)(2,1)} %get-tuple-element.66.refs_0_), channel_id=1, source_target_pairs={{0,6},{2,4},{4,2},{6,0},{8,14},{10,12},{12,10},{14,8},{16,22},{18,... | collective-permute-start | bytes 331784 | tf_op jit(solution)/shard_map/ppermute | solution.py:943
  33.3 13.4 %collective-permute-start.8 = (bf16[576,128]{1,0:T(8,128)(2,1)}, bf16[576,128]{1,0:T(8,128)(2,1)}, u32[]{:S(2)}, u32[]{:S(2)}) collective-permute-start(bf16[576,128]{1,0:T(8,128)(2,1)} %get-tuple-element.72), channel_id=1, source_target_pairs={{0,2},{2,0},{4,6},{6,4},{8,10},{10,8},{12,14},{14,12},{16,18},{18,... | collective-permute-start | bytes 442376 | tf_op jit(solution)/shard_map/ppermute | solution.py:943
  34.7 12.0 %collective-permute-start.9 = (bf16[576,128]{1,0:T(8,128)(2,1)}, bf16[576,128]{1,0:T(8,128)(2,1)}, u32[]{:S(2)}, u32[]{:S(2)}) collective-permute-start(bf16[576,128]{1,0:T(8,128)(2,1)} %get-tuple-element.73), channel_id=1, source_target_pairs={{0,4},{2,6},{4,0},{6,2},{8,12},{10,14},{12,8},{14,10},{16,20},{18,... | collective-permute-start | bytes 442376 | tf_op jit(solution)/shard_map/ppermute | solution.py:943
  43.2 4.7 %collective-permute-start.5 = (bf16[32,1152]{1,0:T(8,128)(2,1)}, bf16[32,1152]{1,0:T(8,128)(2,1)}, u32[]{:S(2)}, u32[]{:S(2)}) collective-permute-start(bf16[32,1152]{1,0:T(8,128)(2,1)} %get-tuple-element.68), channel_id=1, source_target_pairs={{0,8},{2,10},{4,12},{6,14},{8,0},{10,2},{12,4},{14,6},{16,24},{18,... | collective-permute-start | bytes 221192 | tf_op jit(solution)/shard_map/ppermute | solution.py:943
  43.2 8.6 %collective-permute-start.6 = (bf16[32,1152]{1,0:T(8,128)(2,1)}, bf16[32,1152]{1,0:T(8,128)(2,1)}, u32[]{:S(2)}, u32[]{:S(2)}) collective-permute-start(bf16[32,1152]{1,0:T(8,128)(2,1)} %get-tuple-element.69), channel_id=1, source_target_pairs={{0,16},{2,18},{4,20},{6,22},{8,24},{10,26},{12,28},{14,30},{16,0},... | collective-permute-start | bytes 221192 | tf_op jit(solution)/shard_map/ppermute | solution.py:943
  46.3 7.3 %collective-permute-start.7 = (bf16[32,1152]{1,0:T(8,128)(2,1)}, bf16[32,1152]{1,0:T(8,128)(2,1)}, u32[]{:S(2)}, u32[]{:S(2)}) collective-permute-start(bf16[32,1152]{1,0:T(8,128)(2,1)} %get-tuple-element.70), channel_id=1, source_target_pairs={{0,24},{2,26},{4,28},{6,30},{8,16},{10,18},{12,20},{14,22},{16,8},... | collective-permute-start | bytes 221192 | tf_op jit(solution)/shard_map/ppermute | solution.py:943
  70.6 21.8 %collective-permute-start.14 = (bf16[256,1152]{1,0:T(8,128)(2,1)}, bf16[256,1152]{1,0:T(8,128)(2,1)}, u32[]{:S(2)}, u32[]{:S(2)}) collective-permute-start(bf16[256,1152]{1,0:T(8,128)(2,1)} %get-tuple-element.75.here_ref), channel_id=1, source_target_pairs={{0,2},{2,0},{4,6},{6,4},{8,10},{10,8},{12,14},{14,12},{16,18},{18,... | collective-permute-start | bytes 1769480 | tf_op jit(solution)/shard_map/ppermute | solution.py:943
  70.6 21.8 %collective-permute-start.15 = (bf16[256,1152]{1,0:T(8,128)(2,1)}, bf16[256,1152]{1,0:T(8,128)(2,1)}, u32[]{:S(2)}, u32[]{:S(2)}) collective-permute-start(bf16[256,1152]{1,0:T(8,128)(2,1)} %get-tuple-element.75.here_ref), channel_id=1, source_target_pairs={{0,4},{2,6},{4,0},{6,2},{8,12},{10,14},{12,8},{14,10},{16,20},{18,... | collective-permute-start | bytes 1769480 | tf_op jit(solution)/shard_map/ppermute | solution.py:943
  72.8 1.6 collective-permute-start.12
  78.4 53.3 %all-to-all-start = ((bf16[16,72,256]{2,1,0:T(8,128)(2,1)}), bf16[16,72,256]{2,1,0:T(8,128)(2,1)}, u32[]{:S(2)}, u32[]{:S(2)}) async-start(bf16[16,72,256]{2,1,0:T(8,128)(2,1)} %bitcast.17), calls=%async_computation | async-start | bytes 1179648 | tf_op jit(solution)/shard_map/all_to_all | solution.py:989
  83.5 8.9 %collective-permute-start.13 = (f32[8,1152]{1,0:T(8,128)}, f32[8,1152]{1,0:T(8,128)}, u32[]{:S(2)}, u32[]{:S(2)}) collective-permute-start(f32[8,1152]{1,0:T(8,128)} %get-tuple-element.82), channel_id=1, source_target_pairs={{2,0},{4,2},{6,4},{8,6},{10,8},{12,10},{14,12},{16,14},{18,16},{20... | collective-permute-start | bytes 110600 | tf_op jit(solution)/shard_map/ppermute | solution.py:934
  96.4 45.8 %collective-permute-start.16 = (f32[128,1152]{1,0:T(8,128)}, f32[128,1152]{1,0:T(8,128)}, u32[]{:S(2)}, u32[]{:S(2)}) collective-permute-start(f32[128,1152]{1,0:T(8,128)} %get-tuple-element.83), channel_id=1, source_target_pairs={{0,1},{1,0},{2,3},{3,2},{4,5},{5,4},{6,7},{7,6},{8,9},{9,8},{10,11... | collective-permute-start | bytes 1769480 | tf_op jit(solution)/shard_map/ppermute | solution.py:938
  96.4 15.4 %collective-permute-start.17 = (bf16[144,1152]{1,0:T(8,128)(2,1)}, bf16[144,1152]{1,0:T(8,128)(2,1)S(1)}, u32[]{:S(2)}, u32[]{:S(2)}) collective-permute-start(bf16[144,1152]{1,0:T(8,128)(2,1)} %get-tuple-element.85.here_ref), channel_id=1, source_target_pairs={{0,2},{2,0},{4,6},{6,4},{8,10},{10,8},{12,14},{14,12},{16,18},{18,... | collective-permute-start | bytes 995336 | tf_op jit(solution)/shard_map/ppermute | solution.py:943
  96.4 18.7 %collective-permute-start.18 = (bf16[144,1152]{1,0:T(8,128)(2,1)}, bf16[144,1152]{1,0:T(8,128)(2,1)S(1)}, u32[]{:S(2)}, u32[]{:S(2)}) collective-permute-start(bf16[144,1152]{1,0:T(8,128)(2,1)} %get-tuple-element.85.here_ref), channel_id=1, source_target_pairs={{0,4},{2,6},{4,0},{6,2},{8,12},{10,14},{12,8},{14,10},{16,20},{18,... | collective-permute-start | bytes 995336 | tf_op jit(solution)/shard_map/ppermute | solution.py:943
  107.3 14.3 %collective-permute-start.21 = (bf16[128,1152]{1,0:T(8,128)(2,1)S(1)}, bf16[128,1152]{1,0:T(8,128)(2,1)}, u32[]{:S(2)}, u32[]{:S(2)}) collective-permute-start(bf16[128,1152]{1,0:T(8,128)(2,1)S(1)} %slice.58), channel_id=1, source_target_pairs={{0,4},{2,6},{4,0},{6,2},{8,12},{10,14},{12,8},{14,10},{16,20},{18,... | collective-permute-start | bytes 884744 | tf_op jit(solution)/shard_map/ppermute | solution.py:943
  108.4 13.3 %collective-permute-start.22 = (bf16[128,1152]{1,0:T(8,128)(2,1)S(1)}, bf16[128,1152]{1,0:T(8,128)(2,1)}, u32[]{:S(2)}, u32[]{:S(2)}) collective-permute-start(bf16[128,1152]{1,0:T(8,128)(2,1)S(1)} %slice.59), channel_id=1, source_target_pairs={{0,2},{2,0},{4,6},{6,4},{8,10},{10,8},{12,14},{14,12},{16,18},{18,... | collective-permute-start | bytes 884744 | tf_op jit(solution)/shard_map/ppermute | solution.py:943
  111.8 0.7 copy-start
  111.8 70.1 %collective-permute-start.11 = (f32[128,1152]{1,0:T(8,128)}, f32[128,1152]{1,0:T(8,128)}, u32[]{:S(2)}, u32[]{:S(2)}) collective-permute-start(f32[128,1152]{1,0:T(8,128)} %fusion.9), channel_id=1, source_target_pairs={{0,1},{1,0},{2,3},{3,2},{4,5},{5,4},{6,7},{7,6},{8,9},{9,8},{10,11... | collective-permute-start | bytes 1769480 | tf_op jit(solution)/shard_map/ppermute | solution.py:938
  115.2 2.0 %copy-start.1 = (bf16[144,1152]{1,0:T(8,128)(2,1)}, bf16[144,1152]{1,0:T(8,128)(2,1)S(1)}, u32[]{:S(2)}) copy-start(bf16[144,1152]{1,0:T(8,128)(2,1)S(1)} %collective-permute-done.18.y_ref) | copy-start | bytes 995332
  115.2 11.1 %collective-permute-start.19 = (bf16[72,1152]{1,0:T(8,128)(2,1)}, bf16[72,1152]{1,0:T(8,128)(2,1)}, u32[]{:S(2)}, u32[]{:S(2)}) collective-permute-start(bf16[72,1152]{1,0:T(8,128)(2,1)} %slice.56), channel_id=1, source_target_pairs={{0,4},{2,6},{4,0},{6,2},{8,12},{10,14},{12,8},{14,10},{16,20},{18,... | collective-permute-start | bytes 497672 | tf_op jit(solution)/shard_map/ppermute | solution.py:943
  121.6 5.8 %collective-permute-start.20 = (bf16[72,1152]{1,0:T(8,128)(2,1)}, bf16[72,1152]{1,0:T(8,128)(2,1)}, u32[]{:S(2)}, u32[]{:S(2)}) collective-permute-start(bf16[72,1152]{1,0:T(8,128)(2,1)} %slice.57), channel_id=1, source_target_pairs={{0,2},{2,0},{4,6},{6,4},{8,10},{10,8},{12,14},{14,12},{16,18},{18,... | collective-permute-start | bytes 497672 | tf_op jit(solution)/shard_map/ppermute | solution.py:943
  126.3 58.6 %collective-permute-start.27 = (bf16[1,144,1152]{2,1,0:T(8,128)(2,1)}, bf16[1,144,1152]{2,1,0:T(8,128)(2,1)}, u32[]{:S(2)}, u32[]{:S(2)}) collective-permute-start(bf16[1,144,1152]{2,1,0:T(8,128)(2,1)} %get-tuple-element.93), channel_id=1, source_target_pairs={{0,8},{2,10},{4,12},{6,14},{8,0},{10,2},{12,4},{14,6},{16,24},{18,... | collective-permute-start | bytes 995336 | tf_op jit(solution)/shard_map/ppermute | solution.py:943
  130.7 15.1 %collective-permute-start.23 = (bf16[1,88,1152]{2,1,0:T(8,128)(2,1)}, bf16[1,88,1152]{2,1,0:T(8,128)(2,1)}, u32[]{:S(2)}, u32[]{:S(2)}) collective-permute-start(bf16[1,88,1152]{2,1,0:T(8,128)(2,1)} %get-tuple-element.88), channel_id=1, source_target_pairs={{0,8},{2,10},{4,12},{6,14},{8,0},{10,2},{12,4},{14,6},{16,24},{18,... | collective-permute-start | bytes 608264 | tf_op jit(solution)/shard_map/ppermute | solution.py:943
  131.7 15.2 %collective-permute-start.24 = (bf16[1,88,1152]{2,1,0:T(8,128)(2,1)}, bf16[1,88,1152]{2,1,0:T(8,128)(2,1)}, u32[]{:S(2)}, u32[]{:S(2)}) collective-permute-start(bf16[1,88,1152]{2,1,0:T(8,128)(2,1)} %get-tuple-element.89), channel_id=1, source_target_pairs={{0,16},{2,18},{4,20},{6,22},{8,24},{10,26},{12,28},{14,30},{16,0},... | collective-permute-start | bytes 608264 | tf_op jit(solution)/shard_map/ppermute | solution.py:943
  133.7 63.1 %all-to-all-start.1 = ((bf16[16,72,256]{2,1,0:T(8,128)(2,1)}), bf16[16,72,256]{2,1,0:T(8,128)(2,1)}, u32[]{:S(2)}, u32[]{:S(2)}) async-start(bf16[16,72,256]{2,1,0:T(8,128)(2,1)} %spread.1), calls=%async_computation.1 | async-start | bytes 1179648 | tf_op jit(solution)/shard_map/all_to_all | solution.py:1014
  142.2 37.7 %collective-permute-start.25 = (bf16[1,88,1152]{2,1,0:T(8,128)(2,1)}, bf16[1,88,1152]{2,1,0:T(8,128)(2,1)}, u32[]{:S(2)}, u32[]{:S(2)}) collective-permute-start(bf16[1,88,1152]{2,1,0:T(8,128)(2,1)} %get-tuple-element.90), channel_id=1, source_target_pairs={{0,24},{2,26},{4,28},{6,30},{8,16},{10,18},{12,20},{14,22},{16,8},... | collective-permute-start | bytes 608264 | tf_op jit(solution)/shard_map/ppermute | solution.py:943
  145.8 41.1 %collective-permute-start.28 = (bf16[1,144,1152]{2,1,0:T(8,128)(2,1)}, bf16[1,144,1152]{2,1,0:T(8,128)(2,1)}, u32[]{:S(2)}, u32[]{:S(2)}) collective-permute-start(bf16[1,144,1152]{2,1,0:T(8,128)(2,1)} %get-tuple-element.94), channel_id=1, source_target_pairs={{0,16},{2,18},{4,20},{6,22},{8,24},{10,26},{12,28},{14,30},{16,0},... | collective-permute-start | bytes 995336 | tf_op jit(solution)/shard_map/ppermute | solution.py:943
  146.8 46.3 %collective-permute-start.29 = (bf16[1,144,1152]{2,1,0:T(8,128)(2,1)}, bf16[1,144,1152]{2,1,0:T(8,128)(2,1)}, u32[]{:S(2)}, u32[]{:S(2)}) collective-permute-start(bf16[1,144,1152]{2,1,0:T(8,128)(2,1)} %get-tuple-element.95), channel_id=1, source_target_pairs={{0,24},{2,26},{4,28},{6,30},{8,16},{10,18},{12,20},{14,22},{16,8},... | collective-permute-start | bytes 995336 | tf_op jit(solution)/shard_map/ppermute | solution.py:943
  181.9 13.6 %collective-permute-start.26 = (f32[1,1152]{1,0:T(1,128)}, f32[1,1152]{1,0:T(1,128)}, u32[]{:S(2)}, u32[]{:S(2)}) collective-permute-start(f32[1,1152]{1,0:T(1,128)} %get-tuple-element.91), channel_id=1, source_target_pairs={{0,1},{1,0},{2,3},{3,2},{4,5},{5,4},{6,7},{7,6},{8,9},{9,8},{10,11... | collective-permute-start | bytes 13832 | tf_op jit(solution)/shard_map/ppermute | solution.py:938

commit v2 on v1

v2 whole, which is shorter than its diff:
```python
import functools

import jax
import jax.numpy as jnp
from jax import lax
from jax.experimental import pallas as pl
from jax.experimental.pallas import tpu as pltpu
from jax.sharding import PartitionSpec as P

NORM_EPS = 1e-05
LANES = 128
PLANE = 4
CHUNKS = 8
LOG2E = 1.4426950408889634
LN2 = 0.6931471805599453
FAR = 1e30
MIB = 1024 * 1024
TAP_BIAS, STEP_BIAS, SKIP, GAIN = 0, 1, 2, 3


def sigmoid(value):
    return 1.0 / (1.0 + jnp.exp(-value))


def silu_grad(value):
    sigma = sigmoid(value)
    return sigma * (1.0 + value * (1.0 - sigma))


def softplus(value):
    small = jnp.exp(-jnp.abs(value))
    series = small * (1.0 - small * (0.5 - small * (1.0 / 3.0 - small * 0.25)))
    return jnp.maximum(value, 0.0) + jnp.where(small < 0.01, series, jnp.log(1.0 + small))


def dot(first, second, contract):
    return lax.dot_general(
        first, second, (contract, ((), ())), preferred_element_type=jnp.float32
    )


def strided(number, length):
    return pl.ds(number, CHUNKS, stride=length // CHUNKS)


def spread(proj_ref, first, table_ref, states, length):
    for place in range(length // CHUNKS):
        rows = proj_ref[strided(place, length), :]
        for state in range(states):
            column = rows[:, first + state : first + state + 1]
            start = (place * states + state) * CHUNKS
            table_ref[start : start + CHUNKS, :] = jnp.broadcast_to(column, (CHUNKS, LANES))


def tile(ref, place, state, states):
    start = (place * states + state) * CHUNKS
    return ref[start : start + CHUNKS, :]


def padded(number, unit):
    return -(-number // unit) * unit


def row(ref, number):
    return ref[number : number + 1, :]


def inverse_rms(tokens):
    return lax.rsqrt(jnp.mean(tokens * tokens, axis=1, keepdims=True) + NORM_EPS)


def columns(masks_ref, tap):
    return jnp.broadcast_to(row(masks_ref, tap), (LANES, masks_ref.shape[1])).T


def two_rows(line):
    high = line.astype(jnp.bfloat16).astype(jnp.float32)
    number = lax.broadcasted_iota(jnp.int32, (2 * CHUNKS, line.shape[1]), 0)
    return jnp.where(number == 0, high, jnp.where(number == 1, line - high, 0.0)).astype(jnp.bfloat16)


def group_at(group):
    return pl.ds(pl.multiple_of(group * LANES, LANES), LANES)


def params():
    return pltpu.CompilerParams(vmem_limit_bytes=64 * MIB)


def cost(us):
    return pl.CostEstimate(flops=0, bytes_accessed=int(us * 3e6), transcendentals=0)


def shifted(block, rim, back):
    if back == 0:
        return block
    moved = pltpu.roll(block, back, 0)
    near = lax.broadcasted_iota(jnp.int32, (CHUNKS, block.shape[1]), 0)
    top = jnp.where(near < back, pltpu.roll(rim, back, 0), moved[:CHUNKS])
    return jnp.concatenate([top, moved[CHUNKS:]], axis=0)


def enter_kernel(
    kernel, scan_width,
    normed_ref, rim_tokens_ref, cot_ref, tap_bias_ref, step_bias_ref, skip_ref, gain_ref, masks_ref,
    conv_w_ref, gate_w_ref, out_w_ref, taps_ref, weight_ref,
    conv_ref, rim_ref, out_ref, gate_ref, gg_ref, proj_ref, stacked_ref,
    both_ref, mask_ref,
):
    length = normed_ref.shape[0]
    block = conv_w_ref.shape[1]

    @pl.when(pl.program_id(0) == 0)
    def _():
        for number, ref in enumerate((tap_bias_ref, step_bias_ref, skip_ref, gain_ref)):
            stacked_ref[number : number + 1, :] = ref[...].reshape(1, ref.shape[0])
        for tap in range(kernel):
            mask_ref[tap] = columns(masks_ref, tap)
        gain = row(stacked_ref, GAIN)
        rim = rim_tokens_ref[...].astype(jnp.float32)
        rim = (rim * inverse_rms(rim) * gain).astype(jnp.bfloat16)
        both_ref[:length, :] = normed_ref[...]
        both_ref[length:, :] = jnp.concatenate([rim, rim], axis=0)
        proj_ref[...] = jnp.zeros_like(proj_ref)

    normed = both_ref[...]
    conv_in = dot(normed, conv_w_ref[...], ((1,), (0,))).astype(jnp.bfloat16)
    conv_ref[...] = conv_in[:length]
    wide = conv_in[:length].astype(jnp.float32)
    rim = conv_in[length : length + CHUNKS].astype(jnp.float32)
    rim_ref[...] = rim
    at = pl.ds(pl.multiple_of(pl.program_id(0) * block, LANES), block)
    total = jnp.broadcast_to(stacked_ref[TAP_BIAS : TAP_BIAS + 1, at], (length, block))
    for tap in range(kernel):
        mask = jnp.concatenate([mask_ref[tap]] * (block // LANES), axis=1)
        total = total + row(taps_ref, tap) * shifted(wide, rim, kernel - 1 - tap) * mask
    out = (total * sigmoid(total)).astype(jnp.bfloat16)
    out_ref[...] = out
    proj_ref[:, :scan_width] += dot(out, weight_ref[...], ((1,), (1,)))
    gate_ref[...] = dot(normed[:length], gate_w_ref[...], ((1,), (0,)))
    gg_ref[...] = dot(cot_ref[...], out_w_ref[...], ((1,), (1,)))


def run_enter(normed, rim, cot, vectors, masks, conv_w, gate_w, out_w, taps, weight):
    length, model = normed.shape
    width = conv_w.shape[1]
    block = 3 * LANES
    f32, bf16 = jnp.float32, jnp.bfloat16
    flat = pl.BlockSpec(memory_space=pltpu.VMEM)
    return pl.pallas_call(
        functools.partial(enter_kernel, taps.shape[0], weight.shape[0]),
        grid=(width // block,),
        in_specs=[whole(length, model), whole(CHUNKS, model), whole(length, model)] + [flat] * 4 + [
            whole(*masks.shape), column_block(model, block), column_block(model, block),
            pl.BlockSpec((block, model), lambda g: (g, 0)), column_block(taps.shape[0], block),
            column_block(weight.shape[0], block),
        ],
        out_specs=[
            column_block(length, block), column_block(CHUNKS, block), column_block(length, block),
            column_block(length, block), column_block(length, block), whole(length, LANES),
            whole(len(vectors), width),
        ],
        out_shape=[
            jax.ShapeDtypeStruct((length, width), bf16), jax.ShapeDtypeStruct((CHUNKS, width), f32),
            jax.ShapeDtypeStruct((length, width), bf16), jax.ShapeDtypeStruct((length, width), f32),
            jax.ShapeDtypeStruct((length, width), f32), jax.ShapeDtypeStruct((length, LANES), f32),
            jax.ShapeDtypeStruct((len(vectors), width), f32),
        ],
        scratch_shapes=[
            pltpu.VMEM((length + 2 * CHUNKS, model), bf16),
            pltpu.VMEM((taps.shape[0], length, LANES), f32),
        ],
        compiler_params=params(), cost_estimate=cost(6), name="enter",
    )(normed, rim, cot, *vectors, masks, conv_w, gate_w, out_w, taps, weight)


def early_kernel(members, where_ref, tokens_ref, cot_ref, gain_ref, normed_ref, *rest):
    rim_ref, *early_refs, turned_ref = rest
    length, model = tokens_ref.shape
    rim_ref[...] = tokens_ref[length - CHUNKS :, :]
    tokens = tokens_ref[...].astype(jnp.float32)
    gain = gain_ref[...].reshape(1, model)
    normed_ref[...] = (tokens * inverse_rms(tokens) * gain).astype(jnp.bfloat16)
    for group in range(model // LANES):
        at = slice(group * LANES, (group + 1) * LANES)
        turned_ref[at, :] = normed_ref[:, at].astype(jnp.float32).T
        turned_ref[model + group * LANES : model + (group + 1) * LANES, :] = (
            cot_ref[:, at].astype(jnp.float32).T
        )
    rows, lines = model // members, members // PLANE
    for mask, early_ref in enumerate(early_refs):
        place = jnp.bitwise_xor(where_ref[0] % PLANE, mask)
        for source in range(2):
            pieces = []
            for line in range(lines):
                first = source * model + (line * PLANE + place) * rows
                if rows % 8 == 0:
                    first = pl.multiple_of(first, 8)
                pieces.append(turned_ref[pl.ds(first, rows), :])
            at = slice(source * lines * rows, (source + 1) * lines * rows)
            early_ref[at, :] = jnp.concatenate(pieces, axis=0).astype(jnp.bfloat16)


def run_early(where, tokens, cot, gain):
    length, model = tokens.shape
    members = lax.axis_size("seq")
    vmem = pl.BlockSpec(memory_space=pltpu.VMEM)
    early = jax.ShapeDtypeStruct((2 * model // PLANE, length), jnp.bfloat16)
    return pl.pallas_call(
        functools.partial(early_kernel, members),
        in_specs=[pl.BlockSpec(memory_space=pltpu.SMEM), vmem, vmem, vmem],
        out_specs=[vmem] * (2 + PLANE),
        out_shape=[
            jax.ShapeDtypeStruct(tokens.shape, jnp.bfloat16),
            jax.ShapeDtypeStruct((CHUNKS, model), jnp.bfloat16),
        ] + [early] * PLANE,
        scratch_shapes=[pltpu.VMEM((2 * model, length), jnp.float32)],
        compiler_params=params(), cost_estimate=cost(3), name="early",
    )(where, tokens, cot, gain)


def every(width):
    return [(group, slice(group * LANES, (group + 1) * LANES)) for group in range(width // LANES)]


def chunk_sums(long_ref, group, length):
    sums = long_ref[group, strided(0, length), :]
    for place in range(1, length // CHUNKS):
        sums = sums + long_ref[group, strided(place, length), :]
    return sums


def prepare(
    rank, states, own_ref, peer_ref, weight_ref, bias_ref, conv_ref, gg_ref, gate_ref, masks_ref,
    proj_ref, in_ref, out_ref, long_ref, drive_ref, source_ref, true_ref=None,
):
    length, width = conv_ref.shape
    proj_ref[...] = own_ref[...] + peer_ref[...]
    low = proj_ref[:, :rank].astype(jnp.bfloat16)
    step_pre = dot(low, weight_ref[...], ((1,), (0,))) + row(bias_ref, STEP_BIAS)
    spread(proj_ref, rank, in_ref, states, length)
    spread(proj_ref, rank + states, out_ref, states, length)
    same = columns(masks_ref, masks_ref.shape[0] - 2)
    for group, at in every(width):
        step = softplus(step_pre[:, at])
        if true_ref is not None:
            true_ref[group] = step
        long_ref[group] = jnp.where(same > 0.0, step, FAR)
        drive_ref[group] = step * conv_ref[:, at].astype(jnp.float32)
        gate = gate_ref[:, at]
        source_ref[group] = gg_ref[:, at] * gate * sigmoid(gate)
    return step_pre


def ends_kernel(
    rank, states, ndeps,
    own_ref, peer_ref, weight_ref, bias_ref, decay_ref, conv_ref, gg_ref, gate_ref, masks_ref, *rest,
):
    (
        ends_ref, seeds_ref, totals_ref,
        proj_ref, in_ref, out_ref, long_ref, drive_ref, source_ref, end_ref, seed_ref, dec_ref,
    ) = rest[ndeps:]
    length, width = conv_ref.shape
    places = length // CHUNKS
    prepare(
        rank, states, own_ref, peer_ref, weight_ref, bias_ref, conv_ref, gg_ref, gate_ref, masks_ref,
        proj_ref, in_ref, out_ref, long_ref, drive_ref, source_ref,
    )

    @pl.loop(0, width // LANES)
    def _(group):
        rate2 = -jnp.exp(decay_ref[:, group_at(group)]) * LOG2E
        rates = [jnp.broadcast_to(rate2[n : n + 1, :], (CHUNKS, LANES)) for n in range(states)]
        hidden = [None] * states
        for place in range(places):
            long = long_ref[group, strided(place, length), :]
            drive = drive_ref[group, strided(place, length), :]
            for n in range(states):
                term = tile(in_ref, place, n, states) * drive
                decay = jnp.exp2(long * rates[n])
                dec_ref[(place * states + n) * CHUNKS : (place * states + n + 1) * CHUNKS, :] = decay
                hidden[n] = term if place == 0 else decay * hidden[n] + term
        for n in range(states):
            end_ref[group, n * CHUNKS : (n + 1) * CHUNKS, :] = hidden[n]
        back = [None] * states
        for place in reversed(range(places)):
            long = long_ref[group, strided(place, length), :]
            source = source_ref[group, strided(place, length), :]
            for n in range(states):
                term = tile(out_ref, place, n, states) * source
                term = term if place == places - 1 else back[n] + term
                back[n] = tile(dec_ref, place, n, states) * term
        for n in range(states):
            seed_ref[group, n * CHUNKS : (n + 1) * CHUNKS, :] = back[n]

    for group, at in every(width):
        ends_ref[:, at] = end_ref[group]
        seeds_ref[:, at] = seed_ref[group]
        rate2 = -jnp.exp(decay_ref[:, at]) * LOG2E
        sums = chunk_sums(long_ref, group, length)
        decays = [jnp.exp2(rate2 * sums[c : c + 1, :]) for c in range(CHUNKS)]
        end = jnp.zeros((states, LANES), jnp.float32)
        seed = jnp.zeros((states, LANES), jnp.float32)
        for c in range(CHUNKS):
            end = decays[c] * end + end_ref[group, pl.ds(c, states, stride=CHUNKS), :]
        for c in reversed(range(CHUNKS)):
            seed = decays[c] * seed + seed_ref[group, pl.ds(c, states, stride=CHUNKS), :]
        totals_ref[:states, at] = end.astype(jnp.bfloat16)
        totals_ref[states : 2 * states, at] = seed.astype(jnp.bfloat16)
        totals_ref[2 * states :, at] = two_rows(jnp.sum(sums, axis=0, keepdims=True))


def scan_kernel(
    rank, states, members,
    where_ref, own_ref, peer_ref, weight_ref, bias_ref, decay_ref, conv_ref, gg_ref, gate_ref, masks_ref,
    ends_ref, seeds_ref, near_ref, *rest,
):
    stride, radix = levels(members)[-1]
    far_refs = rest[: radix - 1]
    gated_ref, ggate_ref, small_ref, gconv_ref, gproj_ref = rest[-22:-17]
    (
        proj_ref, in_ref, out_ref, long_ref, true_ref, drive_ref, source_ref,
        start_ref, last_ref, hidden_ref, in_acc, out_acc, scan_ref, gstep_ref, mix_ref, log_ref, dec_ref,
    ) = rest[-17:]
    length, width = conv_ref.shape
    places = length // CHUNKS
    step_pre = prepare(
        rank, states, own_ref, peer_ref, weight_ref, bias_ref, conv_ref, gg_ref, gate_ref, masks_ref,
        proj_ref, in_ref, out_ref, long_ref, drive_ref, source_ref, true_ref,
    )
    in_acc[...] = jnp.zeros_like(in_acc)
    out_acc[...] = jnp.zeros_like(out_acc)
    digit = where_ref[0] // stride % radix
    for group, at in every(width):
        start_ref[group] = ends_ref[:, at]
        last_ref[group] = seeds_ref[:, at]
        rate2 = -jnp.exp(decay_ref[:, at]) * LOG2E
        sums = chunk_sums(long_ref, group, length)
        decays = [jnp.exp2(rate2 * sums[c : c + 1, :]) for c in range(CHUNKS)]
        forward, backward = arrive(
            digit, rate2, near_ref[:, at], [ref[:, at] for ref in far_refs], states
        )
        for c in range(CHUNKS):
            rows = pl.ds(c, states, stride=CHUNKS)
            own = start_ref[group, rows, :]
            start_ref[group, rows, :] = forward
            forward = decays[c] * forward + own
        for c in reversed(range(CHUNKS)):
            rows = pl.ds(c, states, stride=CHUNKS)
            own = last_ref[group, rows, :]
            last_ref[group, rows, :] = backward
            backward = decays[c] * backward + own

    @pl.loop(0, width // LANES)
    def _(group):
        rate2 = -jnp.exp(decay_ref[:, group_at(group)]) * LOG2E
        rates = [jnp.broadcast_to(rate2[n : n + 1, :], (CHUNKS, LANES)) for n in range(states)]
        hidden = [start_ref[group, n * CHUNKS : (n + 1) * CHUNKS, :] for n in range(states)]
        for place in range(places):
            long = long_ref[group, strided(place, length), :]
            drive = drive_ref[group, strided(place, length), :]
            source = source_ref[group, strided(place, length), :]
            rows = slice(place * CHUNKS, (place + 1) * CHUNKS)
            scan = None
            for n in range(states):
                lanes = slice(n * LANES, (n + 1) * LANES)
                decay = jnp.exp2(long * rates[n])
                dec_ref[(place * states + n) * CHUNKS : (place * states + n + 1) * CHUNKS, :] = decay
                value = decay * hidden[n] + tile(in_ref, place, n, states) * drive
                hidden[n] = value
                if place < places - 1:
                    first = (place * states + n) * CHUNKS
                    hidden_ref[first : first + CHUNKS, :] = value
                part = tile(out_ref, place, n, states) * value
                scan = part if n == 0 else scan + part
                out_acc[rows, lanes] += source * value
            scan_ref[group, strided(place, length), :] = scan

        back = [last_ref[group, n * CHUNKS : (n + 1) * CHUNKS, :] for n in range(states)]
        logs = [None] * states
        for place in reversed(range(places)):
            long = long_ref[group, strided(place, length), :]
            true = true_ref[group, strided(place, length), :]
            drive = drive_ref[group, strided(place, length), :]
            source = source_ref[group, strided(place, length), :]
            rows = slice(place * CHUNKS, (place + 1) * CHUNKS)
            gstep = None
            mixed = None
            for n in range(states):
                lanes = slice(n * LANES, (n + 1) * LANES)
                grad = back[n] + tile(out_ref, place, n, states) * source
                previous = (
                    start_ref[group, n * CHUNKS : (n + 1) * CHUNKS, :] if place == 0
                    else tile(hidden_ref, place - 1, n, states)
                )
                back[n] = tile(dec_ref, place, n, states) * grad
                log = back[n] * previous
                part = log * true
                logs[n] = part if logs[n] is None else logs[n] + part
                part = log * rates[n]
                gstep = part if n == 0 else gstep + part
                part = grad * tile(in_ref, place, n, states)
                mixed = part if n == 0 else mixed + part
                in_acc[rows, lanes] += grad * drive
            gstep_ref[group, strided(place, length), :] = gstep
            mix_ref[group, strided(place, length), :] = mixed
        for n in range(states):
            log_ref[group, n * CHUNKS : (n + 1) * CHUNKS, :] = logs[n]

    low = proj_ref[...].astype(jnp.bfloat16)
    small_ref[rank + states + 2 :, :] = jnp.zeros((small_ref.shape[0] - rank - states - 2, width), jnp.float32)
    grad_low = jnp.zeros((length, rank), jnp.float32)
    for group, at in every(width):
        conv = conv_ref[:, at].astype(jnp.float32)
        gate, gg = gate_ref[:, at], gg_ref[:, at]
        source, step, mix = source_ref[group], true_ref[group], mix_ref[group]
        sigma = sigmoid(gate)
        skip = bias_ref[SKIP : SKIP + 1, at]
        scan_out = scan_ref[group] + skip * conv
        gated_ref[:, at] = (scan_out * gate * sigma).astype(jnp.bfloat16)
        ggate = gg * scan_out * sigma * (1.0 + gate * (1.0 - sigma))
        ggate_ref[:, at] = ggate.astype(jnp.bfloat16)
        gconv_ref[:, at] = source * skip + mix * step
        gpre = (gstep_ref[group] * LN2 + mix * conv) * sigmoid(step_pre[:, at])
        gpre_low = gpre.astype(jnp.bfloat16)
        grad_low = grad_low + dot(gpre_low, weight_ref[:, at], ((1,), (1,)))
        small_ref[:rank, at] = dot(low, gpre_low, ((0,), (0,)))[:rank]
        decay = -jnp.exp(decay_ref[:, at])
        logs = log_ref[group, pl.ds(0, states, stride=CHUNKS), :]
        for c in range(1, CHUNKS):
            logs = logs + log_ref[group, pl.ds(c, states, stride=CHUNKS), :]
        first = rank + states
        small_ref[rank:first, at] = logs * decay
        small_ref[first : first + 1, at] = jnp.sum(gpre, axis=0, keepdims=True)
        small_ref[first + 1 : first + 2, at] = jnp.sum(source * conv, axis=0, keepdims=True)

    wide = states * LANES
    source_state = lax.broadcasted_iota(jnp.int32, (wide, LANES), 0) // LANES
    column = lax.broadcasted_iota(jnp.int32, (wide, LANES), 1)
    total = jnp.zeros((length, LANES), jnp.float32)
    for acc, first in ((in_acc, rank), (out_acc, rank + states)):
        pick = jnp.where(source_state + first == column, 1.0, 0.0).astype(jnp.bfloat16)
        value = acc[...]
        high = value.astype(jnp.bfloat16)
        rest = (value - high.astype(jnp.float32)).astype(jnp.bfloat16)
        total = total + dot(high, pick, ((1,), (0,))) + dot(rest, pick, ((1,), (0,)))
    scan_ref[0] = total
    for place in range(places):
        mix_ref[0, strided(place, length), :] = scan_ref[0, place * CHUNKS : (place + 1) * CHUNKS, :]
    gproj_ref[...] = mix_ref[0]
    gproj_ref[:, :rank] += grad_low


def column_block(rows, width=LANES):
    return pl.BlockSpec((rows, width), lambda g: (0, g))


def whole(*shape):
    return pl.BlockSpec(shape, lambda g: (0,) * len(shape))


def run_ends(own, peer, weight, stacked, decay_log, conv, gg, gate, masks, deps=()):
    length, width = conv.shape
    rank, states = weight.shape[0], decay_log.shape[0]
    tall = length // CHUNKS * states * CHUNKS
    f32 = jnp.float32
    vmem = pl.BlockSpec(memory_space=pltpu.VMEM)
    return pl.pallas_call(
        functools.partial(ends_kernel, rank, states, len(deps)),
        in_specs=[vmem] * 9 + [pl.BlockSpec(memory_space=pl.ANY) for _ in deps], out_specs=[vmem] * 3,
        out_shape=[
            jax.ShapeDtypeStruct((states * CHUNKS, width), f32),
            jax.ShapeDtypeStruct((states * CHUNKS, width), f32),
            jax.ShapeDtypeStruct((2 * states + 2 * CHUNKS, width), jnp.bfloat16),
        ],
        scratch_shapes=[pltpu.VMEM((length, LANES), f32)]
        + [pltpu.VMEM((tall, LANES), f32)] * 2 + [pltpu.VMEM((width // LANES, length, LANES), f32)] * 3
        + [pltpu.VMEM((width // LANES, states * CHUNKS, LANES), f32)] * 2
        + [pltpu.VMEM((tall, LANES), f32)],
        compiler_params=params(), cost_estimate=cost(8), name="ends",
    )(own, peer, weight, stacked, decay_log, conv, gg, gate, masks, *deps)


def run_scan(where, own, peer, weight, stacked, decay_log, conv, gg, gate, masks, ends, seeds, near, far, deps):
    length, width = conv.shape
    members = lax.axis_size("seq")
    rank, states = weight.shape[0], decay_log.shape[0]
    places = length // CHUNKS
    tall = places * states * CHUNKS
    f32, bf16 = jnp.float32, jnp.bfloat16
    groups = pltpu.VMEM((width // LANES, length, LANES), f32)
    chunks = pltpu.VMEM((width // LANES, states * CHUNKS, LANES), f32)
    table = pltpu.VMEM((tall, LANES), f32)
    vmem = pl.BlockSpec(memory_space=pltpu.VMEM)
    return pl.pallas_call(
        functools.partial(scan_kernel, rank, states, members),
        in_specs=[pl.BlockSpec(memory_space=pltpu.SMEM)] + [vmem] * (12 + len(far))
        + [pl.BlockSpec(memory_space=pl.ANY) for _ in deps],
        out_specs=[vmem] * 5,
        out_shape=[
            jax.ShapeDtypeStruct((length, width), bf16), jax.ShapeDtypeStruct((length, width), bf16),
            jax.ShapeDtypeStruct((padded(rank + states + 2, 8), width), f32),
            jax.ShapeDtypeStruct((length, width), f32),
            jax.ShapeDtypeStruct((length, LANES), f32),
        ],
        scratch_shapes=[pltpu.VMEM((length, LANES), f32), table, table] + [groups] * 4 + [chunks] * 2
        + [table] + [pltpu.VMEM((length, states * LANES), f32)] * 2 + [groups] * 3 + [chunks, table],
        compiler_params=params(), cost_estimate=cost(15), name="scan",
    )(where, own, peer, weight, stacked, decay_log, conv, gg, gate, masks, ends, seeds, near, *far, *deps)


def levels(members):
    found, stride = [], 1
    while stride < members:
        radix = 4 if members // stride % 4 == 0 else 2
        found.append((stride, radix))
        stride *= radix
    return found


def chosen(refs, own, hop):
    value = own
    for mask, ref in enumerate(refs, 1):
        value = jnp.where(hop == mask, ref.astype(jnp.float32), value)
    return value


def arrive(digit, rate2, near, far, states):
    radix = len(far) + 1
    carry = jnp.zeros_like(rate2)
    incoming = jnp.zeros_like(rate2)
    blank = jnp.zeros(far[0].shape, jnp.float32)
    for number in range(radix):
        value = chosen(far, blank, digit ^ number)
        decay = jnp.exp2(rate2 * (value[states : states + 1] + value[states + 1 : states + 2]))
        carry = jnp.where(number < digit, decay * carry + value[:states], carry)
    for number in reversed(range(radix)):
        value = chosen(far, blank, digit ^ number)
        decay = jnp.exp2(rate2 * (value[states : states + 1] + value[states + 1 : states + 2]))
        incoming = jnp.where(number > digit, decay * incoming + value[:states], incoming)
    before, behind = near[2 * states : 2 * states + 1], near[2 * states + 1 : 2 * states + 2]
    carry = near[:states] + jnp.exp2(rate2 * before) * carry
    incoming = near[states : 2 * states] + jnp.exp2(rate2 * behind) * incoming
    return carry, incoming


def fold_kernel(states, level, members, start, where_ref, decay_ref, *refs):
    stride, radix = levels(members)[level]
    next_stride, next_radix = levels(members)[level + 1]
    last = level + 2 == len(levels(members))
    digit = where_ref[0] // stride % radix
    if not start:
        old = refs[0][...]
        refs = refs[1:]
    own = refs[0][...]
    got = [ref[...] for ref in refs[1:radix]]
    near_ref, outs = refs[radix], refs[radix + 1 :]
    rate2 = -jnp.exp(decay_ref[...]) * LOG2E
    own = own.astype(jnp.float32)
    values = [chosen(got, own, digit ^ number) for number in range(radix)]
    first = 2 * states
    sums = [value[first : first + 1] + value[first + 1 : first + 2] for value in values]
    decays = [jnp.exp2(rate2 * one) for one in sums]
    zero, line = jnp.zeros_like(rate2), jnp.zeros_like(sums[0])
    end, seed, carry, incoming, before, behind, total = zero, zero, zero, zero, line, line, line
    for number in range(radix):
        part = values[number][:states]
        end = decays[number] * end + part
        carry = jnp.where(number < digit, decays[number] * carry + part, carry)
        before = jnp.where(number < digit, before + sums[number], before)
        total = total + sums[number]
    for number in reversed(range(radix)):
        part = values[number][states : 2 * states]
        seed = decays[number] * seed + part
        incoming = jnp.where(number > digit, decays[number] * incoming + part, incoming)
        behind = jnp.where(number > digit, behind + sums[number], behind)
    if not start:
        old_before, old_behind = old[2 * states : 2 * states + 1], old[2 * states + 1 : 2 * states + 2]
        carry = old[:states] + jnp.exp2(rate2 * old_before) * carry
        incoming = old[states : 2 * states] + jnp.exp2(rate2 * old_behind) * incoming
        before, behind = before + old_before, behind + old_behind
    pad = jnp.zeros((6, line.shape[1]), jnp.float32)
    near_ref[...] = jnp.concatenate([carry, incoming, before, behind, pad], axis=0)
    tail = two_rows(total)
    if last:
        next_digit = where_ref[0] // next_stride % next_radix
        for mask, out in enumerate(outs, 1):
            value = jnp.where(next_digit < (next_digit ^ mask), end, seed)
            out[:states, :] = value.astype(jnp.bfloat16)
            out[states:, :] = tail
    else:
        outs[0][: 2 * states, :] = jnp.concatenate([end, seed], axis=0).astype(jnp.bfloat16)
        outs[0][2 * states :, :] = tail


def run_fold(level, where, decay_log, near, parts):
    states, width = decay_log.shape
    members = lax.axis_size("seq")
    f32, bf16 = jnp.float32, jnp.bfloat16
    vmem = pl.BlockSpec(memory_space=pltpu.VMEM)
    tall = jax.ShapeDtypeStruct((2 * states + 8, width), f32)
    if level + 2 == len(levels(members)):
        sent = [jax.ShapeDtypeStruct((states + 2 * CHUNKS, width), bf16)] * (levels(members)[-1][1] - 1)
    else:
        sent = [jax.ShapeDtypeStruct((2 * states + 2 * CHUNKS, width), bf16)]
    extra = [] if near is None else [near]
    return pl.pallas_call(
        functools.partial(fold_kernel, states, level, members, near is None),
        in_specs=[pl.BlockSpec(memory_space=pltpu.SMEM)] + [vmem] * (1 + len(extra) + len(parts)),
        out_specs=[vmem] * (1 + len(sent)),
        out_shape=[tall] + sent,
        compiler_params=params(), cost_estimate=cost(2), name="fold",
    )(where, decay_log, *extra, *parts)


def exchange(where, totals, decay_log):
    members = lax.axis_size("seq")
    found = levels(members)
    near = None
    for level, (stride, radix) in enumerate(found[:-1]):
        parts = [totals] + [hop(totals, mask * stride) for mask in range(1, radix)]
        near, *sent = run_fold(level, where, decay_log, near, parts)
        totals = sent[0]
    stride, radix = found[-1]
    return near, [hop(one, mask * stride) for mask, one in enumerate(sent, 1)]


def taps_kernel(
    kernel, ndeps,
    own_ref, peer_ref, conv_ref, in_ref, ext_ref, weight_ref, gconv_ref, taps_ref, params_ref, masks_ref,
    *rest,
):
    main_ref, rim_ref, small_ref = rest[ndeps:]
    length, total_width = conv_ref.shape
    width = weight_ref.shape[0]
    grad_proj = (own_ref[...] + peer_ref[...]).astype(jnp.bfloat16)
    masks = [columns(masks_ref, tap) for tap in range(kernel)]
    near_row = lax.broadcasted_iota(jnp.int32, (CHUNKS, LANES), 0)
    token = lax.broadcasted_iota(jnp.int32, (length, LANES), 0)
    for group in range(total_width // LANES):
        at = slice(group * LANES, (group + 1) * LANES)
        taps = [taps_ref[tap : tap + 1, at] for tap in range(kernel)]
        conv_in = in_ref[:, at].astype(jnp.float32)
        ext = ext_ref[:, at]
        seen = [shifted(conv_in, ext, kernel - 1 - tap) * masks[tap] for tap in range(kernel)]
        pre = jnp.broadcast_to(params_ref[TAP_BIAS : TAP_BIAS + 1, at], (length, LANES))
        for tap in range(kernel):
            pre = pre + taps[tap] * seen[tap]
        small_ref[:width, at] = dot(grad_proj, conv_ref[:, at], ((0,), (0,)))[:width]
        grad = gconv_ref[:, at] + dot(grad_proj[:, :width], weight_ref[:, at], ((1,), (0,)))
        grad = grad * silu_grad(pre)
        lines = []
        main = jnp.zeros((length, LANES), jnp.float32)
        rim = jnp.zeros((CHUNKS, LANES), jnp.float32)
        for tap in range(kernel):
            back = kernel - 1 - tap
            lines.append(jnp.sum(grad * seen[tap], axis=0, keepdims=True))
            masked = grad * masks[tap] * taps[tap]
            if back == 0:
                main = main + masked
            else:
                moved = pltpu.roll(masked, length - back, 0)
                main = main + jnp.where(token < length - back, moved, 0.0)
                rim = rim + jnp.where(
                    near_row >= CHUNKS - back, pltpu.roll(masked[:CHUNKS], CHUNKS - back, 0), 0.0
                )
        main_ref[:, at] = main
        rim_ref[:, at] = rim
        lines.append(jnp.sum(grad, axis=0, keepdims=True))
        lines.append(jnp.zeros((small_ref.shape[0] - width - kernel - 1, LANES), jnp.float32))
        small_ref[width:, at] = jnp.concatenate(lines, axis=0)


def run_taps(own, peer, conv, conv_in, ext, weight, gconv, taps, stacked, masks, deps):
    length, width = conv.shape
    kernel = taps.shape[0]
    f32 = jnp.float32
    vmem = pl.BlockSpec(memory_space=pltpu.VMEM)
    return pl.pallas_call(
        functools.partial(taps_kernel, kernel, len(deps)),
        in_specs=[vmem] * 10 + [pl.BlockSpec(memory_space=pl.ANY) for _ in deps],
        out_specs=[vmem] * 3,
        out_shape=[
            jax.ShapeDtypeStruct((length, width), f32),
            jax.ShapeDtypeStruct((CHUNKS, width), f32),
            jax.ShapeDtypeStruct((padded(weight.shape[0] + kernel + 2, 8), width), f32),
        ],
        compiler_params=params(), cost_estimate=cost(4), name="taps",
    )(own, peer, conv, conv_in, ext, weight, gconv, taps, stacked, masks, *deps)


def inputs_kernel(
    gain_row, ndeps, where_ref, main_ref, rim_ref, weight_ref, gate_part_ref, tokens_ref,
    first_small_ref, second_small_ref, *rest,
):
    x_first_ref, x_second_ref, y_first_ref, y_second_ref, own_ref, normed_ref, small_ref = rest[ndeps:]
    bf16 = jnp.bfloat16
    length, width = main_ref.shape
    half = length // 2
    main = main_ref[...]
    low = jnp.concatenate(
        [main[: length - CHUNKS], main[length - CHUNKS :] + rim_ref[...]], axis=0
    ).astype(bf16)
    normed = dot(low, weight_ref[...], ((1,), (1,))) + gate_part_ref[...]
    normed_ref[...] = normed
    tokens = tokens_ref[...].astype(jnp.float32)
    gain = jnp.sum(normed * tokens * inverse_rms(tokens), axis=0, keepdims=True)
    second = second_small_ref[...]
    number = lax.broadcasted_iota(jnp.int32, second.shape, 0)
    second = jnp.where(number == gain_row, gain, second)
    small = jnp.concatenate([first_small_ref[...], second], axis=0)
    count = small_ref.shape[1]
    blank = jnp.zeros((PLANE * count - small.shape[0], width), jnp.float32)
    small = jnp.concatenate([small, blank], axis=0)
    for quarter in range(PLANE):
        small_ref[quarter] = small[quarter * count : (quarter + 1) * count]
    place = where_ref[0] % PLANE
    own_ref[...] = small_ref[place]
    across = small_ref[jnp.bitwise_xor(place, 3)].astype(bf16)
    x_first_ref[...] = jnp.concatenate([low[:half], across], axis=0)
    x_second_ref[...] = jnp.concatenate([low[half:], small_ref[jnp.bitwise_xor(place, 1)].astype(bf16)], axis=0)
    y_first_ref[...] = jnp.concatenate([low[:half], small_ref[jnp.bitwise_xor(place, 2)].astype(bf16)], axis=0)
    y_second_ref[...] = low[half:]


def run_inputs(gain_row, where, main, rim, weight, gate_part, tokens, first_small, second_small, deps):
    length, width = main.shape
    f32, bf16 = jnp.float32, jnp.bfloat16
    vmem = pl.BlockSpec(memory_space=pltpu.VMEM)
    count = padded(first_small.shape[0] + second_small.shape[0], 8 * PLANE) // PLANE
    tall = jax.ShapeDtypeStruct((length // 2 + count, width), bf16)
    return pl.pallas_call(
        functools.partial(inputs_kernel, gain_row, len(deps)),
        in_specs=[pl.BlockSpec(memory_space=pltpu.SMEM)] + [vmem] * 7
        + [pl.BlockSpec(memory_space=pl.ANY) for _ in deps],
        out_specs=[vmem] * 6,
        out_shape=[
            tall, tall, tall, jax.ShapeDtypeStruct((length // 2, width), bf16),
            jax.ShapeDtypeStruct((count, width), f32),
            jax.ShapeDtypeStruct((length, weight.shape[0]), f32),
        ],
        scratch_shapes=[pltpu.VMEM((PLANE, count, width), f32)],
        compiler_params=params(), cost_estimate=cost(3), name="inputs",
    )(where, main, rim, weight, gate_part, tokens, first_small, second_small, *deps)


def products_kernel(halves, members, ndeps, where_ref, *rest):
    early = rest[:PLANE]
    late = rest[PLANE : 3 * PLANE]
    small = len(halves) == 1
    if small:
        own_ref = rest[3 * PLANE]
        rest = rest[1:]
    kept_ref, *small_refs, sent_ref, total_ref = rest[3 * PLANE + ndeps :]
    lines = members // PLANE
    share, length = early[0].shape[0] // 2, early[0].shape[1]
    rows = share // lines
    for number, half in enumerate(halves):
        total = None
        for mask in range(PLANE):
            if small:
                tops = [late[2 * mask + part][: length // 2, :] for part in range(2)]
                block = jnp.concatenate(tops, axis=0)
            else:
                block = late[2 * mask + number][...]
            part = dot(early[mask][half * share : (half + 1) * share, :], block, ((1,), (0,)))
            total = part if total is None else total + part
        for line in range(lines):
            total_ref[line, number * rows : (number + 1) * rows, :] = total[line * rows : (line + 1) * rows]
    line = None
    if small:
        line = own_ref[...]
        for ref in (late[3], late[4], late[6]):
            line = line + ref[length // 2 :, :].astype(jnp.float32)
    send(where_ref[0], 0, total_ref, line, kept_ref, small_refs, sent_ref)


def send(device, level, total_ref, line, kept_ref, small_refs, sent_ref):
    digit = device // (PLANE << level) % 2
    pieces = []
    if line is not None:
        small_refs[0][...] = line
        pieces.append(line)
    for block in range(total_ref.shape[0] // 2):
        kept_ref[block] = total_ref[2 * block + digit]
        pieces.append(total_ref[2 * block + 1 - digit])
    sent_ref[...] = jnp.concatenate(pieces, axis=0).astype(jnp.bfloat16)


def gather_kernel(level, count, small, ndeps, where_ref, kept_ref, *refs):
    total = kept_ref[...]
    line = None
    first = 0
    if small:
        first = refs[0].shape[0]
        line = refs[0][...] + refs[1][:first, :].astype(jnp.float32)
        refs = refs[1:]
    got = refs[0][first:, :].astype(jnp.float32)
    refs = refs[1 + ndeps :]
    left, rows, width = total.shape
    pieces = [total[index] + got[index * rows : (index + 1) * rows] for index in range(left)]
    if left > 1:
        total_ref = refs[-1]
        for index, piece in enumerate(pieces):
            total_ref[index] = piece
        send(where_ref[0], level + 1, total_ref, line, refs[0], refs[1:-2], refs[-2])
        return
    for index in range(count):
        refs[index][...] = pieces[0][index * (rows // count) : (index + 1) * (rows // count)]
    if small:
        refs[count][...] = line.astype(jnp.bfloat16)


def gather_plane(first, second, x_first, x_second, y_first, y_second):
    near = [first, second, hop(x_first, 1), hop(x_second, 1), hop(y_first, 2), hop(y_second, 2)]
    return near + [hop(near[2], 2), hop(near[5], 1)]


def multiply(halves, where, early, late, small, deps):
    members = lax.axis_size("seq")
    lines = members // PLANE
    width = late[0].shape[1]
    rows = len(halves) * (early[0].shape[0] // 2 // lines)
    vmem = pl.BlockSpec(memory_space=pltpu.VMEM)
    out_shape = level_shapes(lines, rows, width, small)
    extra = [] if small is None else [small]
    return pl.pallas_call(
        functools.partial(products_kernel, halves, members, len(deps)),
        in_specs=[pl.BlockSpec(memory_space=pltpu.SMEM)] + [vmem] * (3 * PLANE + len(extra))
        + [pl.BlockSpec(memory_space=pl.ANY) for _ in deps],
        out_specs=[vmem] * len(out_shape), out_shape=out_shape,
        scratch_shapes=[pltpu.VMEM((lines, rows, width), jnp.float32)],
        compiler_params=params(), cost_estimate=cost(4), name="products",
    )(where, *early, *late, *extra, *deps)


def level_shapes(left, rows, width, small):
    kept = jax.ShapeDtypeStruct((left // 2, rows, width), jnp.float32)
    if small is None:
        return [kept, jax.ShapeDtypeStruct((left // 2 * rows, width), jnp.bfloat16)]
    sent = jax.ShapeDtypeStruct((small.shape[0] + left // 2 * rows, width), jnp.bfloat16)
    return [kept, jax.ShapeDtypeStruct(small.shape, jnp.float32), sent]


def add_line(level, where, parts, count, deps=()):
    f32, bf16 = jnp.float32, jnp.bfloat16
    kept, *small, sent = parts
    vmem = pl.BlockSpec(memory_space=pltpu.VMEM)
    got = hop(sent, PLANE << level)
    left, rows, width = kept.shape
    scratch = []
    if left > 1:
        out_shape = level_shapes(left, rows, width, small[0] if small else None)
        scratch = [pltpu.VMEM((left, rows, width), f32)]
    else:
        out_shape = [jax.ShapeDtypeStruct((rows // count, width), f32)] * count
        out_shape = out_shape + [jax.ShapeDtypeStruct(one.shape, bf16) for one in small]
    return pl.pallas_call(
        functools.partial(gather_kernel, level, count, bool(small), len(deps)),
        in_specs=[pl.BlockSpec(memory_space=pltpu.SMEM)] + [vmem] * (2 + len(small))
        + [pl.BlockSpec(memory_space=pl.ANY) for _ in deps],
        out_specs=[vmem] * len(out_shape), out_shape=out_shape, scratch_shapes=scratch,
        compiler_params=params(), cost_estimate=cost(2), name="gather",
    )(where, kept, *small, got, *deps)


def project_kernel(gated_ref, ggate_ref, out_w_ref, gate_w_ref, branch_ref, part_ref):
    branch_ref[...] = dot(gated_ref[...], out_w_ref[...], ((1,), (0,)))
    part_ref[...] = dot(ggate_ref[...], gate_w_ref[...], ((1,), (1,)))


def run_project(gated, ggate, out_w, gate_w):
    length = gated.shape[0]
    width, model = out_w.shape
    out = jax.ShapeDtypeStruct((length, model), jnp.float32)
    vmem = pl.BlockSpec(memory_space=pltpu.VMEM)
    return pl.pallas_call(
        project_kernel, in_specs=[vmem] * 4, out_specs=[vmem] * 2, out_shape=[out, out],
        compiler_params=params(), cost_estimate=cost(5), name="project",
    )(gated, ggate, out_w, gate_w)


def place_kernel(counts, where_ref, *refs):
    quarters, outs, (table_ref,) = refs[:PLANE], refs[PLANE:-1], refs[-1:]
    place = where_ref[0] % PLANE
    for mask, ref in enumerate(quarters):
        table_ref[jnp.bitwise_xor(place, mask)] = ref[...].astype(jnp.float32)
    table = jnp.concatenate([table_ref[quarter] for quarter in range(PLANE)], axis=0)
    for out, (first, count) in zip(outs, counts, strict=True):
        value = table[first : first + count]
        out[...] = value.reshape(value.shape[1]) if count == 1 else value


def run_place(where, own, counts):
    count, width = own.shape
    f32 = jnp.float32
    x, y = hop(own, 1), hop(own, 2)
    vmem = pl.BlockSpec(memory_space=pltpu.VMEM)
    shapes = [(width,) if number == 1 else (number, width) for _, number in counts]
    return pl.pallas_call(
        functools.partial(place_kernel, counts),
        in_specs=[pl.BlockSpec(memory_space=pltpu.SMEM)] + [vmem] * PLANE,
        out_specs=[vmem] * len(shapes),
        out_shape=[jax.ShapeDtypeStruct(shape, f32) for shape in shapes],
        scratch_shapes=[pltpu.VMEM((PLANE, count, width), f32)],
        compiler_params=params(), cost_estimate=cost(3), name="place",
    )(where, own, x, y, hop(x, 2))


def leave_kernel(tokens_ref, cot_ref, params_ref, branch_ref, branch_peer_ref, own_ref, peer_ref, mixed_ref, grad_ref):
    tokens = tokens_ref[...].astype(jnp.float32)
    mixed_ref[...] = (tokens + (branch_ref[...] + branch_peer_ref[...])).astype(jnp.bfloat16)
    scale = inverse_rms(tokens)
    scaled = (own_ref[...] + peer_ref[...]) * row(params_ref, GAIN)
    mean = jnp.mean(scaled * tokens, axis=1, keepdims=True)
    grad = cot_ref[...].astype(jnp.float32) + scale * scaled
    grad_ref[...] = grad - tokens * (scale * scale * scale * mean)


def run_leave(tokens, cot, stacked, branch, branch_peer, own, peer):
    vmem = pl.BlockSpec(memory_space=pltpu.VMEM)
    return pl.pallas_call(
        leave_kernel, in_specs=[vmem] * 7, out_specs=[vmem] * 2,
        out_shape=[
            jax.ShapeDtypeStruct(tokens.shape, jnp.bfloat16),
            jax.ShapeDtypeStruct(tokens.shape, jnp.float32),
        ],
        compiler_params=params(), cost_estimate=cost(3), name="leave",
    )(tokens, cot, stacked, branch, branch_peer, own, peer)


def from_behind(block, axis, distance):
    devices = range(lax.axis_size(axis))
    route = [(i - distance, i) for i in devices if i - distance in devices]
    return lax.ppermute(block, axis, route)


def swap(block):
    return lax.ppermute(block, "tp", [(0, 1), (1, 0)])


def hop(block, mask):
    members = lax.axis_size("seq")
    return lax.ppermute(block, "seq", [(i, i ^ mask) for i in range(members)])


def shards(
    tokens, norm_gain, in_conv_weight, in_gate_weight, conv_weight, conv_bias, scan_proj_weight,
    step_proj_weight, step_bias, decay_log, skip_gain, out_weight, segment_ids, cotangent,
):
    f32 = jnp.float32
    length, model = tokens.shape
    rank = step_proj_weight.shape[0]
    states = decay_log.shape[0]
    kernel = conv_weight.shape[0]
    width = conv_weight.shape[1]
    members = lax.axis_size("seq")
    device = lax.axis_index("seq")
    where = jnp.stack([device, lax.axis_index("tp")]).astype(jnp.int32)
    scan_width = rank + 2 * states
    padded_ids = jnp.concatenate([jnp.full((kernel,), -1, jnp.int32), segment_ids])
    near_ids = lax.dynamic_slice_in_dim(padded_ids, device * length, length + kernel)
    masks = jnp.stack(
        [near_ids[kernel:] == near_ids[tap + 1 : tap + 1 + length] for tap in range(kernel)]
    ).astype(f32)
    scan_weight = scan_proj_weight.T

    normed, rim_tokens, kept_early, *sent_early = run_early(where, tokens, cotangent, norm_gain)
    rim_tokens = from_behind(rim_tokens, "seq", 1)
    early = [kept_early] + [hop(one, mask) for mask, one in enumerate(sent_early, 1)]
    conv_in, ext, conv_out, gate_in, grad_gated, own, stacked = run_enter(
        normed, rim_tokens, cotangent, (conv_bias, step_bias, skip_gain, norm_gain), masks,
        in_conv_weight, in_gate_weight, out_weight, conv_weight, scan_weight,
    )
    peer = swap(own)
    ends, seeds, totals = run_ends(
        own, peer, step_proj_weight, stacked, decay_log, conv_out, grad_gated, gate_in, masks,
        early[1:],
    )
    near, far = exchange(where, totals, decay_log)
    gated, ggate, first_small, grad_conv, low_own = run_scan(
        where, own, peer, step_proj_weight, stacked, decay_log, conv_out, grad_gated, gate_in, masks,
        ends, seeds, near, far, (),
    )
    low_peer = swap(low_own)
    main, rim, second_small = run_taps(
        low_own, low_peer, conv_out, conv_in, ext, scan_weight, grad_conv, conv_weight, stacked, masks, (),
    )
    rim = from_behind(rim, "seq", -1)
    first_late = gather_plane(gated, ggate, gated, ggate, gated, ggate)
    branch_own, gate_part = run_project(gated, ggate, out_weight, in_gate_weight)
    *sent_late, small, normed_own = run_inputs(
        scan_width + kernel + 1, where, main, rim, in_conv_weight, gate_part, tokens, first_small,
        second_small, first_late[2:6],
    )
    second_late = gather_plane(*sent_late[:2], *sent_late)
    mixed_out, input_grad = run_leave(
        tokens, cotangent, stacked, branch_own, swap(branch_own), normed_own, swap(normed_own)
    )
    first = multiply((1, 0), where, early, first_late, None, (normed_own,))
    second = multiply((0,), where, early, second_late, small, first[:1])
    lines = members // PLANE
    for level in range(lines.bit_length() - 1):
        first = add_line(level, where, first, 2, () if level == 0 else ())
        second = add_line(level, where, second, 1, () if level == 0 else ())
    out_grad, in_gate_grad = first
    in_conv_grad, small = second
    first_row = first_small.shape[0]
    last_row = first_row + scan_width
    (
        step_proj_grad, decay_log_grad, step_bias_grad, skip_grad, scan_proj_grad, conv_weight_grad,
        conv_bias_grad, gain_grad,
    ) = run_place(
        where, small,
        (
            (0, rank), (rank, states), (rank + states, 1), (rank + states + 1, 1), (first_row, scan_width),
            (last_row, kernel), (last_row + kernel, 1), (last_row + kernel + 1, 1),
        ),
    )
    gain_grad = gain_grad + swap(gain_grad)
    return (
        mixed_out, input_grad, gain_grad, in_conv_grad, in_gate_grad, conv_weight_grad,
        conv_bias_grad, scan_proj_grad.T, step_proj_grad, step_bias_grad, decay_log_grad, skip_grad,
        out_grad.T,
    )


def solution(mesh):
    in_specs = (
        P("seq", None), P(), P(None, "tp"), P(None, "tp"), P(None, "tp"), P("tp"), P("tp", None),
        P(None, "tp"), P("tp"), P(None, "tp"), P("tp"), P("tp", None), P(), P("seq", None),
    )
    out_specs = (
        P("seq", None), P("seq", None), P(), P("seq", "tp"), P("seq", "tp"), P(None, "tp"), P("tp"),
        P("tp", None), P(None, "tp"), P("tp"), P(None, "tp"), P("tp"), P("tp", "seq"),
    )
    return jax.shard_map(shards, mesh=mesh, in_specs=in_specs, out_specs=out_specs, check_vma=False)
```

time: 204 us -> 174 us (0.85)
  starting transfers between devices: 53.6 us -> 43.4 us
  waiting for transfers between devices: 62.8 us -> 54.1 us
  Pallas kernels: 61.9 us -> 69.1 us
  matrix products: 6.84 us -> 0 us
  other arithmetic: 9.09 us -> 2.7 us
  local copies, waits for them, and re-layouts: 7.04 us -> 1.5 us
    all_to_all x2 -> x0, starting transfers between devices: 13.6 us -> none  [the longest x1 8.49 us: shards(): small = lax.all_to_all(run_spread(small), 'seq', 0, 0, tiled=True)]
    pallas_call x8 -> x11, Pallas kernels: 29.4 us -> 39.6 us  [the longest x4 9.11 us: add_line(): pl.pallas_call(functools.partial(gather_kernel, level, count, bool(small)...]
    dot_general x2 -> x0, matrix products: 6.84 us -> none  [dot(): lax.dot_general(first, second, (contract, ((), ())), preferred_element_ty...]
    slice x6 -> x0, local copies, waits for them, and re-layouts: 5.46 us -> none  [the longest x4 3.33 us: gather_plane(): return (late, x, y, hop(x[:cut], 2), hop(y[cut:], 1))]
    ppermute x23 -> x28, waiting for transfers between devices: 56.2 us -> 50.9 us  [hop(): return lax.ppermute(block, 'seq', [(i, i ^ mask) for i in range(members)])]
    ppermute x23 -> x28, starting transfers between devices: 32.1 us -> 36.4 us  [hop(): return lax.ppermute(block, 'seq', [(i, i ^ mask) for i in range(members)])]
    ppermute x2, waiting for transfers between devices: 3.4 us -> 0.01 us  [from_behind(): return lax.ppermute(block, axis, route)]
    sub x1 -> x0, other arithmetic: 3.07 us -> none  [shards(): cotangent.astype(f32) + inv_rms * scaled_grad]
  transfers between devices with their start and end apart: 32 -> 35, of which waited for: 14 -> 17; matrix products, arithmetic and copies ran while one was open for 9% -> 1% of each run, Pallas kernels for 13% -> 20%
where the time goes in v2:
time: 174 us; the launch traced here: 172 us
  Pallas kernels  69.1 us (40%)
  waiting for transfers between devices  54.1 us (31%)
  starting transfers between devices  43.4 us (25%)
  other arithmetic  2.7 us (2%)
    ppermute x28, waiting for transfers between devices, hop(): return lax.ppermute(block, 'seq', [(i, i ^ mask) for i in range(members)])  50.9 us
    ppermute x28, starting transfers between devices, hop(): return lax.ppermute(block, 'seq', [(i, i ^ mask) for i in range(members)])  36.4 us
    pallas_call x1, Pallas kernels, run_scan(): pl.pallas_call(functools.partial(scan_kernel, rank, states, members), in_...  14.1 us
    pallas_call x4, Pallas kernels, add_line(): pl.pallas_call(functools.partial(gather_kernel, level, count, bool(small)...  9.11 us
    pallas_call x2, Pallas kernels, multiply(): pl.pallas_call(functools.partial(products_kernel, halves, members, len(de...  8.93 us
    pallas_call x1, Pallas kernels, run_enter(): pl.pallas_call(functools.partial(enter_kernel, taps.shape[0], weight.shap...  7.16 us
    pallas_call x1, Pallas kernels, run_ends(): pl.pallas_call(functools.partial(ends_kernel, rank, states, len(deps)), i...  7.08 us
    ppermute x2, starting transfers between devices, from_behind(): return lax.ppermute(block, axis, route)  6.42 us
  transfers between devices with their start and end apart: 35, of which 17 were waited for; matrix products, arithmetic and copies ran while one was open for 1% of the time, Pallas kernels for 20%

profile of v2, /device:TPU:8, one launch (start us, length us, event | category | flops | bytes accessed | tf_op | source)
XLA Modules:
  0.0 171.6 jit_solution(15054156544144301538)
XLA Ops:
  0.6 0.6 pad_add_fusion.where_ref
  1.3 2.3 %early.1 = (bf16[128,1152]{1,0:T(8,128)(2,1)}, bf16[8,1152]{1,0:T(8,128)(2,1)}, bf16[576,128]{1,0:T(8,128)(2,1)}, bf16[576,128]{1,0:T(8,128)(2,1)}, bf16[576,128]{1,0:T(8,128)(2,1)}, /*index=5*/bf16[576,128]{1,0:T(8,128)(2,1)}) custom-call(s32[2]{0:T(128)} %pad_add_fusion.where_ref, bf16[128,1152]{1,0:T(8,128)(2,1)} %tokens_ref.5, ...), custom_call_target="tpu_custom_call" | custom-call | bytes 9000000 | tf_op jit(solution)/shard_map/early/pallas_call | solution.py:209
  3.6 3.4 %collective-permute-start = (bf16[8,1152]{1,0:T(8,128)(2,1)}, bf16[8,1152]{1,0:T(8,128)(2,1)}, u32[]{:S(2)}, u32[]{:S(2)}) collective-permute-start(bf16[8,1152]{1,0:T(8,128)(2,1)} %get-tuple-element.74), channel_id=1, source_target_pairs={{0,2},{2,4},{4,6},{6,8},{8,10},{10,12},{12,14},{14,16},{16,18},{18... | collective-permute-start | bytes 55304 | tf_op jit(solution)/shard_map/ppermute | solution.py:935
  7.0 1.6 collective-permute-start.2
  8.5 1.5 collective-permute-start.3
  10.0 0.5 collective-permute-start.4
  10.5 0.8 pad_dynamic-slice_fusion
  11.4 0.7 add_convert_fusion.masks_ref
  12.1 7.2 %enter.1 = (bf16[128,1152]{1,0:T(8,128)(2,1)}, f32[8,1152]{1,0:T(8,128)}, bf16[128,1152]{1,0:T(8,128)(2,1)}, f32[128,1152]{1,0:T(8,128)}, f32[128,1152]{1,0:T(8,...) custom-call(bf16[128,1152]{1,0:T(8,128)(2,1)} %get-tuple-element.73.normed_ref, ...), custom_call_target="tpu_custom_call" | custom-call | bytes 18000000 | tf_op jit(solution)/shard_map/enter/pallas_call | solution.py:150
  19.3 1.6 collective-permute-done.1.peer_ref
  20.9 7.1 %ends.1 = (f32[128,1152]{1,0:T(8,128)}, f32[128,1152]{1,0:T(8,128)}, bf16[48,1152]{1,0:T(8,128)(2,1)}) custom-call(f32[128,128]{1,0:T(8,128)} %get-tuple-element.76.own_ref, f32[128,128]{1,0:T(8,128)} %collective-permute-done.1.peer_ref, bf16[72,1152]{1,0:T(8,128)(2,1)} %weight_ref.4, f32[4,1152]{1,0:T(4,128)} %get-tuple-element.75.bias_ref.params_ref, ...), custom_call_target="tpu_custom_call" | custom-call | bytes 24000000 | tf_op jit(solution)/shard_map/ends/pallas_call | solution.py:468
  28.0 1.5 collective-permute-start.5
  29.5 1.5 collective-permute-start.6
  31.0 0.5 collective-permute-start.7
  31.5 1.9 %collective-permute-done.5.refs_1_ = bf16[48,1152]{1,0:T(8,128)(2,1)} collective-permute-done((bf16[48,1152]{1,0:T(8,128)(2,1)}, bf16[48,1152]{1,0:T(8,128)(2,1)}, u32[]{:S(2)}, u32[]{:S(2)}) %collective-permute-start.5) | collective-permute-done | bytes 110624 | tf_op jit(solution)/shard_map/ppermute | solution.py:944
  33.5 3.6 %collective-permute-done.6.refs_2_ = bf16[48,1152]{1,0:T(8,128)(2,1)} collective-permute-done((bf16[48,1152]{1,0:T(8,128)(2,1)}, bf16[48,1152]{1,0:T(8,128)(2,1)}, u32[]{:S(2)}, u32[]{:S(2)}) %collective-permute-start.6) | collective-permute-done | bytes 110624 | tf_op jit(solution)/shard_map/ppermute | solution.py:944
  37.0 2.1 %fold.1 = (f32[40,1152]{1,0:T(8,128)}, bf16[32,1152]{1,0:T(8,128)(2,1)}, bf16[32,1152]{1,0:T(8,128)(2,1)}, bf16[32,1152]{1,0:T(8,128)(2,1)}) custom-call(s32[2]{0:T(128)} %pad_add_fusion.where_ref, f32[16,1152]{1,0:T(8,128)} %decay_ref.5, bf16[48,1152]{1,0:T(8,128)(2,1)} %get-tuple-element.85.refs_0_, bf16[48,1152]{1,0:T(8,128)(2,1)} %collective-permute-done.5.refs_1_, ...), custom_call_target="tpu_custom_call" | custom-call | bytes 6000000 | tf_op jit(solution)/shard_map/fold/pallas_call | solution.py:607
  39.1 1.6 collective-permute-start.10
  40.7 2.5 %collective-permute-start.8 = (bf16[32,1152]{1,0:T(8,128)(2,1)}, bf16[32,1152]{1,0:T(8,128)(2,1)}, u32[]{:S(2)}, u32[]{:S(2)}) collective-permute-start(bf16[32,1152]{1,0:T(8,128)(2,1)} %get-tuple-element.87), channel_id=1, source_target_pairs={{0,8},{2,10},{4,12},{6,14},{8,0},{10,2},{12,4},{14,6},{16,24},{18,... | collective-permute-start | bytes 221192 | tf_op jit(solution)/shard_map/ppermute | solution.py:944
  43.2 2.7 %collective-permute-done.10.rest_2_ = bf16[32,1152]{1,0:T(8,128)(2,1)} collective-permute-done((bf16[32,1152]{1,0:T(8,128)(2,1)}, bf16[32,1152]{1,0:T(8,128)(2,1)}, u32[]{:S(2)}, u32[]{:S(2)}) %collective-permute-start.10) | collective-permute-done | bytes 73760 | tf_op jit(solution)/shard_map/ppermute | solution.py:944
  45.9 1.2 collective-permute-done.8.rest_0_
  47.1 1.6 collective-permute-done.9.rest_1_
  48.7 14.1 %scan.1 = (bf16[128,1152]{1,0:T(8,128)(2,1)}, bf16[128,1152]{1,0:T(8,128)(2,1)}, f32[96,1152]{1,0:T(8,128)}, f32[128,1152]{1,0:T(8,128)}, f32[128,128]{1,0:T(8,128)}) custom-call(s32[2]{0:T(128)} %pad_add_fusion.where_ref, f32[128,128]{1,0:T(8,128)} %get-tuple-element.76.own_ref, f32[128,128]{1,0:T(8,128)} %collective-permute-done.1.peer_ref, ...), custom_call_target="tpu_custom_call" | custom-call | bytes 45000000 | tf_op jit(solution)/shard_map/scan/pallas_call | solution.py:495
  62.8 0.5 collective-permute-start.14
  63.4 1.5 collective-permute-start.15
  65.3 1.6 collective-permute-start.17
  66.9 1.6 collective-permute-done.12.peer_ref
  68.5 3.8 %taps.1 = (f32[128,1152]{1,0:T(8,128)}, f32[8,1152]{1,0:T(8,128)}, f32[112,1152]{1,0:T(8,128)}) custom-call(f32[128,128]{1,0:T(8,128)} %get-tuple-element.93.own_ref, f32[128,128]{1,0:T(8,128)} %collective-permute-done.12.peer_ref, bf16[128,1152]{1,0:T(8,128)(2,1)} %get-tuple-element.77.conv_ref, bf16[128,1152]{1,0:T(8,128)(2,1)} %get-tuple-element.94.in_ref, ...), custom_call_target="tpu_custom_call" | custom-call | bytes 12000000 | tf_op jit(solution)/shard_map/taps/pallas_call | solution.py:679
  72.3 3.0 %collective-permute-start.13 = (f32[8,1152]{1,0:T(8,128)}, f32[8,1152]{1,0:T(8,128)}, u32[]{:S(2)}, u32[]{:S(2)}) collective-permute-start(f32[8,1152]{1,0:T(8,128)} %get-tuple-element.98), channel_id=1, source_target_pairs={{2,0},{4,2},{6,4},{8,6},{10,8},{12,10},{14,12},{16,14},{18,16},{20... | collective-permute-start | bytes 110600 | tf_op jit(solution)/shard_map/ppermute | solution.py:935
  75.4 4.9 %project.1 = (f32[128,1152]{1,0:T(8,128)}, f32[128,1152]{1,0:T(8,128)}) custom-call(bf16[128,1152]{1,0:T(8,128)(2,1)} %get-tuple-element.90.gated_ref.rest_4_, bf16[128,1152]{1,0:T(8,128)(2,1)} %get-tuple-element.91.ggate_ref.rest_5_, bf16[1152,1152]{1,0:T(8,128)(2,1)} %out_w_ref.3, bf16[1152,1152]{1,0:T(8,128)(2,1)} %gate_w_ref.3), custom_call_target="tpu_custom_call" | custom-call | bytes 15000000 | tf_op jit(solution)/shard_map/project/pallas_call | solution.py:877
  80.3 4.6 %inputs.1 = (bf16[120,1152]{1,0:T(8,128)(2,1)}, bf16[120,1152]{1,0:T(8,128)(2,1)}, bf16[120,1152]{1,0:T(8,128)(2,1)}, bf16[64,1152]{1,0:T(8,128)(2,1)}, f32[56,1152]{1,0:T(8,128)}, /*index=5*/f32[128,1152]{1,0:T(8,128)}) custom-call(s32[2]{0:T(128)} %pad_add_fusion.where_ref, f32[128,1152]{1,0:T(8,128)} %get-tuple-element.97.main_ref, ...), custom_call_target="tpu_custom_call" | custom-call | bytes 9000000 | tf_op jit(solution)/shard_map/inputs/pallas_call | solution.py:732
  84.9 1.1 collective-permute-start.19
  85.9 1.0 collective-permute-start.25
  86.9 1.0 collective-permute-start.22
  88.0 1.0 collective-permute-start.26
  88.9 1.1 collective-permute-start.20
  90.0 7.9 %collective-permute-done.22.rest_9_ = bf16[64,1152]{1,0:T(8,128)(2,1)} collective-permute-done((bf16[64,1152]{1,0:T(8,128)(2,1)}, bf16[64,1152]{1,0:T(8,128)(2,1)}, u32[]{:S(2)}, u32[]{:S(2)}) %collective-permute-start.22) | collective-permute-done | bytes 147488 | tf_op jit(solution)/shard_map/ppermute | solution.py:944
  97.9 0.5 collective-permute-start.21
  98.4 1.6 collective-permute-start.23
  100.0 0.9 collective-permute-start.24
  101.0 5.0 %products.2 = (f32[2,144,1152]{2,1,0:T(8,128)}, bf16[288,1152]{1,0:T(8,128)(2,1)}) custom-call(s32[2]{0:T(128)} %pad_add_fusion.where_ref, bf16[576,128]{1,0:T(8,128)(2,1)} %get-tuple-element.105.rest_0_, bf16[576,128]{1,0:T(8,128)(2,1)} %collective-permute-done.2.rest_0_.rest_1_, bf16[576,128]{1,0:T(8,128)(2,1)} %collective-permute-done.3.rest_1_.rest_2_, ...), custom_call_target="tpu_custom_call" | custom-call | bytes 12000000 | tf_op jit(solution)/shard_map/products/pallas_call | solution.py:827
  106.0 0.9 collective-permute-done.20.rest_7_
  106.9 0.9 collective-permute-done.21.rest_8_
  107.8 1.2 collective-permute-done.24.rest_11_
  109.0 2.4 %collective-permute-done.23.rest_10_ = bf16[120,1152]{1,0:T(8,128)(2,1)} collective-permute-done((bf16[120,1152]{1,0:T(8,128)(2,1)}, bf16[120,1152]{1,0:T(8,128)(2,1)}, u32[]{:S(2)}, u32[]{:S(2)}) %collective-permute-start.23) | collective-permute-done | bytes 276512 | tf_op jit(solution)/shard_map/ppermute | solution.py:944
  111.4 3.9 %products.3 = (f32[2,72,1152]{2,1,0:T(8,128)}, f32[56,1152]{1,0:T(8,128)}, bf16[200,1152]{1,0:T(8,128)(2,1)}) custom-call(s32[2]{0:T(128)} %pad_add_fusion.where_ref, bf16[576,128]{1,0:T(8,128)(2,1)} %get-tuple-element.105.rest_0_, bf16[576,128]{1,0:T(8,128)(2,1)} %collective-permute-done.2.rest_0_.rest_1_, ...), custom_call_target="tpu_custom_call" | custom-call | bytes 12000000 | tf_op jit(solution)/shard_map/products/pallas_call | solution.py:827
  115.4 1.9 %collective-permute-start.33 = (bf16[288,1152]{1,0:T(8,128)(2,1)}, bf16[288,1152]{1,0:T(8,128)(2,1)}, u32[]{:S(2)}, u32[]{:S(2)}) collective-permute-start(bf16[288,1152]{1,0:T(8,128)(2,1)} %get-tuple-element.121), channel_id=1, source_target_pairs={{0,8},{2,10},{4,12},{6,14},{8,0},{10,2},{12,4},{14,6},{16,24},{18,... | collective-permute-start | bytes 1990664 | tf_op jit(solution)/shard_map/ppermute | solution.py:944
  117.3 0.5 collective-permute-start.18
  117.8 11.3 %collective-permute-done.27.refs_1_ = bf16[200,1152]{1,0:T(8,128)(2,1)} collective-permute-done((bf16[200,1152]{1,0:T(8,128)(2,1)}, bf16[200,1152]{1,0:T(8,128)(2,1)}, u32[]{:S(2)}, u32[]{:S(2)}) %collective-permute-start.27) | collective-permute-done | bytes 460832 | tf_op jit(solution)/shard_map/ppermute | solution.py:944
  129.1 2.4 %gather.4 = (f32[1,72,1152]{2,1,0:T(8,128)}, f32[56,1152]{1,0:T(8,128)}, bf16[128,1152]{1,0:T(8,128)(2,1)}) custom-call(s32[2]{0:T(128)} %pad_add_fusion.where_ref, f32[2,72,1152]{2,1,0:T(8,128)} %get-tuple-element.112.kept_ref, f32[56,1152]{1,0:T(8,128)} %get-tuple-element.113.refs_0_, bf16[200,1152]{1,0:T(8,128)(2,1)} %collective-permute-done.27.refs_1_), custom_call_target="tpu_custom_call" | custom-call | bytes 6000000 | tf_op jit(solution)/shard_map/gather/pallas_call | solution.py:858
  131.5 5.4 %collective-permute-start.28 = (bf16[128,1152]{1,0:T(8,128)(2,1)}, bf16[128,1152]{1,0:T(8,128)(2,1)}, u32[]{:S(2)}, u32[]{:S(2)}) collective-permute-start(bf16[128,1152]{1,0:T(8,128)(2,1)} %get-tuple-element.117), channel_id=1, source_target_pairs={{0,16},{2,18},{4,20},{6,22},{8,24},{10,26},{12,28},{14,30},{16,0},... | collective-permute-start | bytes 884744 | tf_op jit(solution)/shard_map/ppermute | solution.py:944
  136.9 7.3 %collective-permute-done.33.refs_0_ = bf16[288,1152]{1,0:T(8,128)(2,1)} collective-permute-done((bf16[288,1152]{1,0:T(8,128)(2,1)}, bf16[288,1152]{1,0:T(8,128)(2,1)}, u32[]{:S(2)}, u32[]{:S(2)}) %collective-permute-start.33) | collective-permute-done | bytes 663584 | tf_op jit(solution)/shard_map/ppermute | solution.py:944
  144.2 2.7 %gather.6 = (f32[1,144,1152]{2,1,0:T(8,128)}, bf16[144,1152]{1,0:T(8,128)(2,1)}) custom-call(s32[2]{0:T(128)} %pad_add_fusion.where_ref, f32[2,144,1152]{2,1,0:T(8,128)} %get-tuple-element.111.rest_13_.kept_ref, bf16[288,1152]{1,0:T(8,128)(2,1)} %collective-permute-done.33.refs_0_), custom_call_target="tpu_custom_call" | custom-call | bytes 6000000 | tf_op jit(solution)/shard_map/gather/pallas_call | solution.py:858
  146.9 3.4 %collective-permute-start.34 = (bf16[144,1152]{1,0:T(8,128)(2,1)}, bf16[144,1152]{1,0:T(8,128)(2,1)}, u32[]{:S(2)}, u32[]{:S(2)}) collective-permute-start(bf16[144,1152]{1,0:T(8,128)(2,1)} %get-tuple-element.123), channel_id=1, source_target_pairs={{0,16},{2,18},{4,20},{6,22},{8,24},{10,26},{12,28},{14,30},{16,0},... | collective-permute-start | bytes 995336 | tf_op jit(solution)/shard_map/ppermute | solution.py:944
  150.3 2.0 %gather.5 = (f32[72,1152]{1,0:T(8,128)}, bf16[56,1152]{1,0:T(8,128)(2,1)}) custom-call(s32[2]{0:T(128)} %pad_add_fusion.where_ref, f32[1,72,1152]{2,1,0:T(8,128)} %get-tuple-element.115.kept_ref, f32[56,1152]{1,0:T(8,128)} %get-tuple-element.116.refs_0_, bf16[128,1152]{1,0:T(8,128)(2,1)} %collective-permute-done.28.refs_1_), custom_call_target="tpu_custom_call" | custom-call | bytes 6000000 | tf_op jit(solution)/shard_map/gather/pallas_call | solution.py:858
  152.3 0.8 collective-permute-start.29
  153.1 1.1 collective-permute-start.30
  154.2 3.2 %collective-permute-done.29.refs_1_ = bf16[56,1152]{1,0:T(8,128)(2,1)S(1)} collective-permute-done((bf16[56,1152]{1,0:T(8,128)(2,1)}, bf16[56,1152]{1,0:T(8,128)(2,1)S(1)}, u32[]{:S(2)}, u32[]{:S(2)}) %collective-permute-start.29) | collective-permute-done | bytes 129056 | tf_op jit(solution)/shard_map/ppermute | solution.py:944
  157.5 0.6 copy-done
  158.5 4.7 %collective-permute-done.31.refs_3_ = bf16[56,1152]{1,0:T(8,128)(2,1)} collective-permute-done((bf16[56,1152]{1,0:T(8,128)(2,1)S(1)}, bf16[56,1152]{1,0:T(8,128)(2,1)}, u32[]{:S(2)}, u32[]{:S(2)}) %collective-permute-start.31) | collective-permute-done | bytes 129056 | tf_op jit(solution)/shard_map/ppermute | solution.py:944
  163.2 2.1 %place.1 = (f32[72,1152]{1,0:T(8,128)}, f32[16,1152]{1,0:T(8,128)}, f32[1152]{0:T(1024)}, f32[1152]{0:T(1024)}, f32[104,1152]{1,0:T(8,128)}, /*index=5*/f32[4,1152]{1,0:T(4,128)}, f32[1152]{0:T(1024)}, f32[1152]{0:T(1024)}) custom-call(s32[2]{0:T(128)} %pad_add_fusion.where_ref, bf16[56,1152]{1,0:T(8,128)(2,1)} %get-tuple-element.118.refs_0_, ...), custom_call_target="tpu_custom_call" | custom-call | bytes 9000000 | tf_op jit(solution)/shard_map/place/pallas_call | solution.py:900
  165.3 2.9 %leave.1 = (bf16[128,1152]{1,0:T(8,128)(2,1)}, f32[128,1152]{1,0:T(8,128)}) custom-call(bf16[128,1152]{1,0:T(8,128)(2,1)} %tokens_ref.5, bf16[128,1152]{1,0:T(8,128)(2,1)} %cot_ref.5, f32[4,1152]{1,0:T(4,128)} %get-tuple-element.75.bias_ref.params_ref, f32[128,1152]{1,0:T(8,128)} %get-tuple-element.92.branch_ref, ...), custom_call_target="tpu_custom_call" | custom-call | bytes 9000000 | tf_op jit(solution)/shard_map/leave/pallas_call | solution.py:922
  168.2 2.0 %gather.7 = (f32[72,1152]{1,0:T(8,128)}, f32[72,1152]{1,0:T(8,128)}) custom-call(s32[2]{0:T(128)} %pad_add_fusion.where_ref, f32[1,144,1152]{2,1,0:T(8,128)} %get-tuple-element.122.kept_ref, bf16[144,1152]{1,0:T(8,128)(2,1)} %collective-permute-done.34.refs_0_), custom_call_target="tpu_custom_call" | custom-call | bytes 6000000 | tf_op jit(solution)/shard_map/gather/pallas_call | solution.py:858
  170.3 1.3 add.9
  (30 shorter events, 1.3 us)
Async XLA Ops:
  3.6 8.5 %collective-permute-start = (bf16[8,1152]{1,0:T(8,128)(2,1)}, bf16[8,1152]{1,0:T(8,128)(2,1)}, u32[]{:S(2)}, u32[]{:S(2)}) collective-permute-start(bf16[8,1152]{1,0:T(8,128)(2,1)} %get-tuple-element.74), channel_id=1, source_target_pairs={{0,2},{2,4},{4,6},{6,8},{8,10},{10,12},{12,14},{14,16},{16,18},{18... | collective-permute-start | bytes 55304 | tf_op jit(solution)/shard_map/ppermute | solution.py:935
  7.0 14.0 %collective-permute-start.2 = (bf16[576,128]{1,0:T(8,128)(2,1)}, bf16[576,128]{1,0:T(8,128)(2,1)}, u32[]{:S(2)}, u32[]{:S(2)}) collective-permute-start(bf16[576,128]{1,0:T(8,128)(2,1)} %get-tuple-element.80), channel_id=1, source_target_pairs={{0,2},{2,0},{4,6},{6,4},{8,10},{10,8},{12,14},{14,12},{16,18},{18,... | collective-permute-start | bytes 442376 | tf_op jit(solution)/shard_map/ppermute | solution.py:944
  8.5 12.4 %collective-permute-start.3 = (bf16[576,128]{1,0:T(8,128)(2,1)}, bf16[576,128]{1,0:T(8,128)(2,1)}, u32[]{:S(2)}, u32[]{:S(2)}) collective-permute-start(bf16[576,128]{1,0:T(8,128)(2,1)} %get-tuple-element.81), channel_id=1, source_target_pairs={{0,4},{2,6},{4,0},{6,2},{8,12},{10,14},{12,8},{14,10},{16,20},{18,... | collective-permute-start | bytes 442376 | tf_op jit(solution)/shard_map/ppermute | solution.py:944
  10.0 10.9 %collective-permute-start.4 = (bf16[576,128]{1,0:T(8,128)(2,1)}, bf16[576,128]{1,0:T(8,128)(2,1)}, u32[]{:S(2)}, u32[]{:S(2)}) collective-permute-start(bf16[576,128]{1,0:T(8,128)(2,1)} %get-tuple-element.82), channel_id=1, source_target_pairs={{0,6},{2,4},{4,2},{6,0},{8,14},{10,12},{12,10},{14,8},{16,22},{18,... | collective-permute-start | bytes 442376 | tf_op jit(solution)/shard_map/ppermute | solution.py:944
  19.3 1.7 collective-permute-start.1
  28.0 5.4 %collective-permute-start.5 = (bf16[48,1152]{1,0:T(8,128)(2,1)}, bf16[48,1152]{1,0:T(8,128)(2,1)}, u32[]{:S(2)}, u32[]{:S(2)}) collective-permute-start(bf16[48,1152]{1,0:T(8,128)(2,1)} %get-tuple-element.85.refs_0_), channel_id=1, source_target_pairs={{0,2},{2,0},{4,6},{6,4},{8,10},{10,8},{12,14},{14,12},{16,18},{18,... | collective-permute-start | bytes 331784 | tf_op jit(solution)/shard_map/ppermute | solution.py:944
  29.5 7.5 %collective-permute-start.6 = (bf16[48,1152]{1,0:T(8,128)(2,1)}, bf16[48,1152]{1,0:T(8,128)(2,1)}, u32[]{:S(2)}, u32[]{:S(2)}) collective-permute-start(bf16[48,1152]{1,0:T(8,128)(2,1)} %get-tuple-element.85.refs_0_), channel_id=1, source_target_pairs={{0,4},{2,6},{4,0},{6,2},{8,12},{10,14},{12,8},{14,10},{16,20},{18,... | collective-permute-start | bytes 331784 | tf_op jit(solution)/shard_map/ppermute | solution.py:944
  31.0 6.0 %collective-permute-start.7 = (bf16[48,1152]{1,0:T(8,128)(2,1)}, bf16[48,1152]{1,0:T(8,128)(2,1)}, u32[]{:S(2)}, u32[]{:S(2)}) collective-permute-start(bf16[48,1152]{1,0:T(8,128)(2,1)} %get-tuple-element.85.refs_0_), channel_id=1, source_target_pairs={{0,6},{2,4},{4,2},{6,0},{8,14},{10,12},{12,10},{14,8},{16,22},{18,... | collective-permute-start | bytes 331784 | tf_op jit(solution)/shard_map/ppermute | solution.py:944
  39.1 6.7 %collective-permute-start.10 = (bf16[32,1152]{1,0:T(8,128)(2,1)}, bf16[32,1152]{1,0:T(8,128)(2,1)}, u32[]{:S(2)}, u32[]{:S(2)}) collective-permute-start(bf16[32,1152]{1,0:T(8,128)(2,1)} %get-tuple-element.89), channel_id=1, source_target_pairs={{0,24},{2,26},{4,28},{6,30},{8,16},{10,18},{12,20},{14,22},{16,8},... | collective-permute-start | bytes 221192 | tf_op jit(solution)/shard_map/ppermute | solution.py:944
  40.7 6.4 %collective-permute-start.8 = (bf16[32,1152]{1,0:T(8,128)(2,1)}, bf16[32,1152]{1,0:T(8,128)(2,1)}, u32[]{:S(2)}, u32[]{:S(2)}) collective-permute-start(bf16[32,1152]{1,0:T(8,128)(2,1)} %get-tuple-element.87), channel_id=1, source_target_pairs={{0,8},{2,10},{4,12},{6,14},{8,0},{10,2},{12,4},{14,6},{16,24},{18,... | collective-permute-start | bytes 221192 | tf_op jit(solution)/shard_map/ppermute | solution.py:944
  43.2 5.6 %collective-permute-start.9 = (bf16[32,1152]{1,0:T(8,128)(2,1)}, bf16[32,1152]{1,0:T(8,128)(2,1)}, u32[]{:S(2)}, u32[]{:S(2)}) collective-permute-start(bf16[32,1152]{1,0:T(8,128)(2,1)} %get-tuple-element.88), channel_id=1, source_target_pairs={{0,16},{2,18},{4,20},{6,22},{8,24},{10,26},{12,28},{14,30},{16,0},... | collective-permute-start | bytes 221192 | tf_op jit(solution)/shard_map/ppermute | solution.py:944
  62.8 17.4 %collective-permute-start.14 = (bf16[128,1152]{1,0:T(8,128)(2,1)}, bf16[128,1152]{1,0:T(8,128)(2,1)}, u32[]{:S(2)}, u32[]{:S(2)}) collective-permute-start(bf16[128,1152]{1,0:T(8,128)(2,1)} %get-tuple-element.90.gated_ref.rest_4_), channel_id=1, source_target_pairs={{0,2},{2,0},{4,6},{6,4},{8,10},{10,8},{12,14},{14,12},{16,18},{18,... | collective-permute-start | bytes 884744 | tf_op jit(solution)/shard_map/ppermute | solution.py:944
  63.4 16.9 %collective-permute-start.15 = (bf16[128,1152]{1,0:T(8,128)(2,1)}, bf16[128,1152]{1,0:T(8,128)(2,1)}, u32[]{:S(2)}, u32[]{:S(2)}) collective-permute-start(bf16[128,1152]{1,0:T(8,128)(2,1)} %get-tuple-element.91.ggate_ref.rest_5_), channel_id=1, source_target_pairs={{0,2},{2,0},{4,6},{6,4},{8,10},{10,8},{12,14},{14,12},{16,18},{18,... | collective-permute-start | bytes 884744 | tf_op jit(solution)/shard_map/ppermute | solution.py:944
  64.9 15.4 %collective-permute-start.16 = (bf16[128,1152]{1,0:T(8,128)(2,1)}, bf16[128,1152]{1,0:T(8,128)(2,1)}, u32[]{:S(2)}, u32[]{:S(2)}) collective-permute-start(bf16[128,1152]{1,0:T(8,128)(2,1)} %get-tuple-element.90.gated_ref.rest_4_), channel_id=1, source_target_pairs={{0,4},{2,6},{4,0},{6,2},{8,12},{10,14},{12,8},{14,10},{16,20},{18,... | collective-permute-start | bytes 884744 | tf_op jit(solution)/shard_map/ppermute | solution.py:944
  65.3 15.0 %collective-permute-start.17 = (bf16[128,1152]{1,0:T(8,128)(2,1)}, bf16[128,1152]{1,0:T(8,128)(2,1)}, u32[]{:S(2)}, u32[]{:S(2)}) collective-permute-start(bf16[128,1152]{1,0:T(8,128)(2,1)} %get-tuple-element.91.ggate_ref.rest_5_), channel_id=1, source_target_pairs={{0,4},{2,6},{4,0},{6,2},{8,12},{10,14},{12,8},{14,10},{16,20},{18,... | collective-permute-start | bytes 884744 | tf_op jit(solution)/shard_map/ppermute | solution.py:944
  66.9 1.6 collective-permute-start.12
  72.3 7.9 %collective-permute-start.13 = (f32[8,1152]{1,0:T(8,128)}, f32[8,1152]{1,0:T(8,128)}, u32[]{:S(2)}, u32[]{:S(2)}) collective-permute-start(f32[8,1152]{1,0:T(8,128)} %get-tuple-element.98), channel_id=1, source_target_pairs={{2,0},{4,2},{6,4},{8,6},{10,8},{12,10},{14,12},{16,14},{18,16},{20... | collective-permute-start | bytes 110600 | tf_op jit(solution)/shard_map/ppermute | solution.py:935
  84.9 13.5 %collective-permute-start.19 = (bf16[120,1152]{1,0:T(8,128)(2,1)}, bf16[120,1152]{1,0:T(8,128)(2,1)}, u32[]{:S(2)}, u32[]{:S(2)}) collective-permute-start(bf16[120,1152]{1,0:T(8,128)(2,1)} %get-tuple-element.106.rest_4_), channel_id=1, source_target_pairs={{0,2},{2,0},{4,6},{6,4},{8,10},{10,8},{12,14},{14,12},{16,18},{18,... | collective-permute-start | bytes 829448 | tf_op jit(solution)/shard_map/ppermute | solution.py:944
  85.9 14.0 %collective-permute-start.25 = (bf16[128,1152]{1,0:T(8,128)(2,1)}, bf16[128,1152]{1,0:T(8,128)(2,1)}, u32[]{:S(2)}, u32[]{:S(2)}) collective-permute-start(bf16[128,1152]{1,0:T(8,128)(2,1)} %collective-permute-done.14.rest_0_.rest_6_), channel_id=1, source_target_pairs={{0,4},{2,6},{4,0},{6,2},{8,12},{10,14},{12,8},{14,10},{16,20},{18,... | collective-permute-start | bytes 884744 | tf_op jit(solution)/shard_map/ppermute | solution.py:944
  86.9 11.0 %collective-permute-start.22 = (bf16[64,1152]{1,0:T(8,128)(2,1)}, bf16[64,1152]{1,0:T(8,128)(2,1)}, u32[]{:S(2)}, u32[]{:S(2)}) collective-permute-start(bf16[64,1152]{1,0:T(8,128)(2,1)} %get-tuple-element.109), channel_id=1, source_target_pairs={{0,4},{2,6},{4,0},{6,2},{8,12},{10,14},{12,8},{14,10},{16,20},{18,... | collective-permute-start | bytes 442376 | tf_op jit(solution)/shard_map/ppermute | solution.py:944
  88.0 13.0 %collective-permute-start.26 = (bf16[128,1152]{1,0:T(8,128)(2,1)}, bf16[128,1152]{1,0:T(8,128)(2,1)}, u32[]{:S(2)}, u32[]{:S(2)}) collective-permute-start(bf16[128,1152]{1,0:T(8,128)(2,1)} %collective-permute-done.17.rest_3_.rest_9_), channel_id=1, source_target_pairs={{0,2},{2,0},{4,6},{6,4},{8,10},{10,8},{12,14},{14,12},{16,18},{18,... | collective-permute-start | bytes 884744 | tf_op jit(solution)/shard_map/ppermute | solution.py:944
  88.9 18.0 %collective-permute-start.20 = (bf16[120,1152]{1,0:T(8,128)(2,1)}, bf16[120,1152]{1,0:T(8,128)(2,1)}, u32[]{:S(2)}, u32[]{:S(2)}) collective-permute-start(bf16[120,1152]{1,0:T(8,128)(2,1)} %get-tuple-element.107.rest_5_), channel_id=1, source_target_pairs={{0,2},{2,0},{4,6},{6,4},{8,10},{10,8},{12,14},{14,12},{16,18},{18,... | collective-permute-start | bytes 829448 | tf_op jit(solution)/shard_map/ppermute | solution.py:944
  97.9 9.9 %collective-permute-start.21 = (bf16[120,1152]{1,0:T(8,128)(2,1)}, bf16[120,1152]{1,0:T(8,128)(2,1)}, u32[]{:S(2)}, u32[]{:S(2)}) collective-permute-start(bf16[120,1152]{1,0:T(8,128)(2,1)} %get-tuple-element.108), channel_id=1, source_target_pairs={{0,4},{2,6},{4,0},{6,2},{8,12},{10,14},{12,8},{14,10},{16,20},{18,... | collective-permute-start | bytes 829448 | tf_op jit(solution)/shard_map/ppermute | solution.py:944
  98.4 13.0 %collective-permute-start.23 = (bf16[120,1152]{1,0:T(8,128)(2,1)}, bf16[120,1152]{1,0:T(8,128)(2,1)}, u32[]{:S(2)}, u32[]{:S(2)}) collective-permute-start(bf16[120,1152]{1,0:T(8,128)(2,1)} %collective-permute-done.19.rest_6_), channel_id=1, source_target_pairs={{0,4},{2,6},{4,0},{6,2},{8,12},{10,14},{12,8},{14,10},{16,20},{18,... | collective-permute-start | bytes 829448 | tf_op jit(solution)/shard_map/ppermute | solution.py:944
  100.0 9.0 %collective-permute-start.24 = (bf16[64,1152]{1,0:T(8,128)(2,1)}, bf16[64,1152]{1,0:T(8,128)(2,1)}, u32[]{:S(2)}, u32[]{:S(2)}) collective-permute-start(bf16[64,1152]{1,0:T(8,128)(2,1)} %collective-permute-done.22.rest_9_), channel_id=1, source_target_pairs={{0,2},{2,0},{4,6},{6,4},{8,10},{10,8},{12,14},{14,12},{16,18},{18,... | collective-permute-start | bytes 442376 | tf_op jit(solution)/shard_map/ppermute | solution.py:944
  115.3 13.8 %collective-permute-start.27 = (bf16[200,1152]{1,0:T(8,128)(2,1)}, bf16[200,1152]{1,0:T(8,128)(2,1)}, u32[]{:S(2)}, u32[]{:S(2)}) collective-permute-start(bf16[200,1152]{1,0:T(8,128)(2,1)} %get-tuple-element.114), channel_id=1, source_target_pairs={{0,8},{2,10},{4,12},{6,14},{8,0},{10,2},{12,4},{14,6},{16,24},{18,... | collective-permute-start | bytes 1382408 | tf_op jit(solution)/shard_map/ppermute | solution.py:944
  115.4 28.8 %collective-permute-start.33 = (bf16[288,1152]{1,0:T(8,128)(2,1)}, bf16[288,1152]{1,0:T(8,128)(2,1)}, u32[]{:S(2)}, u32[]{:S(2)}) collective-permute-start(bf16[288,1152]{1,0:T(8,128)(2,1)} %get-tuple-element.121), channel_id=1, source_target_pairs={{0,8},{2,10},{4,12},{6,14},{8,0},{10,2},{12,4},{14,6},{16,24},{18,... | collective-permute-start | bytes 1990664 | tf_op jit(solution)/shard_map/ppermute | solution.py:944
  117.3 48.0 %collective-permute-start.11 = (f32[128,1152]{1,0:T(8,128)}, f32[128,1152]{1,0:T(8,128)}, u32[]{:S(2)}, u32[]{:S(2)}) collective-permute-start(f32[128,1152]{1,0:T(8,128)} %get-tuple-element.92.branch_ref), channel_id=1, source_target_pairs={{0,1},{1,0},{2,3},{3,2},{4,5},{5,4},{6,7},{7,6},{8,9},{9,8},{10,11... | collective-permute-start | bytes 1769480 | tf_op jit(solution)/shard_map/ppermute | solution.py:939
  117.3 48.0 %collective-permute-start.18 = (f32[128,1152]{1,0:T(8,128)}, f32[128,1152]{1,0:T(8,128)}, u32[]{:S(2)}, u32[]{:S(2)}) collective-permute-start(f32[128,1152]{1,0:T(8,128)} %get-tuple-element.102.own_ref.rest_12_), channel_id=1, source_target_pairs={{0,1},{1,0},{2,3},{3,2},{4,5},{5,4},{6,7},{7,6},{8,9},{9,8},{10,11... | collective-permute-start | bytes 1769480 | tf_op jit(solution)/shard_map/ppermute | solution.py:939
  131.5 18.9 %collective-permute-start.28 = (bf16[128,1152]{1,0:T(8,128)(2,1)}, bf16[128,1152]{1,0:T(8,128)(2,1)}, u32[]{:S(2)}, u32[]{:S(2)}) collective-permute-start(bf16[128,1152]{1,0:T(8,128)(2,1)} %get-tuple-element.117), channel_id=1, source_target_pairs={{0,16},{2,18},{4,20},{6,22},{8,24},{10,26},{12,28},{14,30},{16,0},... | collective-permute-start | bytes 884744 | tf_op jit(solution)/shard_map/ppermute | solution.py:944
  146.9 21.4 %collective-permute-start.34 = (bf16[144,1152]{1,0:T(8,128)(2,1)}, bf16[144,1152]{1,0:T(8,128)(2,1)}, u32[]{:S(2)}, u32[]{:S(2)}) collective-permute-start(bf16[144,1152]{1,0:T(8,128)(2,1)} %get-tuple-element.123), channel_id=1, source_target_pairs={{0,16},{2,18},{4,20},{6,22},{8,24},{10,26},{12,28},{14,30},{16,0},... | collective-permute-start | bytes 995336 | tf_op jit(solution)/shard_map/ppermute | solution.py:944
  152.3 5.2 %collective-permute-start.29 = (bf16[56,1152]{1,0:T(8,128)(2,1)}, bf16[56,1152]{1,0:T(8,128)(2,1)S(1)}, u32[]{:S(2)}, u32[]{:S(2)}) collective-permute-start(bf16[56,1152]{1,0:T(8,128)(2,1)} %get-tuple-element.118.refs_0_), channel_id=1, source_target_pairs={{0,2},{2,0},{4,6},{6,4},{8,10},{10,8},{12,14},{14,12},{16,18},{18,... | collective-permute-start | bytes 387080 | tf_op jit(solution)/shard_map/ppermute | solution.py:944
  153.1 5.4 %collective-permute-start.30 = (bf16[56,1152]{1,0:T(8,128)(2,1)}, bf16[56,1152]{1,0:T(8,128)(2,1)}, u32[]{:S(2)}, u32[]{:S(2)}) collective-permute-start(bf16[56,1152]{1,0:T(8,128)(2,1)} %get-tuple-element.118.refs_0_), channel_id=1, source_target_pairs={{0,4},{2,6},{4,0},{6,2},{8,12},{10,14},{12,8},{14,10},{16,20},{18,... | collective-permute-start | bytes 387080 | tf_op jit(solution)/shard_map/ppermute | solution.py:944
  157.5 0.7 copy-start
  158.1 5.1 %collective-permute-start.31 = (bf16[56,1152]{1,0:T(8,128)(2,1)S(1)}, bf16[56,1152]{1,0:T(8,128)(2,1)}, u32[]{:S(2)}, u32[]{:S(2)}) collective-permute-start(bf16[56,1152]{1,0:T(8,128)(2,1)S(1)} %collective-permute-done.29.refs_1_), channel_id=1, source_target_pairs={{0,4},{2,6},{4,0},{6,2},{8,12},{10,14},{12,8},{14,10},{16,20},{18,... | collective-permute-start | bytes 387080 | tf_op jit(solution)/shard_map/ppermute | solution.py:944
  165.3 5.0 %collective-permute-start.32 = (f32[1152]{0:T(1024)}, f32[1152]{0:T(1024)}, u32[]{:S(2)}, u32[]{:S(2)}) collective-permute-start(f32[1152]{0:T(1024)} %get-tuple-element.119), channel_id=1, source_target_pairs={{0,1},{1,0},{2,3},{3,2},{4,5},{5,4},{6,7},{7,6},{8,9},{9,8},{10,11... | collective-permute-start | bytes 13832 | tf_op jit(solution)/shard_map/ppermute | solution.py:939

commit v3 on v2

--- a/solution.py
+++ b/solution.py
@@ -317,7 +317,7 @@
 ):
     stride, radix = levels(members)[-1]
     far_refs = rest[: radix - 1]
-    gated_ref, ggate_ref, small_ref, gconv_ref, gproj_ref = rest[-22:-17]
+    both_ref, small_ref, gconv_ref, gproj_ref = rest[-21:-17]
     (
         proj_ref, in_ref, out_ref, long_ref, true_ref, drive_ref, source_ref,
         start_ref, last_ref, hidden_ref, in_acc, out_acc, scan_ref, gstep_ref, mix_ref, log_ref, dec_ref,
@@ -417,9 +417,9 @@
         sigma = sigmoid(gate)
         skip = bias_ref[SKIP : SKIP + 1, at]
         scan_out = scan_ref[group] + skip * conv
-        gated_ref[:, at] = (scan_out * gate * sigma).astype(jnp.bfloat16)
+        both_ref[:length, at] = (scan_out * gate * sigma).astype(jnp.bfloat16)
         ggate = gg * scan_out * sigma * (1.0 + gate * (1.0 - sigma))
-        ggate_ref[:, at] = ggate.astype(jnp.bfloat16)
+        both_ref[length:, at] = ggate.astype(jnp.bfloat16)
         gconv_ref[:, at] = source * skip + mix * step
         gpre = (gstep_ref[group] * LN2 + mix * conv) * sigmoid(step_pre[:, at])
         gpre_low = gpre.astype(jnp.bfloat16)
@@ -496,9 +496,9 @@
         functools.partial(scan_kernel, rank, states, members),
         in_specs=[pl.BlockSpec(memory_space=pltpu.SMEM)] + [vmem] * (12 + len(far))
         + [pl.BlockSpec(memory_space=pl.ANY) for _ in deps],
-        out_specs=[vmem] * 5,
+        out_specs=[vmem] * 4,
         out_shape=[
-            jax.ShapeDtypeStruct((length, width), bf16), jax.ShapeDtypeStruct((length, width), bf16),
+            jax.ShapeDtypeStruct((2 * length, width), bf16),
             jax.ShapeDtypeStruct((padded(rank + states + 2, 8), width), f32),
             jax.ShapeDtypeStruct((length, width), f32),
             jax.ShapeDtypeStruct((length, LANES), f32),
@@ -626,11 +626,11 @@
 
 
 def taps_kernel(
-    kernel, ndeps,
-    own_ref, peer_ref, conv_ref, in_ref, ext_ref, weight_ref, gconv_ref, taps_ref, params_ref, masks_ref,
-    *rest,
+    kernel,
+    where_ref, own_ref, peer_ref, conv_ref, in_ref, ext_ref, weight_ref, gconv_ref, taps_ref, params_ref, masks_ref,
+    first_small_ref, main_ref, rim_ref, kept_ref, *rest,
 ):
-    main_ref, rim_ref, small_ref = rest[ndeps:]
+    *sent_refs, small_ref, quarter_ref = rest
     length, total_width = conv_ref.shape
     width = weight_ref.shape[0]
     grad_proj = (own_ref[...] + peer_ref[...]).astype(jnp.bfloat16)
@@ -669,151 +669,130 @@
         lines.append(jnp.sum(grad, axis=0, keepdims=True))
         lines.append(jnp.zeros((small_ref.shape[0] - width - kernel - 1, LANES), jnp.float32))
         small_ref[width:, at] = jnp.concatenate(lines, axis=0)
-
-
-def run_taps(own, peer, conv, conv_in, ext, weight, gconv, taps, stacked, masks, deps):
+    small = jnp.concatenate([first_small_ref[...], small_ref[...]], axis=0)
+    count, rows = kept_ref.shape[0], small.shape[0] // PLANE
+    for quarter in range(PLANE):
+        quarter_ref[quarter, :rows, :] = small[quarter * rows : (quarter + 1) * rows]
+        quarter_ref[quarter, rows:, :] = jnp.zeros((count - rows, total_width), jnp.float32)
+    place = where_ref[0] % PLANE
+    kept_ref[...] = quarter_ref[place]
+    for mask, sent_ref in enumerate(sent_refs, 1):
+        sent_ref[...] = quarter_ref[jnp.bitwise_xor(place, mask)].astype(jnp.bfloat16)
+
+
+def run_taps(where, own, peer, conv, conv_in, ext, weight, gconv, taps, stacked, masks, first_small):
     length, width = conv.shape
     kernel = taps.shape[0]
     f32 = jnp.float32
     vmem = pl.BlockSpec(memory_space=pltpu.VMEM)
-    return pl.pallas_call(
-        functools.partial(taps_kernel, kernel, len(deps)),
-        in_specs=[vmem] * 10 + [pl.BlockSpec(memory_space=pl.ANY) for _ in deps],
-        out_specs=[vmem] * 3,
+    tall = padded(weight.shape[0] + kernel + 1, 8)
+    count = padded((first_small.shape[0] + tall) // PLANE, 8)
+    return pl.pallas_call(
+        functools.partial(taps_kernel, kernel),
+        in_specs=[pl.BlockSpec(memory_space=pltpu.SMEM)] + [vmem] * 11, out_specs=[vmem] * (2 + PLANE),
         out_shape=[
-            jax.ShapeDtypeStruct((length, width), f32),
-            jax.ShapeDtypeStruct((CHUNKS, width), f32),
-            jax.ShapeDtypeStruct((padded(weight.shape[0] + kernel + 2, 8), width), f32),
-        ],
+            jax.ShapeDtypeStruct((length, width), f32), jax.ShapeDtypeStruct((CHUNKS, width), f32),
+            jax.ShapeDtypeStruct((count, width), f32),
+        ] + [jax.ShapeDtypeStruct((count, width), jnp.bfloat16)] * (PLANE - 1),
+        scratch_shapes=[pltpu.VMEM((tall, width), f32), pltpu.VMEM((PLANE, count, width), f32)],
         compiler_params=params(), cost_estimate=cost(4), name="taps",
-    )(own, peer, conv, conv_in, ext, weight, gconv, taps, stacked, masks, *deps)
-
-
-def inputs_kernel(
-    gain_row, ndeps, where_ref, main_ref, rim_ref, weight_ref, gate_part_ref, tokens_ref,
-    first_small_ref, second_small_ref, *rest,
-):
-    x_first_ref, x_second_ref, y_first_ref, y_second_ref, own_ref, normed_ref, small_ref = rest[ndeps:]
-    bf16 = jnp.bfloat16
+    )(where, own, peer, conv, conv_in, ext, weight, gconv, taps, stacked, masks, first_small)
+
+
+def inputs_kernel(ndeps, main_ref, rim_ref, weight_ref, both_ref, gate_weight_ref, tokens_ref, *rest):
+    low_ref, normed_ref = rest[ndeps:]
     length, width = main_ref.shape
-    half = length // 2
     main = main_ref[...]
     low = jnp.concatenate(
         [main[: length - CHUNKS], main[length - CHUNKS :] + rim_ref[...]], axis=0
-    ).astype(bf16)
-    normed = dot(low, weight_ref[...], ((1,), (1,))) + gate_part_ref[...]
+    ).astype(jnp.bfloat16)
+    normed = dot(both_ref[length:, :], gate_weight_ref[...], ((1,), (1,)))
+    normed = normed + dot(low, weight_ref[...], ((1,), (1,)))
     normed_ref[...] = normed
     tokens = tokens_ref[...].astype(jnp.float32)
     gain = jnp.sum(normed * tokens * inverse_rms(tokens), axis=0, keepdims=True)
-    second = second_small_ref[...]
-    number = lax.broadcasted_iota(jnp.int32, second.shape, 0)
-    second = jnp.where(number == gain_row, gain, second)
-    small = jnp.concatenate([first_small_ref[...], second], axis=0)
-    count = small_ref.shape[1]
-    blank = jnp.zeros((PLANE * count - small.shape[0], width), jnp.float32)
-    small = jnp.concatenate([small, blank], axis=0)
-    for quarter in range(PLANE):
-        small_ref[quarter] = small[quarter * count : (quarter + 1) * count]
-    place = where_ref[0] % PLANE
-    own_ref[...] = small_ref[place]
-    across = small_ref[jnp.bitwise_xor(place, 3)].astype(bf16)
-    x_first_ref[...] = jnp.concatenate([low[:half], across], axis=0)
-    x_second_ref[...] = jnp.concatenate([low[half:], small_ref[jnp.bitwise_xor(place, 1)].astype(bf16)], axis=0)
-    y_first_ref[...] = jnp.concatenate([low[:half], small_ref[jnp.bitwise_xor(place, 2)].astype(bf16)], axis=0)
-    y_second_ref[...] = low[half:]
-
-
-def run_inputs(gain_row, where, main, rim, weight, gate_part, tokens, first_small, second_small, deps):
+    low_ref[:length, :] = low
+    low_ref[length:, :] = two_rows(gain)
+
+
+def run_inputs(main, rim, weight, both, gate_weight, tokens, deps):
     length, width = main.shape
-    f32, bf16 = jnp.float32, jnp.bfloat16
-    vmem = pl.BlockSpec(memory_space=pltpu.VMEM)
-    count = padded(first_small.shape[0] + second_small.shape[0], 8 * PLANE) // PLANE
-    tall = jax.ShapeDtypeStruct((length // 2 + count, width), bf16)
-    return pl.pallas_call(
-        functools.partial(inputs_kernel, gain_row, len(deps)),
-        in_specs=[pl.BlockSpec(memory_space=pltpu.SMEM)] + [vmem] * 7
-        + [pl.BlockSpec(memory_space=pl.ANY) for _ in deps],
-        out_specs=[vmem] * 6,
+    vmem = pl.BlockSpec(memory_space=pltpu.VMEM)
+    return pl.pallas_call(
+        functools.partial(inputs_kernel, len(deps)),
+        in_specs=[vmem] * 6 + [pl.BlockSpec(memory_space=pl.ANY) for _ in deps], out_specs=[vmem] * 2,
         out_shape=[
-            tall, tall, tall, jax.ShapeDtypeStruct((length // 2, width), bf16),
-            jax.ShapeDtypeStruct((count, width), f32),
-            jax.ShapeDtypeStruct((length, weight.shape[0]), f32),
+            jax.ShapeDtypeStruct((length + 2 * CHUNKS, width), jnp.bfloat16),
+            jax.ShapeDtypeStruct((length, weight.shape[0]), jnp.float32),
         ],
-        scratch_shapes=[pltpu.VMEM((PLANE, count, width), f32)],
         compiler_params=params(), cost_estimate=cost(3), name="inputs",
-    )(where, main, rim, weight, gate_part, tokens, first_small, second_small, *deps)
+    )(main, rim, weight, both, gate_weight, tokens, *deps)
 
 
 def products_kernel(halves, members, ndeps, where_ref, *rest):
-    early = rest[:PLANE]
-    late = rest[PLANE : 3 * PLANE]
-    small = len(halves) == 1
-    if small:
-        own_ref = rest[3 * PLANE]
-        rest = rest[1:]
-    kept_ref, *small_refs, sent_ref, total_ref = rest[3 * PLANE + ndeps :]
+    early, rest = rest[:PLANE], rest[PLANE:]
+    late, rest = list(rest[: 2 + len(halves) + 1]), rest[2 + len(halves) + 1 :]
     lines = members // PLANE
     share, length = early[0].shape[0] // 2, early[0].shape[1]
     rows = share // lines
+    apart = late[0].shape[0] == len(halves) * length
+    if apart:
+        small, rest = rest[:PLANE], rest[PLANE:]
+    kept_ref, small_ref, sent_ref, total_ref = rest[ndeps:]
     for number, half in enumerate(halves):
         total = None
         for mask in range(PLANE):
-            if small:
-                tops = [late[2 * mask + part][: length // 2, :] for part in range(2)]
-                block = jnp.concatenate(tops, axis=0)
+            if mask == 3 and len(halves) > 1:
+                block = late[mask + number][...]
             else:
-                block = late[2 * mask + number][...]
+                block = late[mask][number * length : (number + 1) * length, :]
             part = dot(early[mask][half * share : (half + 1) * share, :], block, ((1,), (0,)))
             total = part if total is None else total + part
         for line in range(lines):
             total_ref[line, number * rows : (number + 1) * rows, :] = total[line * rows : (line + 1) * rows]
-    line = None
-    if small:
-        line = own_ref[...]
-        for ref in (late[3], late[4], late[6]):
-            line = line + ref[length // 2 :, :].astype(jnp.float32)
-    send(where_ref[0], 0, total_ref, line, kept_ref, small_refs, sent_ref)
-
-
-def send(device, level, total_ref, line, kept_ref, small_refs, sent_ref):
+    if apart:
+        line = small[0][...]
+        for ref in small[1:]:
+            line = line + ref[...].astype(jnp.float32)
+    else:
+        line = sum(
+            jnp.sum(ref[len(halves) * length :, :].astype(jnp.float32), axis=0, keepdims=True) for ref in late
+        )
+        number = lax.broadcasted_iota(jnp.int32, small_ref.shape, 0)
+        line = jnp.where(number == 0, line, 0.0)
+    send(where_ref[0], 0, total_ref, line, kept_ref, small_ref, sent_ref)
+
+
+def send(device, level, total_ref, line, kept_ref, small_ref, sent_ref):
     digit = device // (PLANE << level) % 2
-    pieces = []
-    if line is not None:
-        small_refs[0][...] = line
-        pieces.append(line)
+    small_ref[...] = line
+    pieces = [line]
     for block in range(total_ref.shape[0] // 2):
         kept_ref[block] = total_ref[2 * block + digit]
         pieces.append(total_ref[2 * block + 1 - digit])
     sent_ref[...] = jnp.concatenate(pieces, axis=0).astype(jnp.bfloat16)
 
 
-def gather_kernel(level, count, small, ndeps, where_ref, kept_ref, *refs):
+def gather_kernel(level, count, ndeps, where_ref, kept_ref, small_ref, got_ref, *refs):
+    refs = refs[ndeps:]
     total = kept_ref[...]
-    line = None
-    first = 0
-    if small:
-        first = refs[0].shape[0]
-        line = refs[0][...] + refs[1][:first, :].astype(jnp.float32)
-        refs = refs[1:]
-    got = refs[0][first:, :].astype(jnp.float32)
-    refs = refs[1 + ndeps :]
+    got = got_ref[...].astype(jnp.float32)
+    first = small_ref.shape[0]
+    line = small_ref[...] + got[:first]
     left, rows, width = total.shape
-    pieces = [total[index] + got[index * rows : (index + 1) * rows] for index in range(left)]
+    pieces = [total[index] + got[first + index * rows : first + (index + 1) * rows] for index in range(left)]
     if left > 1:
         total_ref = refs[-1]
         for index, piece in enumerate(pieces):
             total_ref[index] = piece
-        send(where_ref[0], level + 1, total_ref, line, refs[0], refs[1:-2], refs[-2])
+        send(where_ref[0], level + 1, total_ref, line, *refs[:-1])
         return
     for index in range(count):
         refs[index][...] = pieces[0][index * (rows // count) : (index + 1) * (rows // count)]
-    if small:
-        refs[count][...] = line.astype(jnp.bfloat16)
-
-
-def gather_plane(first, second, x_first, x_second, y_first, y_second):
-    near = [first, second, hop(x_first, 1), hop(x_second, 1), hop(y_first, 2), hop(y_second, 2)]
-    return near + [hop(near[2], 2), hop(near[5], 1)]
+    if len(refs[count].shape) == 1:
+        refs[count][...] = line[:1].reshape(width)
+    else:
+        refs[count][...] = line.astype(refs[count].dtype)
 
 
 def multiply(halves, where, early, late, small, deps):
@@ -822,89 +801,106 @@
     width = late[0].shape[1]
     rows = len(halves) * (early[0].shape[0] // 2 // lines)
     vmem = pl.BlockSpec(memory_space=pltpu.VMEM)
-    out_shape = level_shapes(lines, rows, width, small)
-    extra = [] if small is None else [small]
+    count = small[0].shape[0] if small else 2 * CHUNKS
+    out_shape = level_shapes(lines, rows, count, width)
     return pl.pallas_call(
         functools.partial(products_kernel, halves, members, len(deps)),
-        in_specs=[pl.BlockSpec(memory_space=pltpu.SMEM)] + [vmem] * (3 * PLANE + len(extra))
+        in_specs=[pl.BlockSpec(memory_space=pltpu.SMEM)] + [vmem] * (PLANE + len(late) + len(small))
         + [pl.BlockSpec(memory_space=pl.ANY) for _ in deps],
         out_specs=[vmem] * len(out_shape), out_shape=out_shape,
         scratch_shapes=[pltpu.VMEM((lines, rows, width), jnp.float32)],
         compiler_params=params(), cost_estimate=cost(4), name="products",
-    )(where, *early, *late, *extra, *deps)
-
-
-def level_shapes(left, rows, width, small):
-    kept = jax.ShapeDtypeStruct((left // 2, rows, width), jnp.float32)
-    if small is None:
-        return [kept, jax.ShapeDtypeStruct((left // 2 * rows, width), jnp.bfloat16)]
-    sent = jax.ShapeDtypeStruct((small.shape[0] + left // 2 * rows, width), jnp.bfloat16)
-    return [kept, jax.ShapeDtypeStruct(small.shape, jnp.float32), sent]
-
-
-def add_line(level, where, parts, count, deps=()):
-    f32, bf16 = jnp.float32, jnp.bfloat16
-    kept, *small, sent = parts
+    )(where, *early, *late, *small, *deps)
+
+
+def level_shapes(left, rows, count, width):
+    return [
+        jax.ShapeDtypeStruct((left // 2, rows, width), jnp.float32),
+        jax.ShapeDtypeStruct((count, width), jnp.float32),
+        jax.ShapeDtypeStruct((count + left // 2 * rows, width), jnp.bfloat16),
+    ]
+
+
+def add_line(level, where, parts, number, deps=()):
+    f32 = jnp.float32
+    kept, small, sent = parts
     vmem = pl.BlockSpec(memory_space=pltpu.VMEM)
     got = hop(sent, PLANE << level)
     left, rows, width = kept.shape
+    count = small.shape[0]
     scratch = []
     if left > 1:
-        out_shape = level_shapes(left, rows, width, small[0] if small else None)
+        out_shape = level_shapes(left, rows, count, width)
         scratch = [pltpu.VMEM((left, rows, width), f32)]
     else:
-        out_shape = [jax.ShapeDtypeStruct((rows // count, width), f32)] * count
-        out_shape = out_shape + [jax.ShapeDtypeStruct(one.shape, bf16) for one in small]
-    return pl.pallas_call(
-        functools.partial(gather_kernel, level, count, bool(small), len(deps)),
-        in_specs=[pl.BlockSpec(memory_space=pltpu.SMEM)] + [vmem] * (2 + len(small))
+        out_shape = [jax.ShapeDtypeStruct((rows // number, width), f32)] * number
+        single = count == 2 * CHUNKS
+        out_shape.append(
+            jax.ShapeDtypeStruct((width,), f32) if single else jax.ShapeDtypeStruct(small.shape, jnp.bfloat16)
+        )
+    return pl.pallas_call(
+        functools.partial(gather_kernel, level, number, len(deps)),
+        in_specs=[pl.BlockSpec(memory_space=pltpu.SMEM)] + [vmem] * 3
         + [pl.BlockSpec(memory_space=pl.ANY) for _ in deps],
         out_specs=[vmem] * len(out_shape), out_shape=out_shape, scratch_shapes=scratch,
         compiler_params=params(), cost_estimate=cost(2), name="gather",
-    )(where, kept, *small, got, *deps)
-
-
-def project_kernel(gated_ref, ggate_ref, out_w_ref, gate_w_ref, branch_ref, part_ref):
-    branch_ref[...] = dot(gated_ref[...], out_w_ref[...], ((1,), (0,)))
-    part_ref[...] = dot(ggate_ref[...], gate_w_ref[...], ((1,), (1,)))
-
-
-def run_project(gated, ggate, out_w, gate_w):
-    length = gated.shape[0]
-    width, model = out_w.shape
-    out = jax.ShapeDtypeStruct((length, model), jnp.float32)
-    vmem = pl.BlockSpec(memory_space=pltpu.VMEM)
-    return pl.pallas_call(
-        project_kernel, in_specs=[vmem] * 4, out_specs=[vmem] * 2, out_shape=[out, out],
-        compiler_params=params(), cost_estimate=cost(5), name="project",
-    )(gated, ggate, out_w, gate_w)
-
-
-def place_kernel(counts, where_ref, *refs):
+    )(where, kept, small, got, *deps)
+
+
+def branch_kernel(both_ref, weight_ref, _, branch_ref):
+    branch_ref[...] = dot(both_ref[: branch_ref.shape[0], :], weight_ref[...], ((1,), (0,)))
+
+
+def run_branch(both, weight, dep):
+    vmem = pl.BlockSpec(memory_space=pltpu.VMEM)
+    return pl.pallas_call(
+        branch_kernel, in_specs=[vmem, vmem, pl.BlockSpec(memory_space=pl.ANY)], out_specs=vmem,
+        out_shape=jax.ShapeDtypeStruct((both.shape[0] // 2, weight.shape[1]), jnp.float32),
+        compiler_params=params(), cost_estimate=cost(5), name="branch",
+    )(both, weight, dep)
+
+
+def place_kernel(rows, counts, where_ref, *refs):
     quarters, outs, (table_ref,) = refs[:PLANE], refs[PLANE:-1], refs[-1:]
     place = where_ref[0] % PLANE
     for mask, ref in enumerate(quarters):
         table_ref[jnp.bitwise_xor(place, mask)] = ref[...].astype(jnp.float32)
-    table = jnp.concatenate([table_ref[quarter] for quarter in range(PLANE)], axis=0)
+    table = jnp.concatenate([table_ref[quarter, :rows, :] for quarter in range(PLANE)], axis=0)
     for out, (first, count) in zip(outs, counts, strict=True):
         value = table[first : first + count]
         out[...] = value.reshape(value.shape[1]) if count == 1 else value
 
 
-def run_place(where, own, counts):
+def run_place(where, own, rows, counts):
     count, width = own.shape
     f32 = jnp.float32
-    x, y = hop(own, 1), hop(own, 2)
     vmem = pl.BlockSpec(memory_space=pltpu.VMEM)
     shapes = [(width,) if number == 1 else (number, width) for _, number in counts]
     return pl.pallas_call(
-        functools.partial(place_kernel, counts),
+        functools.partial(place_kernel, rows, counts),
         in_specs=[pl.BlockSpec(memory_space=pltpu.SMEM)] + [vmem] * PLANE,
         out_specs=[vmem] * len(shapes),
         out_shape=[jax.ShapeDtypeStruct(shape, f32) for shape in shapes],
         scratch_shapes=[pltpu.VMEM((PLANE, count, width), f32)],
         compiler_params=params(), cost_estimate=cost(3), name="place",
-    )(where, own, x, y, hop(x, 2))
+    )(where, own, hop(own, 1), hop(own, 2), hop(own, 3))
+
+
+def relay_kernel(x_ref, y_ref, *rest):
+    from_x_ref, from_y_ref = rest[-2:]
+    length = from_x_ref.shape[0]
+    from_x_ref[...] = x_ref[:length, :]
+    from_y_ref[...] = y_ref[length:, :]
+
+
+def run_relay(x, y, deps):
+    vmem = pl.BlockSpec(memory_space=pltpu.VMEM)
+    half = jax.ShapeDtypeStruct((x.shape[0] // 2, x.shape[1]), x.dtype)
+    return pl.pallas_call(
+        relay_kernel, in_specs=[vmem, vmem] + [pl.BlockSpec(memory_space=pl.ANY) for _ in deps],
+        out_specs=[vmem] * 2,
+        out_shape=[half, half], compiler_params=params(), cost_estimate=cost(1), name="relay",
+    )(x, y, *deps)
 
 
 def leave_kernel(tokens_ref, cot_ref, params_ref, branch_ref, branch_peer_ref, own_ref, peer_ref, mixed_ref, grad_ref):
@@ -978,45 +974,51 @@
         early[1:],
     )
     near, far = exchange(where, totals, decay_log)
-    gated, ggate, first_small, grad_conv, low_own = run_scan(
+    both, first_small, grad_conv, low_own = run_scan(
         where, own, peer, step_proj_weight, stacked, decay_log, conv_out, grad_gated, gate_in, masks,
         ends, seeds, near, far, (),
     )
     low_peer = swap(low_own)
-    main, rim, second_small = run_taps(
-        low_own, low_peer, conv_out, conv_in, ext, scan_weight, grad_conv, conv_weight, stacked, masks, (),
+    main, rim, *small = run_taps(
+        where, low_own, low_peer, conv_out, conv_in, ext, scan_weight, grad_conv, conv_weight, stacked,
+        masks, first_small,
     )
     rim = from_behind(rim, "seq", -1)
-    first_late = gather_plane(gated, ggate, gated, ggate, gated, ggate)
-    branch_own, gate_part = run_project(gated, ggate, out_weight, in_gate_weight)
-    *sent_late, small, normed_own = run_inputs(
-        scan_width + kernel + 1, where, main, rim, in_conv_weight, gate_part, tokens, first_small,
-        second_small, first_late[2:6],
-    )
-    second_late = gather_plane(*sent_late[:2], *sent_late)
+    small = small[:1] + [hop(one, mask) for mask, one in enumerate(small[1:], 1)]
+    x, y = hop(both, 1), hop(both, 2)
+    from_x, from_y = run_relay(x, y, (main, rim, *small[1:3]))
+    low, normed_own = run_inputs(
+        main, rim, in_conv_weight, both, in_gate_weight, tokens, (from_x,)
+    )
+    first_late = [both, x, y, hop(from_x, 2), hop(from_y, 1)]
+    second_late = [low] + [hop(low, mask) for mask in range(1, PLANE)]
+    branch_own = run_branch(both, out_weight, normed_own)
     mixed_out, input_grad = run_leave(
         tokens, cotangent, stacked, branch_own, swap(branch_own), normed_own, swap(normed_own)
     )
-    first = multiply((1, 0), where, early, first_late, None, (normed_own,))
-    second = multiply((0,), where, early, second_late, small, first[:1])
-    lines = members // PLANE
-    for level in range(lines.bit_length() - 1):
-        first = add_line(level, where, first, 2, () if level == 0 else ())
-        second = add_line(level, where, second, 1, () if level == 0 else ())
-    out_grad, in_gate_grad = first
-    in_conv_grad, small = second
+    count = (members // PLANE).bit_length() - 1
+    first = multiply((1, 0), where, early, first_late, small, (normed_own,))
+    first = add_line(0, where, first, 2)
+    second = multiply((0,), where, early, second_late, [], first[:1])
+    for level in range(1, count):
+        first = add_line(level, where, first, 2)
+    out_grad, in_gate_grad, small = first
+    second = add_line(0, where, second, 1, (out_grad,))
     first_row = first_small.shape[0]
     last_row = first_row + scan_width
     (
         step_proj_grad, decay_log_grad, step_bias_grad, skip_grad, scan_proj_grad, conv_weight_grad,
-        conv_bias_grad, gain_grad,
+        conv_bias_grad,
     ) = run_place(
-        where, small,
+        where, small, (first_row + padded(scan_width + kernel + 1, 8)) // PLANE,
         (
             (0, rank), (rank, states), (rank + states, 1), (rank + states + 1, 1), (first_row, scan_width),
-            (last_row, kernel), (last_row + kernel, 1), (last_row + kernel + 1, 1),
+            (last_row, kernel), (last_row + kernel, 1),
         ),
     )
+    for level in range(1, count):
+        second = add_line(level, where, second, 1, (input_grad, step_proj_grad))
+    in_conv_grad, gain_grad = second
     gain_grad = gain_grad + swap(gain_grad)
     return (
         mixed_out, input_grad, gain_grad, in_conv_grad, in_gate_grad, conv_weight_grad,

time: 174 us -> 165 us (0.948)
  waiting for transfers between devices: 54.1 us -> 48.1 us
  starting transfers between devices: 43.4 us -> 39.6 us
  Pallas kernels: 69.1 us -> 71.1 us
    ppermute x28 -> x26, waiting for transfers between devices: 50.9 us -> 39.6 us  [hop(): return lax.ppermute(block, 'seq', [(i, i ^ mask) for i in range(members)])]
    ppermute x2, waiting for transfers between devices: 0.01 us -> 3.92 us  [from_behind(): return lax.ppermute(block, axis, route)]
    ppermute x28 -> x26, starting transfers between devices: 36.4 us -> 33.1 us  [hop(): return lax.ppermute(block, 'seq', [(i, i ^ mask) for i in range(members)])]
    pallas_call x8 -> x9, Pallas kernels: 24.5 us -> 26.4 us  [the longest x4 9.28 us: add_line(): pl.pallas_call(functools.partial(gather_kernel, level, number, len(deps))...]
  transfers between devices with their start and end apart: 35 -> 33, of which waited for: 17 -> 16; matrix products, arithmetic and copies ran while one was open for 1% -> 1% of each run, Pallas kernels for 20% -> 22%
where the time goes in v3:
time: 165 us; the launch traced here: 163 us
  Pallas kernels  71.1 us (43%)
  waiting for transfers between devices  48.1 us (29%)
  starting transfers between devices  39.6 us (24%)
  other arithmetic  2.68 us (2%)
    ppermute x26, waiting for transfers between devices, hop(): return lax.ppermute(block, 'seq', [(i, i ^ mask) for i in range(members)])  39.6 us
    ppermute x26, starting transfers between devices, hop(): return lax.ppermute(block, 'seq', [(i, i ^ mask) for i in range(members)])  33.1 us
    pallas_call x1, Pallas kernels, run_scan(): pl.pallas_call(functools.partial(scan_kernel, rank, states, members), in_...  14.3 us
    pallas_call x4, Pallas kernels, add_line(): pl.pallas_call(functools.partial(gather_kernel, level, number, len(deps))...  9.28 us
    pallas_call x2, Pallas kernels, multiply(): pl.pallas_call(functools.partial(products_kernel, halves, members, len(de...  8.9 us
    pallas_call x1, Pallas kernels, run_enter(): pl.pallas_call(functools.partial(enter_kernel, taps.shape[0], weight.shap...  7.13 us
    pallas_call x1, Pallas kernels, run_ends(): pl.pallas_call(functools.partial(ends_kernel, rank, states, len(deps)), i...  7.08 us
    ppermute x2, starting transfers between devices, from_behind(): return lax.ppermute(block, axis, route)  6.42 us
  transfers between devices with their start and end apart: 33, of which 16 were waited for; matrix products, arithmetic and copies ran while one was open for 1% of the time, Pallas kernels for 22%

profile of v3, /device:TPU:8, one launch (start us, length us, event | category | flops | bytes accessed | tf_op | source)
XLA Modules:
  0.0 163.2 jit_solution(2570821342394213822)
XLA Ops:
  0.6 0.6 pad_add_fusion.where_ref
  1.3 2.3 %early.1 = (bf16[128,1152]{1,0:T(8,128)(2,1)}, bf16[8,1152]{1,0:T(8,128)(2,1)}, bf16[576,128]{1,0:T(8,128)(2,1)}, bf16[576,128]{1,0:T(8,128)(2,1)}, bf16[576,128]{1,0:T(8,128)(2,1)}, /*index=5*/bf16[576,128]{1,0:T(8,128)(2,1)}) custom-call(s32[2]{0:T(128)} %pad_add_fusion.where_ref, bf16[128,1152]{1,0:T(8,128)(2,1)} %tokens_ref.5, ...), custom_call_target="tpu_custom_call" | custom-call | bytes 9000000 | tf_op jit(solution)/shard_map/early/pallas_call | solution.py:209
  3.6 3.4 %collective-permute-start = (bf16[8,1152]{1,0:T(8,128)(2,1)}, bf16[8,1152]{1,0:T(8,128)(2,1)}, u32[]{:S(2)}, u32[]{:S(2)}) collective-permute-start(bf16[8,1152]{1,0:T(8,128)(2,1)} %get-tuple-element.74), channel_id=1, source_target_pairs={{0,2},{2,4},{4,6},{6,8},{8,10},{10,12},{12,14},{14,16},{16,18},{18... | collective-permute-start | bytes 55304 | tf_op jit(solution)/shard_map/ppermute | solution.py:931
  7.0 1.6 collective-permute-start.2
  8.5 1.5 collective-permute-start.3
  10.0 0.5 collective-permute-start.4
  10.5 0.8 pad_dynamic-slice_fusion
  11.4 0.7 add_convert_fusion.masks_ref
  12.1 7.1 %enter.1 = (bf16[128,1152]{1,0:T(8,128)(2,1)}, f32[8,1152]{1,0:T(8,128)}, bf16[128,1152]{1,0:T(8,128)(2,1)}, f32[128,1152]{1,0:T(8,128)}, f32[128,1152]{1,0:T(8,...) custom-call(bf16[128,1152]{1,0:T(8,128)(2,1)} %get-tuple-element.73.normed_ref, ...), custom_call_target="tpu_custom_call" | custom-call | bytes 18000000 | tf_op jit(solution)/shard_map/enter/pallas_call | solution.py:150
  19.3 1.6 collective-permute-done.1.peer_ref
  20.9 7.1 %ends.1 = (f32[128,1152]{1,0:T(8,128)}, f32[128,1152]{1,0:T(8,128)}, bf16[48,1152]{1,0:T(8,128)(2,1)}) custom-call(f32[128,128]{1,0:T(8,128)} %get-tuple-element.76.own_ref, f32[128,128]{1,0:T(8,128)} %collective-permute-done.1.peer_ref, bf16[72,1152]{1,0:T(8,128)(2,1)} %weight_ref.5, f32[4,1152]{1,0:T(4,128)} %get-tuple-element.75.bias_ref.params_ref, ...), custom_call_target="tpu_custom_call" | custom-call | bytes 24000000 | tf_op jit(solution)/shard_map/ends/pallas_call | solution.py:468
  28.0 1.5 collective-permute-start.5
  29.5 1.5 collective-permute-start.6
  31.0 0.5 collective-permute-start.7
  31.5 1.9 %collective-permute-done.5.refs_1_ = bf16[48,1152]{1,0:T(8,128)(2,1)} collective-permute-done((bf16[48,1152]{1,0:T(8,128)(2,1)}, bf16[48,1152]{1,0:T(8,128)(2,1)}, u32[]{:S(2)}, u32[]{:S(2)}) %collective-permute-start.5) | collective-permute-done | bytes 110624 | tf_op jit(solution)/shard_map/ppermute | solution.py:940
  33.4 2.8 %collective-permute-done.6.refs_2_ = bf16[48,1152]{1,0:T(8,128)(2,1)} collective-permute-done((bf16[48,1152]{1,0:T(8,128)(2,1)}, bf16[48,1152]{1,0:T(8,128)(2,1)}, u32[]{:S(2)}, u32[]{:S(2)}) %collective-permute-start.6) | collective-permute-done | bytes 110624 | tf_op jit(solution)/shard_map/ppermute | solution.py:940
  36.2 0.8 collective-permute-done.7.refs_3_
  37.0 2.1 %fold.1 = (f32[40,1152]{1,0:T(8,128)}, bf16[32,1152]{1,0:T(8,128)(2,1)}, bf16[32,1152]{1,0:T(8,128)(2,1)}, bf16[32,1152]{1,0:T(8,128)(2,1)}) custom-call(s32[2]{0:T(128)} %pad_add_fusion.where_ref, f32[16,1152]{1,0:T(8,128)} %decay_ref.5, bf16[48,1152]{1,0:T(8,128)(2,1)} %get-tuple-element.85.refs_0_, bf16[48,1152]{1,0:T(8,128)(2,1)} %collective-permute-done.5.refs_1_, ...), custom_call_target="tpu_custom_call" | custom-call | bytes 6000000 | tf_op jit(solution)/shard_map/fold/pallas_call | solution.py:607
  39.1 1.5 collective-permute-start.10
  40.7 2.5 %collective-permute-start.8 = (bf16[32,1152]{1,0:T(8,128)(2,1)}, bf16[32,1152]{1,0:T(8,128)(2,1)}, u32[]{:S(2)}, u32[]{:S(2)}) collective-permute-start(bf16[32,1152]{1,0:T(8,128)(2,1)} %get-tuple-element.87), channel_id=1, source_target_pairs={{0,8},{2,10},{4,12},{6,14},{8,0},{10,2},{12,4},{14,6},{16,24},{18,... | collective-permute-start | bytes 221192 | tf_op jit(solution)/shard_map/ppermute | solution.py:940
  43.2 2.6 %collective-permute-done.10.rest_2_ = bf16[32,1152]{1,0:T(8,128)(2,1)} collective-permute-done((bf16[32,1152]{1,0:T(8,128)(2,1)}, bf16[32,1152]{1,0:T(8,128)(2,1)}, u32[]{:S(2)}, u32[]{:S(2)}) %collective-permute-start.10) | collective-permute-done | bytes 73760 | tf_op jit(solution)/shard_map/ppermute | solution.py:940
  45.7 1.4 collective-permute-done.8.rest_0_
  47.1 1.6 collective-permute-done.9.rest_1_
  48.7 14.3 %scan.1 = (bf16[256,1152]{1,0:T(8,128)(2,1)}, f32[96,1152]{1,0:T(8,128)}, f32[128,1152]{1,0:T(8,128)}, f32[128,128]{1,0:T(8,128)}) custom-call(s32[2]{0:T(128)} %pad_add_fusion.where_ref, f32[128,128]{1,0:T(8,128)} %get-tuple-element.76.own_ref, f32[128,128]{1,0:T(8,128)} %collective-permute-done.1.peer_ref, bf16[72,1152]{1,0:T(8,128)(2,1)} %weight_ref.5, ...), custom_call_target="tpu_custom_call" | custom-call | bytes 45000000 | tf_op jit(solution)/shard_map/scan/pallas_call | solution.py:495
  63.0 0.5 collective-permute-start.13
  63.6 1.5 collective-permute-start.14
  65.1 1.6 collective-permute-done.11.peer_ref
  66.7 4.0 %taps.1 = (f32[128,1152]{1,0:T(8,128)}, f32[8,1152]{1,0:T(8,128)}, f32[56,1152]{1,0:T(8,128)}, bf16[56,1152]{1,0:T(8,128)(2,1)}, bf16[56,1152]{1,0:T(8,128)(2,1)}, /*index=5*/bf16[56,1152]{1,0:T(8,128)(2,1)}) custom-call(s32[2]{0:T(128)} %pad_add_fusion.where_ref, f32[128,128]{1,0:T(8,128)} %get-tuple-element.91.own_ref, ...), custom_call_target="tpu_custom_call" | custom-call | bytes 12000000 | tf_op jit(solution)/shard_map/taps/pallas_call | solution.py:690
  70.7 0.4 collective-permute-start.15
  71.1 1.6 collective-permute-start.16
  72.7 3.0 %collective-permute-start.12 = (f32[8,1152]{1,0:T(8,128)}, f32[8,1152]{1,0:T(8,128)}, u32[]{:S(2)}, u32[]{:S(2)}) collective-permute-start(f32[8,1152]{1,0:T(8,128)} %get-tuple-element.97), channel_id=1, source_target_pairs={{2,0},{4,2},{6,4},{8,6},{10,8},{12,10},{14,12},{16,14},{18,16},{20... | collective-permute-start | bytes 110600 | tf_op jit(solution)/shard_map/ppermute | solution.py:931
  75.8 3.9 %collective-permute-done.12.rest_1_.rim_ref = f32[8,1152]{1,0:T(8,128)} collective-permute-done((f32[8,1152]{1,0:T(8,128)}, f32[8,1152]{1,0:T(8,128)}, u32[]{:S(2)}, u32[]{:S(2)}) %collective-permute-start.12) | collective-permute-done | bytes 36896 | tf_op jit(solution)/shard_map/ppermute | solution.py:931
  79.7 2.1 %relay.1 = (bf16[128,1152]{1,0:T(8,128)(2,1)}, bf16[128,1152]{1,0:T(8,128)(2,1)}) custom-call(bf16[256,1152]{1,0:T(8,128)(2,1)} %collective-permute-done.13.x_ref.rest_5_, bf16[256,1152]{1,0:T(8,128)(2,1)} %collective-permute-done.14.y_ref.rest_6_, f32[128,1152]{1,0:T(8,128)} %get-tuple-element.96.rest_0_.main_ref, ...), custom_call_target="tpu_custom_call" | custom-call | bytes 3000000 | tf_op jit(solution)/shard_map/relay/pallas_call | solution.py:899
  81.8 0.8 collective-permute-start.22
  82.6 2.3 %collective-permute-start.23 = (bf16[128,1152]{1,0:T(8,128)(2,1)}, bf16[128,1152]{1,0:T(8,128)(2,1)}, u32[]{:S(2)}, u32[]{:S(2)}) collective-permute-start(bf16[128,1152]{1,0:T(8,128)(2,1)} %get-tuple-element.106), channel_id=1, source_target_pairs={{0,2},{2,0},{4,6},{6,4},{8,10},{10,8},{12,14},{14,12},{16,18},{18,... | collective-permute-start | bytes 884744 | tf_op jit(solution)/shard_map/ppermute | solution.py:940
  84.9 0.4 collective-permute-start.24
  85.3 5.6 %inputs.1 = (bf16[144,1152]{1,0:T(8,128)(2,1)}, f32[128,1152]{1,0:T(8,128)}) custom-call(f32[128,1152]{1,0:T(8,128)} %get-tuple-element.96.rest_0_.main_ref, f32[8,1152]{1,0:T(8,128)} %collective-permute-done.12.rest_1_.rim_ref, bf16[1152,1152]{1,0:T(8,128)(2,1)} %weight_ref.6, bf16[256,1152]{1,0:T(8,128)(2,1)} %get-tuple-element.90.both_ref.rest_4_, ...), custom_call_target="tpu_custom_call" | custom-call | bytes 9000000 | tf_op jit(solution)/shard_map/inputs/pallas_call | solution.py:721
  90.8 2.5 %collective-permute-done.24.rest_12_ = bf16[56,1152]{1,0:T(8,128)(2,1)} collective-permute-done((bf16[56,1152]{1,0:T(8,128)(2,1)}, bf16[56,1152]{1,0:T(8,128)(2,1)}, u32[]{:S(2)}, u32[]{:S(2)}) %collective-permute-start.24) | collective-permute-done | bytes 129056 | tf_op jit(solution)/shard_map/ppermute | solution.py:940
  93.4 5.4 %products.2 = (f32[2,144,1152]{2,1,0:T(8,128)}, f32[56,1152]{1,0:T(8,128)}, bf16[344,1152]{1,0:T(8,128)(2,1)}) custom-call(s32[2]{0:T(128)} %pad_add_fusion.where_ref, bf16[576,128]{1,0:T(8,128)(2,1)} %get-tuple-element.104.rest_0_, bf16[576,128]{1,0:T(8,128)(2,1)} %collective-permute-done.2.rest_0_.rest_1_, ...), custom_call_target="tpu_custom_call" | custom-call | bytes 12000000 | tf_op jit(solution)/shard_map/products/pallas_call | solution.py:806
  98.7 1.2 collective-permute-start.25
  100.0 1.0 collective-permute-start.19
  100.9 1.1 collective-permute-start.20
  102.0 1.4 collective-permute-start.21
  103.4 3.4 %branch.1.branch_ref = f32[128,1152]{1,0:T(8,128)} custom-call(bf16[256,1152]{1,0:T(8,128)(2,1)} %get-tuple-element.90.both_ref.rest_4_, bf16[1152,1152]{1,0:T(8,128)(2,1)} %weight_ref.7, f32[128,1152]{1,0:T(8,128)} %get-tuple-element.101._.own_ref.rest_13_), custom_call_target="tpu_custom_call" | custom-call | bytes 15000000 | tf_op jit(solution)/shard_map/branch/pallas_call | solution.py:856
  106.8 8.7 %collective-permute-done.25.got_ref = bf16[344,1152]{1,0:T(8,128)(2,1)} collective-permute-done((bf16[344,1152]{1,0:T(8,128)(2,1)}, bf16[344,1152]{1,0:T(8,128)(2,1)}, u32[]{:S(2)}, u32[]{:S(2)}) %collective-permute-start.25) | collective-permute-done | bytes 792608 | tf_op jit(solution)/shard_map/ppermute | solution.py:940
  115.5 3.0 %gather.4 = (f32[1,144,1152]{2,1,0:T(8,128)}, f32[56,1152]{1,0:T(8,128)}, bf16[200,1152]{1,0:T(8,128)(2,1)}) custom-call(s32[2]{0:T(128)} %pad_add_fusion.where_ref, f32[2,144,1152]{2,1,0:T(8,128)} %get-tuple-element.109.kept_ref, f32[56,1152]{1,0:T(8,128)} %get-tuple-element.110.small_ref, bf16[344,1152]{1,0:T(8,128)(2,1)} %collective-permute-done.25.got_ref), custom_call_target="tpu_custom_call" | custom-call | bytes 6000000 | tf_op jit(solution)/shard_map/gather/pallas_call | solution.py:841
  118.5 2.1 %collective-permute-start.27 = (bf16[200,1152]{1,0:T(8,128)(2,1)}, bf16[200,1152]{1,0:T(8,128)(2,1)}, u32[]{:S(2)}, u32[]{:S(2)}) collective-permute-start(bf16[200,1152]{1,0:T(8,128)(2,1)} %get-tuple-element.117), channel_id=1, source_target_pairs={{0,16},{2,18},{4,20},{6,22},{8,24},{10,26},{12,28},{14,30},{16,0},... | collective-permute-start | bytes 1382408 | tf_op jit(solution)/shard_map/ppermute | solution.py:940
  120.7 3.5 %products.3 = (f32[2,72,1152]{2,1,0:T(8,128)}, f32[16,1152]{1,0:T(8,128)}, bf16[160,1152]{1,0:T(8,128)(2,1)}) custom-call(s32[2]{0:T(128)} %pad_add_fusion.where_ref, bf16[576,128]{1,0:T(8,128)(2,1)} %get-tuple-element.104.rest_0_, bf16[576,128]{1,0:T(8,128)(2,1)} %collective-permute-done.2.rest_0_.rest_1_, ...), custom_call_target="tpu_custom_call" | custom-call | bytes 12000000 | tf_op jit(solution)/shard_map/products/pallas_call | solution.py:806
  124.2 0.3 collective-permute-start.26
  124.5 11.7 %collective-permute-done.27.got_ref = bf16[200,1152]{1,0:T(8,128)(2,1)} collective-permute-done((bf16[200,1152]{1,0:T(8,128)(2,1)}, bf16[200,1152]{1,0:T(8,128)(2,1)}, u32[]{:S(2)}, u32[]{:S(2)}) %collective-permute-start.27) | collective-permute-done | bytes 460832 | tf_op jit(solution)/shard_map/ppermute | solution.py:940
  136.2 2.3 %gather.5 = (f32[72,1152]{1,0:T(8,128)}, f32[72,1152]{1,0:T(8,128)}, bf16[56,1152]{1,0:T(8,128)(2,1)}) custom-call(s32[2]{0:T(128)} %pad_add_fusion.where_ref, f32[1,144,1152]{2,1,0:T(8,128)} %get-tuple-element.112.rest_8_.kept_ref, f32[56,1152]{1,0:T(8,128)} %get-tuple-element.116.small_ref, bf16[200,1152]{1,0:T(8,128)(2,1)} %collective-permute-done.27.got_ref), custom_call_target="tpu_custom_call" | custom-call | bytes 6000000 | tf_op jit(solution)/shard_map/gather/pallas_call | solution.py:841
  138.5 3.3 %collective-permute-done.26.got_ref = bf16[160,1152]{1,0:T(8,128)(2,1)} collective-permute-done((bf16[160,1152]{1,0:T(8,128)(2,1)}, bf16[160,1152]{1,0:T(8,128)(2,1)}, u32[]{:S(2)}, u32[]{:S(2)}) %collective-permute-start.26) | collective-permute-done | bytes 368672 | tf_op jit(solution)/shard_map/ppermute | solution.py:940
  141.8 2.2 %gather.6 = (f32[1,72,1152]{2,1,0:T(8,128)}, f32[16,1152]{1,0:T(8,128)}, bf16[88,1152]{1,0:T(8,128)(2,1)}) custom-call(s32[2]{0:T(128)} %pad_add_fusion.where_ref, f32[2,72,1152]{2,1,0:T(8,128)} %get-tuple-element.113.kept_ref, f32[16,1152]{1,0:T(8,128)} %get-tuple-element.114.small_ref, bf16[160,1152]{1,0:T(8,128)(2,1)} %collective-permute-done.26.got_ref, ...), custom_call_target="tpu_custom_call" | custom-call | bytes 6000000 | tf_op jit(solution)/shard_map/gather/pallas_call | solution.py:841
  144.0 4.0 %collective-permute-start.28 = (bf16[88,1152]{1,0:T(8,128)(2,1)}, bf16[88,1152]{1,0:T(8,128)(2,1)}, u32[]{:S(2)}, u32[]{:S(2)}) collective-permute-start(bf16[88,1152]{1,0:T(8,128)(2,1)} %get-tuple-element.121), channel_id=1, source_target_pairs={{0,16},{2,18},{4,20},{6,22},{8,24},{10,26},{12,28},{14,30},{16,0},... | collective-permute-start | bytes 608264 | tf_op jit(solution)/shard_map/ppermute | solution.py:940
  147.9 0.4 collective-permute-start.29
  148.3 2.0 %collective-permute-start.30 = (bf16[56,1152]{1,0:T(8,128)(2,1)}, bf16[56,1152]{1,0:T(8,128)(2,1)}, u32[]{:S(2)}, u32[]{:S(2)}) collective-permute-start(bf16[56,1152]{1,0:T(8,128)(2,1)} %get-tuple-element.122.refs_0_), channel_id=1, source_target_pairs={{0,4},{2,6},{4,0},{6,2},{8,12},{10,14},{12,8},{14,10},{16,20},{18,... | collective-permute-start | bytes 387080 | tf_op jit(solution)/shard_map/ppermute | solution.py:940
  150.3 1.1 collective-permute-start.31
  151.4 2.9 %leave.1 = (bf16[128,1152]{1,0:T(8,128)(2,1)}, f32[128,1152]{1,0:T(8,128)}) custom-call(bf16[128,1152]{1,0:T(8,128)(2,1)} %tokens_ref.5, bf16[128,1152]{1,0:T(8,128)(2,1)} %cot_ref.5, f32[4,1152]{1,0:T(4,128)} %get-tuple-element.75.bias_ref.params_ref, f32[128,1152]{1,0:T(8,128)} %branch.1.branch_ref, f32[128,1152]{1,0:T(8,128)} %collective-permute-done.17.branch_peer_ref, ...), custom_call_target="tpu_custom_call" | custom-call | bytes 9000000 | tf_op jit(solution)/shard_map/leave/pallas_call | solution.py:918
  154.3 1.3 collective-permute-done.30.refs_2_
  155.6 0.9 collective-permute-done.31.refs_3_
  156.5 2.1 %place.1 = (f32[72,1152]{1,0:T(8,128)}, f32[16,1152]{1,0:T(8,128)}, f32[1152]{0:T(1024)}, f32[1152]{0:T(1024)}, f32[104,1152]{1,0:T(8,128)}, /*index=5*/f32[4,1152]{1,0:T(4,128)}, f32[1152]{0:T(1024)}) custom-call(s32[2]{0:T(128)} %pad_add_fusion.where_ref, bf16[56,1152]{1,0:T(8,128)(2,1)} %get-tuple-element.122.refs_0_, ...), custom_call_target="tpu_custom_call" | custom-call | bytes 9000000 | tf_op jit(solution)/shard_map/place/pallas_call | solution.py:879
  158.6 1.8 %gather.7 = (f32[72,1152]{1,0:T(8,128)}, f32[1152]{0:T(1024)}) custom-call(s32[2]{0:T(128)} %pad_add_fusion.where_ref, f32[1,72,1152]{2,1,0:T(8,128)} %get-tuple-element.119.kept_ref, f32[16,1152]{1,0:T(8,128)} %get-tuple-element.120.small_ref, bf16[88,1152]{1,0:T(8,128)(2,1)} %collective-permute-done.28.got_ref, f32[128,1152]{1,0:T(8,128)} %get-tuple-element.61.refs_0_, ...), custom_call_target="tpu_custom_call" | custom-call | bytes 6000000 | tf_op jit(solution)/shard_map/gather/pallas_call | solution.py:841
  160.5 1.4 collective-permute-done.32
  161.9 1.3 add.9
  (25 shorter events, 0.3 us)
Async XLA Ops:
  3.6 8.5 %collective-permute-start = (bf16[8,1152]{1,0:T(8,128)(2,1)}, bf16[8,1152]{1,0:T(8,128)(2,1)}, u32[]{:S(2)}, u32[]{:S(2)}) collective-permute-start(bf16[8,1152]{1,0:T(8,128)(2,1)} %get-tuple-element.74), channel_id=1, source_target_pairs={{0,2},{2,4},{4,6},{6,8},{8,10},{10,12},{12,14},{14,16},{16,18},{18... | collective-permute-start | bytes 55304 | tf_op jit(solution)/shard_map/ppermute | solution.py:931
  7.0 13.9 %collective-permute-start.2 = (bf16[576,128]{1,0:T(8,128)(2,1)}, bf16[576,128]{1,0:T(8,128)(2,1)}, u32[]{:S(2)}, u32[]{:S(2)}) collective-permute-start(bf16[576,128]{1,0:T(8,128)(2,1)} %get-tuple-element.80), channel_id=1, source_target_pairs={{0,2},{2,0},{4,6},{6,4},{8,10},{10,8},{12,14},{14,12},{16,18},{18,... | collective-permute-start | bytes 442376 | tf_op jit(solution)/shard_map/ppermute | solution.py:940
  8.5 12.4 %collective-permute-start.3 = (bf16[576,128]{1,0:T(8,128)(2,1)}, bf16[576,128]{1,0:T(8,128)(2,1)}, u32[]{:S(2)}, u32[]{:S(2)}) collective-permute-start(bf16[576,128]{1,0:T(8,128)(2,1)} %get-tuple-element.81), channel_id=1, source_target_pairs={{0,4},{2,6},{4,0},{6,2},{8,12},{10,14},{12,8},{14,10},{16,20},{18,... | collective-permute-start | bytes 442376 | tf_op jit(solution)/shard_map/ppermute | solution.py:940
  10.0 10.9 %collective-permute-start.4 = (bf16[576,128]{1,0:T(8,128)(2,1)}, bf16[576,128]{1,0:T(8,128)(2,1)}, u32[]{:S(2)}, u32[]{:S(2)}) collective-permute-start(bf16[576,128]{1,0:T(8,128)(2,1)} %get-tuple-element.82), channel_id=1, source_target_pairs={{0,6},{2,4},{4,2},{6,0},{8,14},{10,12},{12,10},{14,8},{16,22},{18,... | collective-permute-start | bytes 442376 | tf_op jit(solution)/shard_map/ppermute | solution.py:940
  19.2 1.7 %collective-permute-start.1 = (f32[128,128]{1,0:T(8,128)}, f32[128,128]{1,0:T(8,128)}, u32[]{:S(2)}, u32[]{:S(2)}) collective-permute-start(f32[128,128]{1,0:T(8,128)} %get-tuple-element.76.own_ref), channel_id=1, source_target_pairs={{0,1},{1,0},{2,3},{3,2},{4,5},{5,4},{6,7},{7,6},{8,9},{9,8},{10,11... | collective-permute-start | bytes 196616 | tf_op jit(solution)/shard_map/ppermute | solution.py:935
  28.0 5.4 %collective-permute-start.5 = (bf16[48,1152]{1,0:T(8,128)(2,1)}, bf16[48,1152]{1,0:T(8,128)(2,1)}, u32[]{:S(2)}, u32[]{:S(2)}) collective-permute-start(bf16[48,1152]{1,0:T(8,128)(2,1)} %get-tuple-element.85.refs_0_), channel_id=1, source_target_pairs={{0,2},{2,0},{4,6},{6,4},{8,10},{10,8},{12,14},{14,12},{16,18},{18,... | collective-permute-start | bytes 331784 | tf_op jit(solution)/shard_map/ppermute | solution.py:940
  29.5 6.7 %collective-permute-start.6 = (bf16[48,1152]{1,0:T(8,128)(2,1)}, bf16[48,1152]{1,0:T(8,128)(2,1)}, u32[]{:S(2)}, u32[]{:S(2)}) collective-permute-start(bf16[48,1152]{1,0:T(8,128)(2,1)} %get-tuple-element.85.refs_0_), channel_id=1, source_target_pairs={{0,4},{2,6},{4,0},{6,2},{8,12},{10,14},{12,8},{14,10},{16,20},{18,... | collective-permute-start | bytes 331784 | tf_op jit(solution)/shard_map/ppermute | solution.py:940
  31.0 6.0 %collective-permute-start.7 = (bf16[48,1152]{1,0:T(8,128)(2,1)}, bf16[48,1152]{1,0:T(8,128)(2,1)}, u32[]{:S(2)}, u32[]{:S(2)}) collective-permute-start(bf16[48,1152]{1,0:T(8,128)(2,1)} %get-tuple-element.85.refs_0_), channel_id=1, source_target_pairs={{0,6},{2,4},{4,2},{6,0},{8,14},{10,12},{12,10},{14,8},{16,22},{18,... | collective-permute-start | bytes 331784 | tf_op jit(solution)/shard_map/ppermute | solution.py:940
  39.1 6.6 %collective-permute-start.10 = (bf16[32,1152]{1,0:T(8,128)(2,1)}, bf16[32,1152]{1,0:T(8,128)(2,1)}, u32[]{:S(2)}, u32[]{:S(2)}) collective-permute-start(bf16[32,1152]{1,0:T(8,128)(2,1)} %get-tuple-element.89), channel_id=1, source_target_pairs={{0,24},{2,26},{4,28},{6,30},{8,16},{10,18},{12,20},{14,22},{16,8},... | collective-permute-start | bytes 221192 | tf_op jit(solution)/shard_map/ppermute | solution.py:940
  40.7 6.4 %collective-permute-start.8 = (bf16[32,1152]{1,0:T(8,128)(2,1)}, bf16[32,1152]{1,0:T(8,128)(2,1)}, u32[]{:S(2)}, u32[]{:S(2)}) collective-permute-start(bf16[32,1152]{1,0:T(8,128)(2,1)} %get-tuple-element.87), channel_id=1, source_target_pairs={{0,8},{2,10},{4,12},{6,14},{8,0},{10,2},{12,4},{14,6},{16,24},{18,... | collective-permute-start | bytes 221192 | tf_op jit(solution)/shard_map/ppermute | solution.py:940
  43.1 5.6 %collective-permute-start.9 = (bf16[32,1152]{1,0:T(8,128)(2,1)}, bf16[32,1152]{1,0:T(8,128)(2,1)}, u32[]{:S(2)}, u32[]{:S(2)}) collective-permute-start(bf16[32,1152]{1,0:T(8,128)(2,1)} %get-tuple-element.88), channel_id=1, source_target_pairs={{0,16},{2,18},{4,20},{6,22},{8,24},{10,26},{12,28},{14,30},{16,0},... | collective-permute-start | bytes 221192 | tf_op jit(solution)/shard_map/ppermute | solution.py:940
  63.0 16.7 %collective-permute-start.13 = (bf16[256,1152]{1,0:T(8,128)(2,1)}, bf16[256,1152]{1,0:T(8,128)(2,1)}, u32[]{:S(2)}, u32[]{:S(2)}) collective-permute-start(bf16[256,1152]{1,0:T(8,128)(2,1)} %get-tuple-element.90.both_ref.rest_4_), channel_id=1, source_target_pairs={{0,2},{2,0},{4,6},{6,4},{8,10},{10,8},{12,14},{14,12},{16,18},{18,... | collective-permute-start | bytes 1769480 | tf_op jit(solution)/shard_map/ppermute | solution.py:940
  63.6 16.1 %collective-permute-start.14 = (bf16[256,1152]{1,0:T(8,128)(2,1)}, bf16[256,1152]{1,0:T(8,128)(2,1)}, u32[]{:S(2)}, u32[]{:S(2)}) collective-permute-start(bf16[256,1152]{1,0:T(8,128)(2,1)} %get-tuple-element.90.both_ref.rest_4_), channel_id=1, source_target_pairs={{0,4},{2,6},{4,0},{6,2},{8,12},{10,14},{12,8},{14,10},{16,20},{18,... | collective-permute-start | bytes 1769480 | tf_op jit(solution)/shard_map/ppermute | solution.py:940
  65.1 1.6 collective-permute-start.11
  70.7 8.9 %collective-permute-start.15 = (bf16[56,1152]{1,0:T(8,128)(2,1)}, bf16[56,1152]{1,0:T(8,128)(2,1)}, u32[]{:S(2)}, u32[]{:S(2)}) collective-permute-start(bf16[56,1152]{1,0:T(8,128)(2,1)} %get-tuple-element.98), channel_id=1, source_target_pairs={{0,2},{2,0},{4,6},{6,4},{8,10},{10,8},{12,14},{14,12},{16,18},{18,... | collective-permute-start | bytes 387080 | tf_op jit(solution)/shard_map/ppermute | solution.py:940
  71.1 8.5 %collective-permute-start.16 = (bf16[56,1152]{1,0:T(8,128)(2,1)}, bf16[56,1152]{1,0:T(8,128)(2,1)}, u32[]{:S(2)}, u32[]{:S(2)}) collective-permute-start(bf16[56,1152]{1,0:T(8,128)(2,1)} %get-tuple-element.99), channel_id=1, source_target_pairs={{0,4},{2,6},{4,0},{6,2},{8,12},{10,14},{12,8},{14,10},{16,20},{18,... | collective-permute-start | bytes 387080 | tf_op jit(solution)/shard_map/ppermute | solution.py:940
  72.7 7.0 %collective-permute-start.12 = (f32[8,1152]{1,0:T(8,128)}, f32[8,1152]{1,0:T(8,128)}, u32[]{:S(2)}, u32[]{:S(2)}) collective-permute-start(f32[8,1152]{1,0:T(8,128)} %get-tuple-element.97), channel_id=1, source_target_pairs={{2,0},{4,2},{6,4},{8,6},{10,8},{12,10},{14,12},{16,14},{18,16},{20... | collective-permute-start | bytes 110600 | tf_op jit(solution)/shard_map/ppermute | solution.py:931
  81.8 11.6 %collective-permute-start.22 = (bf16[128,1152]{1,0:T(8,128)(2,1)}, bf16[128,1152]{1,0:T(8,128)(2,1)}, u32[]{:S(2)}, u32[]{:S(2)}) collective-permute-start(bf16[128,1152]{1,0:T(8,128)(2,1)} %get-tuple-element.100.rest_0_), channel_id=1, source_target_pairs={{0,4},{2,6},{4,0},{6,2},{8,12},{10,14},{12,8},{14,10},{16,20},{18,... | collective-permute-start | bytes 884744 | tf_op jit(solution)/shard_map/ppermute | solution.py:940
  82.6 10.8 %collective-permute-start.23 = (bf16[128,1152]{1,0:T(8,128)(2,1)}, bf16[128,1152]{1,0:T(8,128)(2,1)}, u32[]{:S(2)}, u32[]{:S(2)}) collective-permute-start(bf16[128,1152]{1,0:T(8,128)(2,1)} %get-tuple-element.106), channel_id=1, source_target_pairs={{0,2},{2,0},{4,6},{6,4},{8,10},{10,8},{12,14},{14,12},{16,18},{18,... | collective-permute-start | bytes 884744 | tf_op jit(solution)/shard_map/ppermute | solution.py:940
  84.9 8.5 %collective-permute-start.24 = (bf16[56,1152]{1,0:T(8,128)(2,1)}, bf16[56,1152]{1,0:T(8,128)(2,1)}, u32[]{:S(2)}, u32[]{:S(2)}) collective-permute-start(bf16[56,1152]{1,0:T(8,128)(2,1)} %get-tuple-element.108), channel_id=1, source_target_pairs={{0,6},{2,4},{4,2},{6,0},{8,14},{10,12},{12,10},{14,8},{16,22},{18,... | collective-permute-start | bytes 387080 | tf_op jit(solution)/shard_map/ppermute | solution.py:940
  98.7 16.8 %collective-permute-start.25 = (bf16[344,1152]{1,0:T(8,128)(2,1)}, bf16[344,1152]{1,0:T(8,128)(2,1)}, u32[]{:S(2)}, u32[]{:S(2)}) collective-permute-start(bf16[344,1152]{1,0:T(8,128)(2,1)} %get-tuple-element.111), channel_id=1, source_target_pairs={{0,8},{2,10},{4,12},{6,14},{8,0},{10,2},{12,4},{14,6},{16,24},{18,... | collective-permute-start | bytes 2377736 | tf_op jit(solution)/shard_map/ppermute | solution.py:940
  100.0 20.7 %collective-permute-start.19 = (bf16[144,1152]{1,0:T(8,128)(2,1)}, bf16[144,1152]{1,0:T(8,128)(2,1)}, u32[]{:S(2)}, u32[]{:S(2)}) collective-permute-start(bf16[144,1152]{1,0:T(8,128)(2,1)} %get-tuple-element.105.rest_4_), channel_id=1, source_target_pairs={{0,2},{2,0},{4,6},{6,4},{8,10},{10,8},{12,14},{14,12},{16,18},{18,... | collective-permute-start | bytes 995336 | tf_op jit(solution)/shard_map/ppermute | solution.py:940
  100.9 19.7 %collective-permute-start.20 = (bf16[144,1152]{1,0:T(8,128)(2,1)}, bf16[144,1152]{1,0:T(8,128)(2,1)}, u32[]{:S(2)}, u32[]{:S(2)}) collective-permute-start(bf16[144,1152]{1,0:T(8,128)(2,1)} %get-tuple-element.105.rest_4_), channel_id=1, source_target_pairs={{0,4},{2,6},{4,0},{6,2},{8,12},{10,14},{12,8},{14,10},{16,20},{18,... | collective-permute-start | bytes 995336 | tf_op jit(solution)/shard_map/ppermute | solution.py:940
  102.0 18.6 %collective-permute-start.21 = (bf16[144,1152]{1,0:T(8,128)(2,1)}, bf16[144,1152]{1,0:T(8,128)(2,1)}, u32[]{:S(2)}, u32[]{:S(2)}) collective-permute-start(bf16[144,1152]{1,0:T(8,128)(2,1)} %get-tuple-element.105.rest_4_), channel_id=1, source_target_pairs={{0,6},{2,4},{4,2},{6,0},{8,14},{10,12},{12,10},{14,8},{16,22},{18,... | collective-permute-start | bytes 995336 | tf_op jit(solution)/shard_map/ppermute | solution.py:940
  106.8 43.5 %collective-permute-start.17 = (f32[128,1152]{1,0:T(8,128)}, f32[128,1152]{1,0:T(8,128)}, u32[]{:S(2)}, u32[]{:S(2)}) collective-permute-start(f32[128,1152]{1,0:T(8,128)} %branch.1.branch_ref), channel_id=1, source_target_pairs={{0,1},{1,0},{2,3},{3,2},{4,5},{5,4},{6,7},{7,6},{8,9},{9,8},{10,11... | collective-permute-start | bytes 1769480 | tf_op jit(solution)/shard_map/ppermute | solution.py:935
  118.5 17.7 %collective-permute-start.27 = (bf16[200,1152]{1,0:T(8,128)(2,1)}, bf16[200,1152]{1,0:T(8,128)(2,1)}, u32[]{:S(2)}, u32[]{:S(2)}) collective-permute-start(bf16[200,1152]{1,0:T(8,128)(2,1)} %get-tuple-element.117), channel_id=1, source_target_pairs={{0,16},{2,18},{4,20},{6,22},{8,24},{10,26},{12,28},{14,30},{16,0},... | collective-permute-start | bytes 1382408 | tf_op jit(solution)/shard_map/ppermute | solution.py:940
  120.6 30.8 %collective-permute-start.18 = (f32[128,1152]{1,0:T(8,128)}, f32[128,1152]{1,0:T(8,128)}, u32[]{:S(2)}, u32[]{:S(2)}) collective-permute-start(f32[128,1152]{1,0:T(8,128)} %get-tuple-element.101._.own_ref.rest_13_), channel_id=1, source_target_pairs={{0,1},{1,0},{2,3},{3,2},{4,5},{5,4},{6,7},{7,6},{8,9},{9,8},{10,11... | collective-permute-start | bytes 1769480 | tf_op jit(solution)/shard_map/ppermute | solution.py:935
  124.2 17.6 %collective-permute-start.26 = (bf16[160,1152]{1,0:T(8,128)(2,1)}, bf16[160,1152]{1,0:T(8,128)(2,1)}, u32[]{:S(2)}, u32[]{:S(2)}) collective-permute-start(bf16[160,1152]{1,0:T(8,128)(2,1)} %get-tuple-element.115), channel_id=1, source_target_pairs={{0,8},{2,10},{4,12},{6,14},{8,0},{10,2},{12,4},{14,6},{16,24},{18,... | collective-permute-start | bytes 1105928 | tf_op jit(solution)/shard_map/ppermute | solution.py:940
  144.0 14.7 %collective-permute-start.28 = (bf16[88,1152]{1,0:T(8,128)(2,1)}, bf16[88,1152]{1,0:T(8,128)(2,1)}, u32[]{:S(2)}, u32[]{:S(2)}) collective-permute-start(bf16[88,1152]{1,0:T(8,128)(2,1)} %get-tuple-element.121), channel_id=1, source_target_pairs={{0,16},{2,18},{4,20},{6,22},{8,24},{10,26},{12,28},{14,30},{16,0},... | collective-permute-start | bytes 608264 | tf_op jit(solution)/shard_map/ppermute | solution.py:940
  147.9 6.4 %collective-permute-start.29 = (bf16[56,1152]{1,0:T(8,128)(2,1)}, bf16[56,1152]{1,0:T(8,128)(2,1)}, u32[]{:S(2)}, u32[]{:S(2)}) collective-permute-start(bf16[56,1152]{1,0:T(8,128)(2,1)} %get-tuple-element.122.refs_0_), channel_id=1, source_target_pairs={{0,2},{2,0},{4,6},{6,4},{8,10},{10,8},{12,14},{14,12},{16,18},{18,... | collective-permute-start | bytes 387080 | tf_op jit(solution)/shard_map/ppermute | solution.py:940
  148.3 7.3 %collective-permute-start.30 = (bf16[56,1152]{1,0:T(8,128)(2,1)}, bf16[56,1152]{1,0:T(8,128)(2,1)}, u32[]{:S(2)}, u32[]{:S(2)}) collective-permute-start(bf16[56,1152]{1,0:T(8,128)(2,1)} %get-tuple-element.122.refs_0_), channel_id=1, source_target_pairs={{0,4},{2,6},{4,0},{6,2},{8,12},{10,14},{12,8},{14,10},{16,20},{18,... | collective-permute-start | bytes 387080 | tf_op jit(solution)/shard_map/ppermute | solution.py:940
  150.3 6.2 %collective-permute-start.31 = (bf16[56,1152]{1,0:T(8,128)(2,1)}, bf16[56,1152]{1,0:T(8,128)(2,1)}, u32[]{:S(2)}, u32[]{:S(2)}) collective-permute-start(bf16[56,1152]{1,0:T(8,128)(2,1)} %get-tuple-element.122.refs_0_), channel_id=1, source_target_pairs={{0,6},{2,4},{4,2},{6,0},{8,14},{10,12},{12,10},{14,8},{16,22},{18,... | collective-permute-start | bytes 387080 | tf_op jit(solution)/shard_map/ppermute | solution.py:940
  160.5 1.4 collective-permute-start.32

commit v4 on v3

--- a/solution.py
+++ b/solution.py
@@ -103,63 +103,60 @@
 def enter_kernel(
     kernel, scan_width,
     normed_ref, rim_tokens_ref, cot_ref, tap_bias_ref, step_bias_ref, skip_ref, gain_ref, masks_ref,
-    conv_w_ref, gate_w_ref, out_w_ref, taps_ref, weight_ref,
+    taps_ref, weight_ref, conv_w_hbm, gate_w_hbm, out_w_hbm,
     conv_ref, rim_ref, out_ref, gate_ref, gg_ref, proj_ref, stacked_ref,
-    both_ref, mask_ref,
+    conv_w_ref, gate_w_ref, out_w_ref, sems,
 ):
-    length = normed_ref.shape[0]
-    block = conv_w_ref.shape[1]
-
-    @pl.when(pl.program_id(0) == 0)
-    def _():
-        for number, ref in enumerate((tap_bias_ref, step_bias_ref, skip_ref, gain_ref)):
-            stacked_ref[number : number + 1, :] = ref[...].reshape(1, ref.shape[0])
+    length, width = conv_ref.shape
+    block = 3 * LANES
+    blocks = [slice(first, first + block) for first in range(0, width, block)]
+    copies = []
+    for at in blocks:
+        piece = len(copies)
+        copies.append(pltpu.make_async_copy(conv_w_hbm.at[:, at], conv_w_ref.at[:, at], sems.at[piece]))
+    copies.append(pltpu.make_async_copy(gate_w_hbm, gate_w_ref, sems.at[len(blocks)]))
+    copies.append(pltpu.make_async_copy(out_w_hbm, out_w_ref, sems.at[len(blocks) + 1]))
+    for copy in copies:
+        copy.start()
+    vectors = [ref[...].reshape(1, width) for ref in (tap_bias_ref, step_bias_ref, skip_ref, gain_ref)]
+    stacked_ref[...] = jnp.concatenate(vectors, axis=0)
+    masks = [jnp.concatenate([columns(masks_ref, tap)] * (block // LANES), axis=1) for tap in range(kernel)]
+    rim = rim_tokens_ref[...].astype(jnp.float32)
+    rim = (rim * inverse_rms(rim) * vectors[GAIN]).astype(jnp.bfloat16)
+    normed = normed_ref[...]
+    both = jnp.concatenate([normed, rim, rim], axis=0)
+    proj = jnp.zeros((length, scan_width), jnp.float32)
+    for piece, at in enumerate(blocks):
+        copies[piece].wait()
+        conv_in = dot(both, conv_w_ref[:, at], ((1,), (0,))).astype(jnp.bfloat16)
+        conv_ref[:, at] = conv_in[:length]
+        wide = conv_in[:length].astype(jnp.float32)
+        rim = conv_in[length : length + CHUNKS].astype(jnp.float32)
+        rim_ref[:, at] = rim
+        total = jnp.broadcast_to(vectors[TAP_BIAS][:, at], (length, block))
         for tap in range(kernel):
-            mask_ref[tap] = columns(masks_ref, tap)
-        gain = row(stacked_ref, GAIN)
-        rim = rim_tokens_ref[...].astype(jnp.float32)
-        rim = (rim * inverse_rms(rim) * gain).astype(jnp.bfloat16)
-        both_ref[:length, :] = normed_ref[...]
-        both_ref[length:, :] = jnp.concatenate([rim, rim], axis=0)
-        proj_ref[...] = jnp.zeros_like(proj_ref)
-
-    normed = both_ref[...]
-    conv_in = dot(normed, conv_w_ref[...], ((1,), (0,))).astype(jnp.bfloat16)
-    conv_ref[...] = conv_in[:length]
-    wide = conv_in[:length].astype(jnp.float32)
-    rim = conv_in[length : length + CHUNKS].astype(jnp.float32)
-    rim_ref[...] = rim
-    at = pl.ds(pl.multiple_of(pl.program_id(0) * block, LANES), block)
-    total = jnp.broadcast_to(stacked_ref[TAP_BIAS : TAP_BIAS + 1, at], (length, block))
-    for tap in range(kernel):
-        mask = jnp.concatenate([mask_ref[tap]] * (block // LANES), axis=1)
-        total = total + row(taps_ref, tap) * shifted(wide, rim, kernel - 1 - tap) * mask
-    out = (total * sigmoid(total)).astype(jnp.bfloat16)
-    out_ref[...] = out
-    proj_ref[:, :scan_width] += dot(out, weight_ref[...], ((1,), (1,)))
-    gate_ref[...] = dot(normed[:length], gate_w_ref[...], ((1,), (0,)))
-    gg_ref[...] = dot(cot_ref[...], out_w_ref[...], ((1,), (1,)))
+            moved = shifted(wide, rim, kernel - 1 - tap)
+            total = total + taps_ref[tap : tap + 1, at] * moved * masks[tap]
+        out = (total * sigmoid(total)).astype(jnp.bfloat16)
+        out_ref[:, at] = out
+        proj = proj + dot(out, weight_ref[:, at], ((1,), (1,)))
+    proj_ref[...] = jnp.concatenate([proj, jnp.zeros((length, LANES - scan_width), jnp.float32)], axis=1)
+    copies[-2].wait()
+    for at in blocks:
+        gate_ref[:, at] = dot(normed, gate_w_ref[:, at], ((1,), (0,)))
+    copies[-1].wait()
+    for at in blocks:
+        gg_ref[:, at] = dot(cot_ref[...], out_w_ref[at, :], ((1,), (1,)))
 
 
 def run_enter(normed, rim, cot, vectors, masks, conv_w, gate_w, out_w, taps, weight):
     length, model = normed.shape
     width = conv_w.shape[1]
-    block = 3 * LANES
     f32, bf16 = jnp.float32, jnp.bfloat16
-    flat = pl.BlockSpec(memory_space=pltpu.VMEM)
+    vmem, hbm = pl.BlockSpec(memory_space=pltpu.VMEM), pl.BlockSpec(memory_space=pl.ANY)
     return pl.pallas_call(
         functools.partial(enter_kernel, taps.shape[0], weight.shape[0]),
-        grid=(width // block,),
-        in_specs=[whole(length, model), whole(CHUNKS, model), whole(length, model)] + [flat] * 4 + [
-            whole(*masks.shape), column_block(model, block), column_block(model, block),
-            pl.BlockSpec((block, model), lambda g: (g, 0)), column_block(taps.shape[0], block),
-            column_block(weight.shape[0], block),
-        ],
-        out_specs=[
-            column_block(length, block), column_block(CHUNKS, block), column_block(length, block),
-            column_block(length, block), column_block(length, block), whole(length, LANES),
-            whole(len(vectors), width),
-        ],
+        in_specs=[vmem] * 10 + [hbm] * 3, out_specs=[vmem] * 7,
         out_shape=[
             jax.ShapeDtypeStruct((length, width), bf16), jax.ShapeDtypeStruct((CHUNKS, width), f32),
             jax.ShapeDtypeStruct((length, width), bf16), jax.ShapeDtypeStruct((length, width), f32),
@@ -167,16 +164,28 @@
             jax.ShapeDtypeStruct((len(vectors), width), f32),
         ],
         scratch_shapes=[
-            pltpu.VMEM((length + 2 * CHUNKS, model), bf16),
-            pltpu.VMEM((taps.shape[0], length, LANES), f32),
+            pltpu.VMEM(conv_w.shape, bf16), pltpu.VMEM(gate_w.shape, bf16), pltpu.VMEM(out_w.shape, bf16),
+            pltpu.SemaphoreType.DMA((width // (3 * LANES) + 2,)),
         ],
         compiler_params=params(), cost_estimate=cost(6), name="enter",
-    )(normed, rim, cot, *vectors, masks, conv_w, gate_w, out_w, taps, weight)
-
-
-def early_kernel(members, where_ref, tokens_ref, cot_ref, gain_ref, normed_ref, *rest):
-    rim_ref, *early_refs, turned_ref = rest
+    )(normed, rim, cot, *vectors, masks, taps, weight, conv_w, gate_w, out_w)
+
+
+def early_kernel(members, kernel, tokens_ref, cot_ref, gain_ref, ids_ref, normed_ref, masks_ref, *rest):
+    rim_ref, *early_refs, turned_ref, rows_ref = rest
     length, model = tokens_ref.shape
+    device = lax.axis_index("seq")
+    rows_ref[...] = ids_ref[...].reshape(members, length)
+    ids = rows_ref[pl.ds(device, 1), :]
+    before = rows_ref[pl.ds(jnp.maximum(device - 1, 0), 1), :]
+    before = jnp.where(device > 0, before, -1)
+    lane = lax.broadcasted_iota(jnp.int32, ids.shape, 1)
+    for tap in range(kernel):
+        back = kernel - 1 - tap
+        seen = ids
+        if back:
+            seen = jnp.where(lane < back, pltpu.roll(before, back, 1), pltpu.roll(ids, back, 1))
+        masks_ref[tap : tap + 1, :] = jnp.where(ids == seen, 1.0, 0.0)
     rim_ref[...] = tokens_ref[length - CHUNKS :, :]
     tokens = tokens_ref[...].astype(jnp.float32)
     gain = gain_ref[...].reshape(1, model)
@@ -189,7 +198,7 @@
         )
     rows, lines = model // members, members // PLANE
     for mask, early_ref in enumerate(early_refs):
-        place = jnp.bitwise_xor(where_ref[0] % PLANE, mask)
+        place = jnp.bitwise_xor(device % PLANE, mask)
         for source in range(2):
             pieces = []
             for line in range(lines):
@@ -201,22 +210,24 @@
             early_ref[at, :] = jnp.concatenate(pieces, axis=0).astype(jnp.bfloat16)
 
 
-def run_early(where, tokens, cot, gain):
+def run_early(tokens, cot, gain, ids, kernel):
     length, model = tokens.shape
     members = lax.axis_size("seq")
     vmem = pl.BlockSpec(memory_space=pltpu.VMEM)
     early = jax.ShapeDtypeStruct((2 * model // PLANE, length), jnp.bfloat16)
     return pl.pallas_call(
-        functools.partial(early_kernel, members),
-        in_specs=[pl.BlockSpec(memory_space=pltpu.SMEM), vmem, vmem, vmem],
-        out_specs=[vmem] * (2 + PLANE),
+        functools.partial(early_kernel, members, kernel),
+        in_specs=[vmem] * 4, out_specs=[vmem] * (3 + PLANE),
         out_shape=[
             jax.ShapeDtypeStruct(tokens.shape, jnp.bfloat16),
+            jax.ShapeDtypeStruct((kernel, length), jnp.float32),
             jax.ShapeDtypeStruct((CHUNKS, model), jnp.bfloat16),
         ] + [early] * PLANE,
-        scratch_shapes=[pltpu.VMEM((2 * model, length), jnp.float32)],
+        scratch_shapes=[
+            pltpu.VMEM((2 * model, length), jnp.float32), pltpu.VMEM((members, length), jnp.int32),
+        ],
         compiler_params=params(), cost_estimate=cost(3), name="early",
-    )(where, tokens, cot, gain)
+    )(tokens, cot, gain, ids)
 
 
 def every(width):
@@ -544,7 +555,7 @@
     return carry, incoming
 
 
-def fold_kernel(states, level, members, start, where_ref, decay_ref, *refs):
+def fold_kernel(states, level, members, start, ndeps, where_ref, decay_ref, *refs):
     stride, radix = levels(members)[level]
     next_stride, next_radix = levels(members)[level + 1]
     last = level + 2 == len(levels(members))
@@ -554,7 +565,7 @@
         refs = refs[1:]
     own = refs[0][...]
     got = [ref[...] for ref in refs[1:radix]]
-    near_ref, outs = refs[radix], refs[radix + 1 :]
+    near_ref, *outs = refs[radix + ndeps :]
     rate2 = -jnp.exp(decay_ref[...]) * LOG2E
     own = own.astype(jnp.float32)
     values = [chosen(got, own, digit ^ number) for number in range(radix)]
@@ -593,7 +604,7 @@
         outs[0][2 * states :, :] = tail
 
 
-def run_fold(level, where, decay_log, near, parts):
+def run_fold(level, where, decay_log, near, parts, deps):
     states, width = decay_log.shape
     members = lax.axis_size("seq")
     f32, bf16 = jnp.float32, jnp.bfloat16
@@ -605,21 +616,22 @@
         sent = [jax.ShapeDtypeStruct((2 * states + 2 * CHUNKS, width), bf16)]
     extra = [] if near is None else [near]
     return pl.pallas_call(
-        functools.partial(fold_kernel, states, level, members, near is None),
-        in_specs=[pl.BlockSpec(memory_space=pltpu.SMEM)] + [vmem] * (1 + len(extra) + len(parts)),
+        functools.partial(fold_kernel, states, level, members, near is None, len(deps)),
+        in_specs=[pl.BlockSpec(memory_space=pltpu.SMEM)] + [vmem] * (1 + len(extra) + len(parts))
+        + [pl.BlockSpec(memory_space=pl.ANY) for _ in deps],
         out_specs=[vmem] * (1 + len(sent)),
         out_shape=[tall] + sent,
         compiler_params=params(), cost_estimate=cost(2), name="fold",
-    )(where, decay_log, *extra, *parts)
-
-
-def exchange(where, totals, decay_log):
+    )(where, decay_log, *extra, *parts, *deps)
+
+
+def exchange(where, totals, decay_log, deps):
     members = lax.axis_size("seq")
     found = levels(members)
     near = None
     for level, (stride, radix) in enumerate(found[:-1]):
         parts = [totals] + [hop(totals, mask * stride) for mask in range(1, radix)]
-        near, *sent = run_fold(level, where, decay_log, near, parts)
+        near, *sent = run_fold(level, where, decay_log, near, parts, deps)
         totals = sent[0]
     stride, radix = found[-1]
     return near, [hop(one, mask * stride) for mask, one in enumerate(sent, 1)]
@@ -954,14 +966,11 @@
     device = lax.axis_index("seq")
     where = jnp.stack([device, lax.axis_index("tp")]).astype(jnp.int32)
     scan_width = rank + 2 * states
-    padded_ids = jnp.concatenate([jnp.full((kernel,), -1, jnp.int32), segment_ids])
-    near_ids = lax.dynamic_slice_in_dim(padded_ids, device * length, length + kernel)
-    masks = jnp.stack(
-        [near_ids[kernel:] == near_ids[tap + 1 : tap + 1 + length] for tap in range(kernel)]
-    ).astype(f32)
     scan_weight = scan_proj_weight.T
 
-    normed, rim_tokens, kept_early, *sent_early = run_early(where, tokens, cotangent, norm_gain)
+    normed, masks, rim_tokens, kept_early, *sent_early = run_early(
+        tokens, cotangent, norm_gain, segment_ids, kernel
+    )
     rim_tokens = from_behind(rim_tokens, "seq", 1)
     early = [kept_early] + [hop(one, mask) for mask, one in enumerate(sent_early, 1)]
     conv_in, ext, conv_out, gate_in, grad_gated, own, stacked = run_enter(
@@ -970,10 +979,9 @@
     )
     peer = swap(own)
     ends, seeds, totals = run_ends(
-        own, peer, step_proj_weight, stacked, decay_log, conv_out, grad_gated, gate_in, masks,
-        early[1:],
-    )
-    near, far = exchange(where, totals, decay_log)
+        own, peer, step_proj_weight, stacked, decay_log, conv_out, grad_gated, gate_in, masks
+    )
+    near, far = exchange(where, totals, decay_log, early[1:])
     both, first_small, grad_conv, low_own = run_scan(
         where, own, peer, step_proj_weight, stacked, decay_log, conv_out, grad_gated, gate_in, masks,
         ends, seeds, near, far, (),
@@ -999,7 +1007,7 @@
     count = (members // PLANE).bit_length() - 1
     first = multiply((1, 0), where, early, first_late, small, (normed_own,))
     first = add_line(0, where, first, 2)
-    second = multiply((0,), where, early, second_late, [], first[:1])
+    second = multiply((0,), where, early, second_late, [], (first[0], input_grad))
     for level in range(1, count):
         first = add_line(level, where, first, 2)
     out_grad, in_gate_grad, small = first
@@ -1017,7 +1025,7 @@
         ),
     )
     for level in range(1, count):
-        second = add_line(level, where, second, 1, (input_grad, step_proj_grad))
+        second = add_line(level, where, second, 1)
     in_conv_grad, gain_grad = second
     gain_grad = gain_grad + swap(gain_grad)
     return (

time: 165 us -> 163 us (0.988)
  starting transfers between devices: 39.6 us -> 36 us
  waiting for transfers between devices: 48.1 us -> 51.2 us
    ppermute x2, waiting for transfers between devices: 3.92 us -> 8.78 us  [from_behind(): return lax.ppermute(block, axis, route)]
    ppermute x26, starting transfers between devices: 33.1 us -> 30.3 us  [hop(): return lax.ppermute(block, 'seq', [(i, i ^ mask) for i in range(members)])]
    ppermute x5, waiting for transfers between devices: 4.56 us -> 2.49 us  [swap(): return lax.ppermute(block, 'tp', [(0, 1), (1, 0)])]
  transfers between devices with their start and end apart: 33 -> 33, of which waited for: 16 -> 17; matrix products, arithmetic and copies ran while one was open for 1% -> 0% of each run, Pallas kernels for 22% -> 26%
where the time goes in v4:
time: 163 us; the launch traced here: 161 us
  Pallas kernels  70.8 us (43%)
  waiting for transfers between devices  51.2 us (31%)
  starting transfers between devices  36 us (22%)
  other arithmetic  1.98 us (1%)
    ppermute x26, waiting for transfers between devices, hop(): return lax.ppermute(block, 'seq', [(i, i ^ mask) for i in range(members)])  39.9 us
    ppermute x26, starting transfers between devices, hop(): return lax.ppermute(block, 'seq', [(i, i ^ mask) for i in range(members)])  30.3 us
    pallas_call x1, Pallas kernels, run_scan(): pl.pallas_call(functools.partial(scan_kernel, rank, states, members), in_...  14.3 us
    pallas_call x4, Pallas kernels, add_line(): pl.pallas_call(functools.partial(gather_kernel, level, number, len(deps))...  9.26 us
    pallas_call x2, Pallas kernels, multiply(): pl.pallas_call(functools.partial(products_kernel, halves, members, len(de...  8.92 us
    ppermute x2, waiting for transfers between devices, from_behind(): return lax.ppermute(block, axis, route)  8.78 us
    pallas_call x1, Pallas kernels, run_ends(): pl.pallas_call(functools.partial(ends_kernel, rank, states, len(deps)), i...  7.29 us
    pallas_call x1, Pallas kernels, run_enter(): pl.pallas_call(functools.partial(enter_kernel, taps.shape[0], weight.shap...  6.65 us
  transfers between devices with their start and end apart: 33, of which 17 were waited for; matrix products, arithmetic and copies ran while one was open for 0% of the time, Pallas kernels for 26%

profile of v4, /device:TPU:8, one launch (start us, length us, event | category | flops | bytes accessed | tf_op | source)
XLA Modules:
  0.0 160.8 jit_solution(3734673456951884849)
XLA Ops:
  0.6 2.2 %early.1 = (bf16[128,1152]{1,0:T(8,128)(2,1)}, f32[4,128]{1,0:T(4,128)}, bf16[8,1152]{1,0:T(8,128)(2,1)}, bf16[576,128]{1,0:T(8,128)(2,1)}, bf16[576,128]{1,0:T(...) custom-call(bf16[128,1152]{1,0:T(8,128)(2,1)} %tokens_ref.5, bf16[128,1152]{1,0:T(8,128)(2,1)} %cot_ref.5, ...), custom_call_target="tpu_custom_call" | custom-call | bytes 9000000 | tf_op jit(solution)/shard_map/early/pallas_call | solution.py:218
  2.9 1.5 collective-permute-start.5
  4.4 2.4 %collective-permute-start = (bf16[8,1152]{1,0:T(8,128)(2,1)}, bf16[8,1152]{1,0:T(8,128)(2,1)}, u32[]{:S(2)}, u32[]{:S(2)}) collective-permute-start(bf16[8,1152]{1,0:T(8,128)(2,1)} %get-tuple-element.75), channel_id=1, source_target_pairs={{0,2},{2,4},{4,6},{6,8},{8,10},{10,12},{12,14},{14,16},{16,18},{18... | collective-permute-start | bytes 55304 | tf_op jit(solution)/shard_map/ppermute | solution.py:943
  6.8 5.3 %collective-permute-done.rim_tokens_ref = bf16[8,1152]{1,0:T(8,128)(2,1)} collective-permute-done((bf16[8,1152]{1,0:T(8,128)(2,1)}, bf16[8,1152]{1,0:T(8,128)(2,1)}, u32[]{:S(2)}, u32[]{:S(2)}) %collective-permute-start) | collective-permute-done | bytes 18464 | tf_op jit(solution)/shard_map/ppermute | solution.py:943
  12.1 6.6 %enter.1 = (bf16[128,1152]{1,0:T(8,128)(2,1)}, f32[8,1152]{1,0:T(8,128)}, bf16[128,1152]{1,0:T(8,128)(2,1)}, f32[128,1152]{1,0:T(8,128)}, f32[128,1152]{1,0:T(8,...) custom-call(bf16[128,1152]{1,0:T(8,128)(2,1)} %get-tuple-element.74.normed_ref, ...), custom_call_target="tpu_custom_call" | custom-call | bytes 18000000 | tf_op jit(solution)/shard_map/enter/pallas_call | solution.py:157
  18.8 0.1 collective-permute-start.1
  18.9 0.7 collective-permute-start.6
  19.6 0.0 collective-permute-start.7
  19.6 0.9 collective-permute-done.1.peer_ref
  20.5 7.3 %ends.1 = (f32[128,1152]{1,0:T(8,128)}, f32[128,1152]{1,0:T(8,128)}, bf16[48,1152]{1,0:T(8,128)(2,1)}) custom-call(f32[128,128]{1,0:T(8,128)} %get-tuple-element.78.own_ref, f32[128,128]{1,0:T(8,128)} %collective-permute-done.1.peer_ref, bf16[72,1152]{1,0:T(8,128)(2,1)} %weight_ref.5, f32[4,1152]{1,0:T(4,128)} %get-tuple-element.77.bias_ref.params_ref, ...), custom_call_target="tpu_custom_call" | custom-call | bytes 24000000 | tf_op jit(solution)/shard_map/ends/pallas_call | solution.py:479
  27.7 2.0 %collective-permute-start.2 = (bf16[48,1152]{1,0:T(8,128)(2,1)}, bf16[48,1152]{1,0:T(8,128)(2,1)}, u32[]{:S(2)}, u32[]{:S(2)}) collective-permute-start(bf16[48,1152]{1,0:T(8,128)(2,1)} %get-tuple-element.84.refs_0_), channel_id=1, source_target_pairs={{0,2},{2,0},{4,6},{6,4},{8,10},{10,8},{12,14},{14,12},{16,18},{18,... | collective-permute-start | bytes 331784 | tf_op jit(solution)/shard_map/ppermute | solution.py:952
  29.7 0.6 collective-permute-start.3
  30.3 0.0 collective-permute-done.5.refs_4_.rest_1_
  30.3 0.9 collective-permute-start.4
  31.2 0.7 pad_add_fusion.where_ref
  31.9 1.6 collective-permute-done.2.refs_1_
  33.5 3.5 %collective-permute-done.3.refs_2_ = bf16[48,1152]{1,0:T(8,128)(2,1)} collective-permute-done((bf16[48,1152]{1,0:T(8,128)(2,1)}, bf16[48,1152]{1,0:T(8,128)(2,1)}, u32[]{:S(2)}, u32[]{:S(2)}) %collective-permute-start.3) | collective-permute-done | bytes 110624 | tf_op jit(solution)/shard_map/ppermute | solution.py:952
  37.0 2.1 %fold.1 = (f32[40,1152]{1,0:T(8,128)}, bf16[32,1152]{1,0:T(8,128)(2,1)}, bf16[32,1152]{1,0:T(8,128)(2,1)}, bf16[32,1152]{1,0:T(8,128)(2,1)}) custom-call(s32[2]{0:T(128)} %pad_add_fusion.where_ref, f32[16,1152]{1,0:T(8,128)} %decay_ref.5, bf16[48,1152]{1,0:T(8,128)(2,1)} %get-tuple-element.84.refs_0_, bf16[48,1152]{1,0:T(8,128)(2,1)} %collective-permute-done.2.refs_1_, ...), custom_call_target="tpu_custom_call" | custom-call | bytes 6000000 | tf_op jit(solution)/shard_map/fold/pallas_call | solution.py:618
  39.1 1.6 collective-permute-start.10
  40.7 2.5 %collective-permute-start.8 = (bf16[32,1152]{1,0:T(8,128)(2,1)}, bf16[32,1152]{1,0:T(8,128)(2,1)}, u32[]{:S(2)}, u32[]{:S(2)}) collective-permute-start(bf16[32,1152]{1,0:T(8,128)(2,1)} %get-tuple-element.89), channel_id=1, source_target_pairs={{0,8},{2,10},{4,12},{6,14},{8,0},{10,2},{12,4},{14,6},{16,24},{18,... | collective-permute-start | bytes 221192 | tf_op jit(solution)/shard_map/ppermute | solution.py:952
  43.2 2.8 %collective-permute-done.10.rest_2_ = bf16[32,1152]{1,0:T(8,128)(2,1)} collective-permute-done((bf16[32,1152]{1,0:T(8,128)(2,1)}, bf16[32,1152]{1,0:T(8,128)(2,1)}, u32[]{:S(2)}, u32[]{:S(2)}) %collective-permute-start.10) | collective-permute-done | bytes 73760 | tf_op jit(solution)/shard_map/ppermute | solution.py:952
  46.0 0.7 collective-permute-done.8.rest_0_
  46.6 2.1 %collective-permute-done.9.rest_1_ = bf16[32,1152]{1,0:T(8,128)(2,1)} collective-permute-done((bf16[32,1152]{1,0:T(8,128)(2,1)}, bf16[32,1152]{1,0:T(8,128)(2,1)}, u32[]{:S(2)}, u32[]{:S(2)}) %collective-permute-start.9) | collective-permute-done | bytes 73760 | tf_op jit(solution)/shard_map/ppermute | solution.py:952
  48.8 14.3 %scan.1 = (bf16[256,1152]{1,0:T(8,128)(2,1)}, f32[96,1152]{1,0:T(8,128)}, f32[128,1152]{1,0:T(8,128)}, f32[128,128]{1,0:T(8,128)}) custom-call(s32[2]{0:T(128)} %pad_add_fusion.where_ref, f32[128,128]{1,0:T(8,128)} %get-tuple-element.78.own_ref, f32[128,128]{1,0:T(8,128)} %collective-permute-done.1.peer_ref, bf16[72,1152]{1,0:T(8,128)(2,1)} %weight_ref.5, ...), custom_call_target="tpu_custom_call" | custom-call | bytes 45000000 | tf_op jit(solution)/shard_map/scan/pallas_call | solution.py:506
  63.1 0.3 collective-permute-start.13
  63.3 1.4 collective-permute-start.14
  64.8 1.6 collective-permute-done.11.peer_ref
  66.3 4.0 %taps.1 = (f32[128,1152]{1,0:T(8,128)}, f32[8,1152]{1,0:T(8,128)}, f32[56,1152]{1,0:T(8,128)}, bf16[56,1152]{1,0:T(8,128)(2,1)}, bf16[56,1152]{1,0:T(8,128)(2,1)}, /*index=5*/bf16[56,1152]{1,0:T(8,128)(2,1)}) custom-call(s32[2]{0:T(128)} %pad_add_fusion.where_ref, f32[128,128]{1,0:T(8,128)} %get-tuple-element.93.own_ref, ...), custom_call_target="tpu_custom_call" | custom-call | bytes 12000000 | tf_op jit(solution)/shard_map/taps/pallas_call | solution.py:702
  70.4 1.1 collective-permute-start.15
  71.5 1.3 collective-permute-start.16
  72.8 2.7 %collective-permute-start.12 = (f32[8,1152]{1,0:T(8,128)}, f32[8,1152]{1,0:T(8,128)}, u32[]{:S(2)}, u32[]{:S(2)}) collective-permute-start(f32[8,1152]{1,0:T(8,128)} %get-tuple-element.99), channel_id=1, source_target_pairs={{2,0},{4,2},{6,4},{8,6},{10,8},{12,10},{14,12},{16,14},{18,16},{20... | collective-permute-start | bytes 110600 | tf_op jit(solution)/shard_map/ppermute | solution.py:943
  75.5 3.5 %collective-permute-done.12.rest_1_.rim_ref = f32[8,1152]{1,0:T(8,128)} collective-permute-done((f32[8,1152]{1,0:T(8,128)}, f32[8,1152]{1,0:T(8,128)}, u32[]{:S(2)}, u32[]{:S(2)}) %collective-permute-start.12) | collective-permute-done | bytes 36896 | tf_op jit(solution)/shard_map/ppermute | solution.py:943
  78.9 2.1 %relay.1 = (bf16[128,1152]{1,0:T(8,128)(2,1)}, bf16[128,1152]{1,0:T(8,128)(2,1)}) custom-call(bf16[256,1152]{1,0:T(8,128)(2,1)} %collective-permute-done.13.x_ref.rest_5_, bf16[256,1152]{1,0:T(8,128)(2,1)} %collective-permute-done.14.y_ref.rest_6_, f32[128,1152]{1,0:T(8,128)} %get-tuple-element.98.rest_0_.main_ref, ...), custom_call_target="tpu_custom_call" | custom-call | bytes 3000000 | tf_op jit(solution)/shard_map/relay/pallas_call | solution.py:911
  81.0 1.2 collective-permute-start.22
  82.3 2.2 %collective-permute-start.23 = (bf16[128,1152]{1,0:T(8,128)(2,1)}, bf16[128,1152]{1,0:T(8,128)(2,1)}, u32[]{:S(2)}, u32[]{:S(2)}) collective-permute-start(bf16[128,1152]{1,0:T(8,128)(2,1)} %get-tuple-element.108), channel_id=1, source_target_pairs={{0,2},{2,0},{4,6},{6,4},{8,10},{10,8},{12,14},{14,12},{16,18},{18,... | collective-permute-start | bytes 884744 | tf_op jit(solution)/shard_map/ppermute | solution.py:952
  84.5 0.0 collective-permute-start.24
  84.5 5.6 %inputs.1 = (bf16[144,1152]{1,0:T(8,128)(2,1)}, f32[128,1152]{1,0:T(8,128)}) custom-call(f32[128,1152]{1,0:T(8,128)} %get-tuple-element.98.rest_0_.main_ref, f32[8,1152]{1,0:T(8,128)} %collective-permute-done.12.rest_1_.rim_ref, bf16[1152,1152]{1,0:T(8,128)(2,1)} %weight_ref.6, bf16[256,1152]{1,0:T(8,128)(2,1)} %get-tuple-element.92.both_ref.rest_4_, ...), custom_call_target="tpu_custom_call" | custom-call | bytes 9000000 | tf_op jit(solution)/shard_map/inputs/pallas_call | solution.py:733
  90.1 3.3 %collective-permute-done.24.rest_12_ = bf16[56,1152]{1,0:T(8,128)(2,1)} collective-permute-done((bf16[56,1152]{1,0:T(8,128)(2,1)}, bf16[56,1152]{1,0:T(8,128)(2,1)}, u32[]{:S(2)}, u32[]{:S(2)}) %collective-permute-start.24) | collective-permute-done | bytes 129056 | tf_op jit(solution)/shard_map/ppermute | solution.py:952
  93.4 5.4 %products.2 = (f32[2,144,1152]{2,1,0:T(8,128)}, f32[56,1152]{1,0:T(8,128)}, bf16[344,1152]{1,0:T(8,128)(2,1)}) custom-call(s32[2]{0:T(128)} %pad_add_fusion.where_ref, bf16[576,128]{1,0:T(8,128)(2,1)} %get-tuple-element.106.rest_0_, bf16[576,128]{1,0:T(8,128)(2,1)} %collective-permute-done.5.refs_4_.rest_1_, ...), custom_call_target="tpu_custom_call" | custom-call | bytes 12000000 | tf_op jit(solution)/shard_map/products/pallas_call | solution.py:818
  98.8 3.4 %branch.1.branch_ref = f32[128,1152]{1,0:T(8,128)} custom-call(bf16[256,1152]{1,0:T(8,128)(2,1)} %get-tuple-element.92.both_ref.rest_4_, bf16[1152,1152]{1,0:T(8,128)(2,1)} %weight_ref.7, f32[128,1152]{1,0:T(8,128)} %get-tuple-element.103._.own_ref.rest_13_), custom_call_target="tpu_custom_call" | custom-call | bytes 15000000 | tf_op jit(solution)/shard_map/branch/pallas_call | solution.py:868
  102.2 0.5 collective-permute-start.18
  102.7 1.3 collective-permute-start.19
  103.9 1.6 %collective-permute-start.20 = (bf16[144,1152]{1,0:T(8,128)(2,1)}, bf16[144,1152]{1,0:T(8,128)(2,1)}, u32[]{:S(2)}, u32[]{:S(2)}) collective-permute-start(bf16[144,1152]{1,0:T(8,128)(2,1)} %get-tuple-element.107.rest_4_), channel_id=1, source_target_pairs={{0,4},{2,6},{4,0},{6,2},{8,12},{10,14},{12,8},{14,10},{16,20},{18,... | collective-permute-start | bytes 995336 | tf_op jit(solution)/shard_map/ppermute | solution.py:952
  105.5 10.8 %collective-permute-done.25.got_ref = bf16[344,1152]{1,0:T(8,128)(2,1)} collective-permute-done((bf16[344,1152]{1,0:T(8,128)(2,1)}, bf16[344,1152]{1,0:T(8,128)(2,1)}, u32[]{:S(2)}, u32[]{:S(2)}) %collective-permute-start.25) | collective-permute-done | bytes 792608 | tf_op jit(solution)/shard_map/ppermute | solution.py:952
  116.4 1.6 %collective-permute-start.21 = (bf16[144,1152]{1,0:T(8,128)(2,1)}, bf16[144,1152]{1,0:T(8,128)(2,1)}, u32[]{:S(2)}, u32[]{:S(2)}) collective-permute-start(bf16[144,1152]{1,0:T(8,128)(2,1)} %get-tuple-element.107.rest_4_), channel_id=1, source_target_pairs={{0,6},{2,4},{4,2},{6,0},{8,14},{10,12},{12,10},{14,8},{16,22},{18,... | collective-permute-start | bytes 995336 | tf_op jit(solution)/shard_map/ppermute | solution.py:952
  118.0 3.0 %gather.4 = (f32[1,144,1152]{2,1,0:T(8,128)}, f32[56,1152]{1,0:T(8,128)}, bf16[200,1152]{1,0:T(8,128)(2,1)}) custom-call(s32[2]{0:T(128)} %pad_add_fusion.where_ref, f32[2,144,1152]{2,1,0:T(8,128)} %get-tuple-element.111.kept_ref, f32[56,1152]{1,0:T(8,128)} %get-tuple-element.112.small_ref, bf16[344,1152]{1,0:T(8,128)(2,1)} %collective-permute-done.25.got_ref), custom_call_target="tpu_custom_call" | custom-call | bytes 6000000 | tf_op jit(solution)/shard_map/gather/pallas_call | solution.py:853
  121.0 0.5 collective-permute-start.27
  121.5 2.9 %leave.1 = (bf16[128,1152]{1,0:T(8,128)(2,1)}, f32[128,1152]{1,0:T(8,128)}) custom-call(bf16[128,1152]{1,0:T(8,128)(2,1)} %tokens_ref.5, bf16[128,1152]{1,0:T(8,128)(2,1)} %cot_ref.5, f32[4,1152]{1,0:T(4,128)} %get-tuple-element.77.bias_ref.params_ref, f32[128,1152]{1,0:T(8,128)} %branch.1.branch_ref, f32[128,1152]{1,0:T(8,128)} %collective-permute-done.17.branch_peer_ref, ...), custom_call_target="tpu_custom_call" | custom-call | bytes 9000000 | tf_op jit(solution)/shard_map/leave/pallas_call | solution.py:930
  124.4 0.3 collective-permute-done.21.rest_7_
  124.7 3.5 %products.3 = (f32[2,72,1152]{2,1,0:T(8,128)}, f32[16,1152]{1,0:T(8,128)}, bf16[160,1152]{1,0:T(8,128)(2,1)}) custom-call(s32[2]{0:T(128)} %pad_add_fusion.where_ref, bf16[576,128]{1,0:T(8,128)(2,1)} %get-tuple-element.106.rest_0_, bf16[576,128]{1,0:T(8,128)(2,1)} %collective-permute-done.5.refs_4_.rest_1_, ...), custom_call_target="tpu_custom_call" | custom-call | bytes 12000000 | tf_op jit(solution)/shard_map/products/pallas_call | solution.py:818
  128.3 1.4 collective-permute-start.26
  129.7 7.7 %collective-permute-done.27.got_ref = bf16[200,1152]{1,0:T(8,128)(2,1)} collective-permute-done((bf16[200,1152]{1,0:T(8,128)(2,1)}, bf16[200,1152]{1,0:T(8,128)(2,1)}, u32[]{:S(2)}, u32[]{:S(2)}) %collective-permute-start.27) | collective-permute-done | bytes 460832 | tf_op jit(solution)/shard_map/ppermute | solution.py:952
  137.4 2.3 %gather.5 = (f32[72,1152]{1,0:T(8,128)}, f32[72,1152]{1,0:T(8,128)}, bf16[56,1152]{1,0:T(8,128)(2,1)}) custom-call(s32[2]{0:T(128)} %pad_add_fusion.where_ref, f32[1,144,1152]{2,1,0:T(8,128)} %get-tuple-element.114.rest_8_.kept_ref, f32[56,1152]{1,0:T(8,128)} %get-tuple-element.118.small_ref, bf16[200,1152]{1,0:T(8,128)(2,1)} %collective-permute-done.27.got_ref), custom_call_target="tpu_custom_call" | custom-call | bytes 6000000 | tf_op jit(solution)/shard_map/gather/pallas_call | solution.py:853
  139.6 2.7 %collective-permute-done.26.got_ref = bf16[160,1152]{1,0:T(8,128)(2,1)} collective-permute-done((bf16[160,1152]{1,0:T(8,128)(2,1)}, bf16[160,1152]{1,0:T(8,128)(2,1)}, u32[]{:S(2)}, u32[]{:S(2)}) %collective-permute-start.26) | collective-permute-done | bytes 368672 | tf_op jit(solution)/shard_map/ppermute | solution.py:952
  142.4 2.2 %gather.6 = (f32[1,72,1152]{2,1,0:T(8,128)}, f32[16,1152]{1,0:T(8,128)}, bf16[88,1152]{1,0:T(8,128)(2,1)}) custom-call(s32[2]{0:T(128)} %pad_add_fusion.where_ref, f32[2,72,1152]{2,1,0:T(8,128)} %get-tuple-element.115.kept_ref, f32[16,1152]{1,0:T(8,128)} %get-tuple-element.116.small_ref, bf16[160,1152]{1,0:T(8,128)(2,1)} %collective-permute-done.26.got_ref, ...), custom_call_target="tpu_custom_call" | custom-call | bytes 6000000 | tf_op jit(solution)/shard_map/gather/pallas_call | solution.py:853
  144.5 2.8 %collective-permute-start.28 = (bf16[88,1152]{1,0:T(8,128)(2,1)}, bf16[88,1152]{1,0:T(8,128)(2,1)}, u32[]{:S(2)}, u32[]{:S(2)}) collective-permute-start(bf16[88,1152]{1,0:T(8,128)(2,1)} %get-tuple-element.123), channel_id=1, source_target_pairs={{0,16},{2,18},{4,20},{6,22},{8,24},{10,26},{12,28},{14,30},{16,0},... | collective-permute-start | bytes 608264 | tf_op jit(solution)/shard_map/ppermute | solution.py:952
  147.3 1.2 collective-permute-start.30
  148.5 2.7 %collective-permute-start.31 = (bf16[56,1152]{1,0:T(8,128)(2,1)}, bf16[56,1152]{1,0:T(8,128)(2,1)}, u32[]{:S(2)}, u32[]{:S(2)}) collective-permute-start(bf16[56,1152]{1,0:T(8,128)(2,1)} %get-tuple-element.127.refs_0_), channel_id=1, source_target_pairs={{0,4},{2,6},{4,0},{6,2},{8,12},{10,14},{12,8},{14,10},{16,20},{18,... | collective-permute-start | bytes 387080 | tf_op jit(solution)/shard_map/ppermute | solution.py:952
  151.2 2.0 %collective-permute-done.28.got_ref = bf16[88,1152]{1,0:T(8,128)(2,1)} collective-permute-done((bf16[88,1152]{1,0:T(8,128)(2,1)}, bf16[88,1152]{1,0:T(8,128)(2,1)}, u32[]{:S(2)}, u32[]{:S(2)}) %collective-permute-start.28) | collective-permute-done | bytes 202784 | tf_op jit(solution)/shard_map/ppermute | solution.py:952
  153.2 1.8 %gather.7 = (f32[72,1152]{1,0:T(8,128)}, f32[1152]{0:T(1024)}) custom-call(s32[2]{0:T(128)} %pad_add_fusion.where_ref, f32[1,72,1152]{2,1,0:T(8,128)} %get-tuple-element.121.kept_ref, f32[16,1152]{1,0:T(8,128)} %get-tuple-element.122.small_ref, bf16[88,1152]{1,0:T(8,128)(2,1)} %collective-permute-done.28.got_ref), custom_call_target="tpu_custom_call" | custom-call | bytes 6000000 | tf_op jit(solution)/shard_map/gather/pallas_call | solution.py:853
  155.1 0.3 collective-permute-done.31.refs_2_
  155.4 2.0 %collective-permute-done.32.refs_3_ = bf16[56,1152]{1,0:T(8,128)(2,1)} collective-permute-done((bf16[56,1152]{1,0:T(8,128)(2,1)}, bf16[56,1152]{1,0:T(8,128)(2,1)}, u32[]{:S(2)}, u32[]{:S(2)}) %collective-permute-start.32) | collective-permute-done | bytes 129056 | tf_op jit(solution)/shard_map/ppermute | solution.py:952
  157.4 2.1 %place.1 = (f32[72,1152]{1,0:T(8,128)}, f32[16,1152]{1,0:T(8,128)}, f32[1152]{0:T(1024)}, f32[1152]{0:T(1024)}, f32[104,1152]{1,0:T(8,128)}, /*index=5*/f32[4,1152]{1,0:T(4,128)}, f32[1152]{0:T(1024)}) custom-call(s32[2]{0:T(128)} %pad_add_fusion.where_ref, bf16[56,1152]{1,0:T(8,128)(2,1)} %get-tuple-element.127.refs_0_, ...), custom_call_target="tpu_custom_call" | custom-call | bytes 9000000 | tf_op jit(solution)/shard_map/place/pallas_call | solution.py:891
  159.5 1.3 add.3
  (21 shorter events, 0.1 us)
Async XLA Ops:
  2.9 27.5 %collective-permute-start.5 = (bf16[576,128]{1,0:T(8,128)(2,1)}, bf16[576,128]{1,0:T(8,128)(2,1)}, u32[]{:S(2)}, u32[]{:S(2)}) collective-permute-start(bf16[576,128]{1,0:T(8,128)(2,1)} %get-tuple-element.85), channel_id=1, source_target_pairs={{0,2},{2,0},{4,6},{6,4},{8,10},{10,8},{12,14},{14,12},{16,18},{18,... | collective-permute-start | bytes 442376 | tf_op jit(solution)/shard_map/ppermute | solution.py:952
  4.4 7.8 %collective-permute-start = (bf16[8,1152]{1,0:T(8,128)(2,1)}, bf16[8,1152]{1,0:T(8,128)(2,1)}, u32[]{:S(2)}, u32[]{:S(2)}) collective-permute-start(bf16[8,1152]{1,0:T(8,128)(2,1)} %get-tuple-element.75), channel_id=1, source_target_pairs={{0,2},{2,4},{4,6},{6,8},{8,10},{10,12},{12,14},{14,16},{16,18},{18... | collective-permute-start | bytes 55304 | tf_op jit(solution)/shard_map/ppermute | solution.py:943
  18.8 1.7 %collective-permute-start.1 = (f32[128,128]{1,0:T(8,128)}, f32[128,128]{1,0:T(8,128)}, u32[]{:S(2)}, u32[]{:S(2)}) collective-permute-start(f32[128,128]{1,0:T(8,128)} %get-tuple-element.78.own_ref), channel_id=1, source_target_pairs={{0,1},{1,0},{2,3},{3,2},{4,5},{5,4},{6,7},{7,6},{8,9},{9,8},{10,11... | collective-permute-start | bytes 196616 | tf_op jit(solution)/shard_map/ppermute | solution.py:947
  18.9 13.0 %collective-permute-start.6 = (bf16[576,128]{1,0:T(8,128)(2,1)}, bf16[576,128]{1,0:T(8,128)(2,1)}, u32[]{:S(2)}, u32[]{:S(2)}) collective-permute-start(bf16[576,128]{1,0:T(8,128)(2,1)} %get-tuple-element.86), channel_id=1, source_target_pairs={{0,4},{2,6},{4,0},{6,2},{8,12},{10,14},{12,8},{14,10},{16,20},{18,... | collective-permute-start | bytes 442376 | tf_op jit(solution)/shard_map/ppermute | solution.py:952
  19.6 12.3 %collective-permute-start.7 = (bf16[576,128]{1,0:T(8,128)(2,1)}, bf16[576,128]{1,0:T(8,128)(2,1)}, u32[]{:S(2)}, u32[]{:S(2)}) collective-permute-start(bf16[576,128]{1,0:T(8,128)(2,1)} %get-tuple-element.87), channel_id=1, source_target_pairs={{0,6},{2,4},{4,2},{6,0},{8,14},{10,12},{12,10},{14,8},{16,22},{18,... | collective-permute-start | bytes 442376 | tf_op jit(solution)/shard_map/ppermute | solution.py:952
  27.7 5.8 %collective-permute-start.2 = (bf16[48,1152]{1,0:T(8,128)(2,1)}, bf16[48,1152]{1,0:T(8,128)(2,1)}, u32[]{:S(2)}, u32[]{:S(2)}) collective-permute-start(bf16[48,1152]{1,0:T(8,128)(2,1)} %get-tuple-element.84.refs_0_), channel_id=1, source_target_pairs={{0,2},{2,0},{4,6},{6,4},{8,10},{10,8},{12,14},{14,12},{16,18},{18,... | collective-permute-start | bytes 331784 | tf_op jit(solution)/shard_map/ppermute | solution.py:952
  29.7 7.3 %collective-permute-start.3 = (bf16[48,1152]{1,0:T(8,128)(2,1)}, bf16[48,1152]{1,0:T(8,128)(2,1)}, u32[]{:S(2)}, u32[]{:S(2)}) collective-permute-start(bf16[48,1152]{1,0:T(8,128)(2,1)} %get-tuple-element.84.refs_0_), channel_id=1, source_target_pairs={{0,4},{2,6},{4,0},{6,2},{8,12},{10,14},{12,8},{14,10},{16,20},{18,... | collective-permute-start | bytes 331784 | tf_op jit(solution)/shard_map/ppermute | solution.py:952
  30.3 6.7 %collective-permute-start.4 = (bf16[48,1152]{1,0:T(8,128)(2,1)}, bf16[48,1152]{1,0:T(8,128)(2,1)}, u32[]{:S(2)}, u32[]{:S(2)}) collective-permute-start(bf16[48,1152]{1,0:T(8,128)(2,1)} %get-tuple-element.84.refs_0_), channel_id=1, source_target_pairs={{0,6},{2,4},{4,2},{6,0},{8,14},{10,12},{12,10},{14,8},{16,22},{18,... | collective-permute-start | bytes 331784 | tf_op jit(solution)/shard_map/ppermute | solution.py:952
  39.1 6.8 %collective-permute-start.10 = (bf16[32,1152]{1,0:T(8,128)(2,1)}, bf16[32,1152]{1,0:T(8,128)(2,1)}, u32[]{:S(2)}, u32[]{:S(2)}) collective-permute-start(bf16[32,1152]{1,0:T(8,128)(2,1)} %get-tuple-element.91), channel_id=1, source_target_pairs={{0,24},{2,26},{4,28},{6,30},{8,16},{10,18},{12,20},{14,22},{16,8},... | collective-permute-start | bytes 221192 | tf_op jit(solution)/shard_map/ppermute | solution.py:952
  40.7 5.9 %collective-permute-start.8 = (bf16[32,1152]{1,0:T(8,128)(2,1)}, bf16[32,1152]{1,0:T(8,128)(2,1)}, u32[]{:S(2)}, u32[]{:S(2)}) collective-permute-start(bf16[32,1152]{1,0:T(8,128)(2,1)} %get-tuple-element.89), channel_id=1, source_target_pairs={{0,8},{2,10},{4,12},{6,14},{8,0},{10,2},{12,4},{14,6},{16,24},{18,... | collective-permute-start | bytes 221192 | tf_op jit(solution)/shard_map/ppermute | solution.py:952
  43.2 5.6 %collective-permute-start.9 = (bf16[32,1152]{1,0:T(8,128)(2,1)}, bf16[32,1152]{1,0:T(8,128)(2,1)}, u32[]{:S(2)}, u32[]{:S(2)}) collective-permute-start(bf16[32,1152]{1,0:T(8,128)(2,1)} %get-tuple-element.90), channel_id=1, source_target_pairs={{0,16},{2,18},{4,20},{6,22},{8,24},{10,26},{12,28},{14,30},{16,0},... | collective-permute-start | bytes 221192 | tf_op jit(solution)/shard_map/ppermute | solution.py:952
  63.1 15.9 %collective-permute-start.13 = (bf16[256,1152]{1,0:T(8,128)(2,1)}, bf16[256,1152]{1,0:T(8,128)(2,1)}, u32[]{:S(2)}, u32[]{:S(2)}) collective-permute-start(bf16[256,1152]{1,0:T(8,128)(2,1)} %get-tuple-element.92.both_ref.rest_4_), channel_id=1, source_target_pairs={{0,2},{2,0},{4,6},{6,4},{8,10},{10,8},{12,14},{14,12},{16,18},{18,... | collective-permute-start | bytes 1769480 | tf_op jit(solution)/shard_map/ppermute | solution.py:952
  63.3 15.6 %collective-permute-start.14 = (bf16[256,1152]{1,0:T(8,128)(2,1)}, bf16[256,1152]{1,0:T(8,128)(2,1)}, u32[]{:S(2)}, u32[]{:S(2)}) collective-permute-start(bf16[256,1152]{1,0:T(8,128)(2,1)} %get-tuple-element.92.both_ref.rest_4_), channel_id=1, source_target_pairs={{0,4},{2,6},{4,0},{6,2},{8,12},{10,14},{12,8},{14,10},{16,20},{18,... | collective-permute-start | bytes 1769480 | tf_op jit(solution)/shard_map/ppermute | solution.py:952
  64.7 1.6 collective-permute-start.11
  70.4 8.5 %collective-permute-start.15 = (bf16[56,1152]{1,0:T(8,128)(2,1)}, bf16[56,1152]{1,0:T(8,128)(2,1)}, u32[]{:S(2)}, u32[]{:S(2)}) collective-permute-start(bf16[56,1152]{1,0:T(8,128)(2,1)} %get-tuple-element.100), channel_id=1, source_target_pairs={{0,2},{2,0},{4,6},{6,4},{8,10},{10,8},{12,14},{14,12},{16,18},{18,... | collective-permute-start | bytes 387080 | tf_op jit(solution)/shard_map/ppermute | solution.py:952
  71.5 7.5 %collective-permute-start.16 = (bf16[56,1152]{1,0:T(8,128)(2,1)}, bf16[56,1152]{1,0:T(8,128)(2,1)}, u32[]{:S(2)}, u32[]{:S(2)}) collective-permute-start(bf16[56,1152]{1,0:T(8,128)(2,1)} %get-tuple-element.101), channel_id=1, source_target_pairs={{0,4},{2,6},{4,0},{6,2},{8,12},{10,14},{12,8},{14,10},{16,20},{18,... | collective-permute-start | bytes 387080 | tf_op jit(solution)/shard_map/ppermute | solution.py:952
  72.8 6.2 %collective-permute-start.12 = (f32[8,1152]{1,0:T(8,128)}, f32[8,1152]{1,0:T(8,128)}, u32[]{:S(2)}, u32[]{:S(2)}) collective-permute-start(f32[8,1152]{1,0:T(8,128)} %get-tuple-element.99), channel_id=1, source_target_pairs={{2,0},{4,2},{6,4},{8,6},{10,8},{12,10},{14,12},{16,14},{18,16},{20... | collective-permute-start | bytes 110600 | tf_op jit(solution)/shard_map/ppermute | solution.py:943
  81.0 12.4 %collective-permute-start.22 = (bf16[128,1152]{1,0:T(8,128)(2,1)}, bf16[128,1152]{1,0:T(8,128)(2,1)}, u32[]{:S(2)}, u32[]{:S(2)}) collective-permute-start(bf16[128,1152]{1,0:T(8,128)(2,1)} %get-tuple-element.102.rest_0_), channel_id=1, source_target_pairs={{0,4},{2,6},{4,0},{6,2},{8,12},{10,14},{12,8},{14,10},{16,20},{18,... | collective-permute-start | bytes 884744 | tf_op jit(solution)/shard_map/ppermute | solution.py:952
  82.3 11.1 %collective-permute-start.23 = (bf16[128,1152]{1,0:T(8,128)(2,1)}, bf16[128,1152]{1,0:T(8,128)(2,1)}, u32[]{:S(2)}, u32[]{:S(2)}) collective-permute-start(bf16[128,1152]{1,0:T(8,128)(2,1)} %get-tuple-element.108), channel_id=1, source_target_pairs={{0,2},{2,0},{4,6},{6,4},{8,10},{10,8},{12,14},{14,12},{16,18},{18,... | collective-permute-start | bytes 884744 | tf_op jit(solution)/shard_map/ppermute | solution.py:952
  84.5 8.9 %collective-permute-start.24 = (bf16[56,1152]{1,0:T(8,128)(2,1)}, bf16[56,1152]{1,0:T(8,128)(2,1)}, u32[]{:S(2)}, u32[]{:S(2)}) collective-permute-start(bf16[56,1152]{1,0:T(8,128)(2,1)} %get-tuple-element.110), channel_id=1, source_target_pairs={{0,6},{2,4},{4,2},{6,0},{8,14},{10,12},{12,10},{14,8},{16,22},{18,... | collective-permute-start | bytes 387080 | tf_op jit(solution)/shard_map/ppermute | solution.py:952
  98.8 17.6 %collective-permute-start.25 = (bf16[344,1152]{1,0:T(8,128)(2,1)}, bf16[344,1152]{1,0:T(8,128)(2,1)}, u32[]{:S(2)}, u32[]{:S(2)}) collective-permute-start(bf16[344,1152]{1,0:T(8,128)(2,1)} %get-tuple-element.113), channel_id=1, source_target_pairs={{0,8},{2,10},{4,12},{6,14},{8,0},{10,2},{12,4},{14,6},{16,24},{18,... | collective-permute-start | bytes 2377736 | tf_op jit(solution)/shard_map/ppermute | solution.py:952
  102.2 18.8 %collective-permute-start.17 = (f32[128,1152]{1,0:T(8,128)}, f32[128,1152]{1,0:T(8,128)}, u32[]{:S(2)}, u32[]{:S(2)}) collective-permute-start(f32[128,1152]{1,0:T(8,128)} %branch.1.branch_ref), channel_id=1, source_target_pairs={{0,1},{1,0},{2,3},{3,2},{4,5},{5,4},{6,7},{7,6},{8,9},{9,8},{10,11... | collective-permute-start | bytes 1769480 | tf_op jit(solution)/shard_map/ppermute | solution.py:947
  102.2 19.3 %collective-permute-start.18 = (f32[128,1152]{1,0:T(8,128)}, f32[128,1152]{1,0:T(8,128)}, u32[]{:S(2)}, u32[]{:S(2)}) collective-permute-start(f32[128,1152]{1,0:T(8,128)} %get-tuple-element.103._.own_ref.rest_13_), channel_id=1, source_target_pairs={{0,1},{1,0},{2,3},{3,2},{4,5},{5,4},{6,7},{7,6},{8,9},{9,8},{10,11... | collective-permute-start | bytes 1769480 | tf_op jit(solution)/shard_map/ppermute | solution.py:947
  102.7 21.7 %collective-permute-start.19 = (bf16[144,1152]{1,0:T(8,128)(2,1)}, bf16[144,1152]{1,0:T(8,128)(2,1)}, u32[]{:S(2)}, u32[]{:S(2)}) collective-permute-start(bf16[144,1152]{1,0:T(8,128)(2,1)} %get-tuple-element.107.rest_4_), channel_id=1, source_target_pairs={{0,2},{2,0},{4,6},{6,4},{8,10},{10,8},{12,14},{14,12},{16,18},{18,... | collective-permute-start | bytes 995336 | tf_op jit(solution)/shard_map/ppermute | solution.py:952
  103.9 20.5 %collective-permute-start.20 = (bf16[144,1152]{1,0:T(8,128)(2,1)}, bf16[144,1152]{1,0:T(8,128)(2,1)}, u32[]{:S(2)}, u32[]{:S(2)}) collective-permute-start(bf16[144,1152]{1,0:T(8,128)(2,1)} %get-tuple-element.107.rest_4_), channel_id=1, source_target_pairs={{0,4},{2,6},{4,0},{6,2},{8,12},{10,14},{12,8},{14,10},{16,20},{18,... | collective-permute-start | bytes 995336 | tf_op jit(solution)/shard_map/ppermute | solution.py:952
  116.4 8.3 %collective-permute-start.21 = (bf16[144,1152]{1,0:T(8,128)(2,1)}, bf16[144,1152]{1,0:T(8,128)(2,1)}, u32[]{:S(2)}, u32[]{:S(2)}) collective-permute-start(bf16[144,1152]{1,0:T(8,128)(2,1)} %get-tuple-element.107.rest_4_), channel_id=1, source_target_pairs={{0,6},{2,4},{4,2},{6,0},{8,14},{10,12},{12,10},{14,8},{16,22},{18,... | collective-permute-start | bytes 995336 | tf_op jit(solution)/shard_map/ppermute | solution.py:952
  121.0 16.4 %collective-permute-start.27 = (bf16[200,1152]{1,0:T(8,128)(2,1)}, bf16[200,1152]{1,0:T(8,128)(2,1)}, u32[]{:S(2)}, u32[]{:S(2)}) collective-permute-start(bf16[200,1152]{1,0:T(8,128)(2,1)} %get-tuple-element.119), channel_id=1, source_target_pairs={{0,16},{2,18},{4,20},{6,22},{8,24},{10,26},{12,28},{14,30},{16,0},... | collective-permute-start | bytes 1382408 | tf_op jit(solution)/shard_map/ppermute | solution.py:952
  128.3 14.1 %collective-permute-start.26 = (bf16[160,1152]{1,0:T(8,128)(2,1)}, bf16[160,1152]{1,0:T(8,128)(2,1)}, u32[]{:S(2)}, u32[]{:S(2)}) collective-permute-start(bf16[160,1152]{1,0:T(8,128)(2,1)} %get-tuple-element.117), channel_id=1, source_target_pairs={{0,8},{2,10},{4,12},{6,14},{8,0},{10,2},{12,4},{14,6},{16,24},{18,... | collective-permute-start | bytes 1105928 | tf_op jit(solution)/shard_map/ppermute | solution.py:952
  144.5 8.7 %collective-permute-start.28 = (bf16[88,1152]{1,0:T(8,128)(2,1)}, bf16[88,1152]{1,0:T(8,128)(2,1)}, u32[]{:S(2)}, u32[]{:S(2)}) collective-permute-start(bf16[88,1152]{1,0:T(8,128)(2,1)} %get-tuple-element.123), channel_id=1, source_target_pairs={{0,16},{2,18},{4,20},{6,22},{8,24},{10,26},{12,28},{14,30},{16,0},... | collective-permute-start | bytes 608264 | tf_op jit(solution)/shard_map/ppermute | solution.py:952
  147.3 7.8 %collective-permute-start.30 = (bf16[56,1152]{1,0:T(8,128)(2,1)}, bf16[56,1152]{1,0:T(8,128)(2,1)}, u32[]{:S(2)}, u32[]{:S(2)}) collective-permute-start(bf16[56,1152]{1,0:T(8,128)(2,1)} %get-tuple-element.127.refs_0_), channel_id=1, source_target_pairs={{0,2},{2,0},{4,6},{6,4},{8,10},{10,8},{12,14},{14,12},{16,18},{18,... | collective-permute-start | bytes 387080 | tf_op jit(solution)/shard_map/ppermute | solution.py:952
  148.5 6.9 %collective-permute-start.31 = (bf16[56,1152]{1,0:T(8,128)(2,1)}, bf16[56,1152]{1,0:T(8,128)(2,1)}, u32[]{:S(2)}, u32[]{:S(2)}) collective-permute-start(bf16[56,1152]{1,0:T(8,128)(2,1)} %get-tuple-element.127.refs_0_), channel_id=1, source_target_pairs={{0,4},{2,6},{4,0},{6,2},{8,12},{10,14},{12,8},{14,10},{16,20},{18,... | collective-permute-start | bytes 387080 | tf_op jit(solution)/shard_map/ppermute | solution.py:952
  151.2 6.2 %collective-permute-start.32 = (bf16[56,1152]{1,0:T(8,128)(2,1)}, bf16[56,1152]{1,0:T(8,128)(2,1)}, u32[]{:S(2)}, u32[]{:S(2)}) collective-permute-start(bf16[56,1152]{1,0:T(8,128)(2,1)} %get-tuple-element.127.refs_0_), channel_id=1, source_target_pairs={{0,6},{2,4},{4,2},{6,0},{8,14},{10,12},{12,10},{14,8},{16,22},{18,... | collective-permute-start | bytes 387080 | tf_op jit(solution)/shard_map/ppermute | solution.py:952
  155.1 4.4 %collective-permute-start.29 = (f32[1152]{0:T(1024)}, f32[1152]{0:T(1024)}, u32[]{:S(2)}, u32[]{:S(2)}) collective-permute-start(f32[1152]{0:T(1024)} %get-tuple-element.124), channel_id=1, source_target_pairs={{0,1},{1,0},{2,3},{3,2},{4,5},{5,4},{6,7},{7,6},{8,9},{9,8},{10,11... | collective-permute-start | bytes 13832 | tf_op jit(solution)/shard_map/ppermute | solution.py:947
